TPU v7x, 256 devices: a whole 4x4x8 slice. The times are simulated.
256 devices in a mesh: len: 16 (over y, x), chan: 16 (over z, core).
Axes of the slice: x: 4, y: 4, z: 8, core: 2. Of those that a mesh axis runs over, the one named last changes fastest.
Arguments:
- inputs: bfloat16 [2048, 32768], P(None, ('len', 'chan')), may hold values from -6 to 6
- grad_output: bfloat16 [2048, 32768], P(None, ('len', 'chan')), may hold values from -6 to 6
- pole_values: float32 [2048, 16], P('chan'), may hold values from 0.94 to 0.99998474, as said below
- residue_values: float32 [2048, 16], P('chan'), may hold values from -0.25 to 0.25
Outputs:
- input_grad: bfloat16 [2048, 32768], P(None, ('len', 'chan'))
- residue_grad: float32 [2048, 16], P('chan')
- pole_grad: float32 [2048, 16], P('chan')
Inputs may be any that keep to these rules, and one draw needn't show every extreme that they name: `pole_values`: 1 - pole lies between 1 / 65536 and 0.06.
All inputs are finite; a program needn't handle non-finite values.
Results may differ from a plain program's by a relative error of at most 0.00105.
Values may be sent and summed in bfloat16 or wider, within the bound.
No kernel may reach another device: no remote copies, remote signals or barrier semaphores. Data moves between devices by JAX's collectives and lax.ppermute only.
A program may use at most 256 MiB of HBM per device.

v0:
```python
import math

import jax
import jax.numpy as jnp
from jax import lax
from jax.sharding import PartitionSpec as P

LEN_DEV = 2048
BLOCK = 128


PRECISE = lax.Precision.HIGHEST


def carried_in(shard, axis, combine, identity, reverse):
    length, place = (lax.axis_size(axis), lax.axis_index(axis))
    everything = jax.tree.map(lambda part: lax.all_gather(part, axis), shard)
    start = jax.tree.map(
        lambda part, zero: jnp.broadcast_to(jnp.asarray(zero, part.dtype), part.shape),
        shard,
        identity,
    )

    def turn(k, before):
        at = length - 1 - k if reverse else k
        reached = at > place if reverse else at < place
        new = combine(before, jax.tree.map(lambda part: part[at], everything))
        return jax.tree.map(lambda a, b: jnp.where(reached, a, b), new, before)

    return lax.fori_loop(0, length, turn, start)


def link_pairs(earlier, latter):
    return (earlier[0] * latter[0], latter[0] * earlier[1] + latter[1])


def log_rates(pole_values):
    return jnp.log1p(-(1.0 - pole_values))


def finish_span(
    intra_state, intra_adjoint, output_blocks, pole_values, residue_values, state_in, adjoint_after
):
    block_len = intra_state.shape[3]
    log_rate = log_rates(pole_values)[:, :, None]
    offsets = jnp.arange(block_len, dtype=jnp.float32)
    whole_step = jnp.broadcast_to(jnp.exp(log_rate * block_len), intra_state.shape[:3])
    forward_seq = jnp.concatenate([state_in[:, :, None], intra_state[:, :, :-1, -1]], axis=2)
    state_start = lax.associative_scan(link_pairs, (whole_step, forward_seq), axis=2)[1]
    backward_seq = jnp.concatenate([intra_adjoint[:, :, 1:, 0], adjoint_after[:, :, None]], axis=2)
    adjoint_next = lax.associative_scan(
        link_pairs, (whole_step, backward_seq), reverse=True, axis=2
    )[1]
    rate_four = log_rate[..., None]
    state_full = intra_state + jnp.exp(rate_four * (offsets + 1.0)) * state_start[..., None]
    shifted = jnp.concatenate([jnp.zeros_like(intra_state[..., :1]), intra_state[..., :-1]], axis=3)
    previous = shifted + jnp.exp(rate_four * offsets) * state_start[..., None]
    adjoint = intra_adjoint + jnp.exp(rate_four * (block_len - offsets)) * adjoint_next[..., None]
    residue_raw = jnp.einsum("cpnt,cnt->cp", state_full, output_blocks, precision=PRECISE)
    pole_raw = residue_values * jnp.sum(adjoint * previous, axis=(2, 3))
    input_grad = jnp.einsum("cp,cpnt->cnt", residue_values, adjoint, precision=PRECISE)
    return (input_grad, residue_raw, pole_raw)


def span_pass(input_blocks, output_blocks, pole_values, residue_values, state_in, adjoint_after):
    block_len = input_blocks.shape[2]
    log_rate = log_rates(pole_values)[:, :, None, None]
    offsets = jnp.arange(block_len, dtype=jnp.float32)
    decay_up = jnp.exp(log_rate * offsets)
    growth = jnp.exp(-log_rate * offsets)
    triangle = (offsets[:, None] >= offsets[None, :]).astype(jnp.float32)
    intra_state = decay_up * jnp.einsum(
        "cpnj,tj->cpnt", input_blocks[:, None] * growth, triangle, precision=PRECISE
    )
    intra_adjoint = growth * jnp.einsum(
        "cpnt,tj->cpnj", output_blocks[:, None] * decay_up, triangle, precision=PRECISE
    )
    return finish_span(
        intra_state,
        intra_adjoint,
        output_blocks,
        pole_values,
        residue_values,
        state_in,
        adjoint_after,
    )


def grouped_pass(
    input_rows, output_rows, pole_values, residue_values, state_in, adjoint_after, block_len
):
    chans, span_len = input_rows.shape
    group_size = math.gcd(chans, max(1, 256 * block_len // span_len))
    groups = chans // group_size
    block_count = span_len // block_len
    packed = (
        input_rows.reshape(groups, group_size, block_count, block_len),
        output_rows.reshape(groups, group_size, block_count, block_len),
        pole_values.reshape(groups, group_size, -1),
        residue_values.reshape(groups, group_size, -1),
        state_in.reshape(groups, group_size, -1),
        adjoint_after.reshape(groups, group_size, -1),
    )
    input_grad, residue_raw, pole_raw = lax.map(lambda items: span_pass(*items), packed)
    return (
        input_grad.reshape(chans, span_len),
        residue_raw.reshape(chans, -1),
        pole_raw.reshape(chans, -1),
    )


def boundary_terms(input_rows, output_rows, pole_values, block_len):
    chans, span_len = input_rows.shape
    block_count = span_len // block_len
    log_rate = log_rates(pole_values)
    offsets = jnp.arange(block_len, dtype=jnp.float32)
    tail_pow = jnp.exp(log_rate[:, :, None] * (block_len - 1.0 - offsets))
    head_pow = jnp.exp(log_rate[:, :, None] * offsets)
    input_blocks = input_rows.reshape(chans, block_count, block_len)
    output_blocks = output_rows.reshape(chans, block_count, block_len)
    block_ends = jnp.einsum("cpj,cnj->cpn", tail_pow, input_blocks, precision=PRECISE)
    block_starts = jnp.einsum("cpj,cnj->cpn", head_pow, output_blocks, precision=PRECISE)
    positions = jnp.arange(block_count, dtype=jnp.float32)
    end_state = jnp.sum(
        jnp.exp(log_rate[:, :, None] * block_len * (block_count - 1.0 - positions)) * block_ends,
        axis=2,
    )
    start_adjoint = jnp.sum(
        jnp.exp(log_rate[:, :, None] * block_len * positions) * block_starts, axis=2
    )
    return (end_state, start_adjoint)


def scale_grads(residue_raw, pole_raw, pole_values, token_total):
    mode_width = (1.0 - pole_values) * (1.0 + pole_values)
    root_total = math.sqrt(token_total)
    return (residue_raw * jnp.sqrt(mode_width) / root_total, pole_raw * mode_width / root_total)


def body(inputs, grad_output, pole_values, residue_values):
    block_len = BLOCK
    token_total = LEN_DEV * lax.axis_size("len")
    moved_inputs, moved_grads = (
        lax.all_to_all(inputs, "chan", split_axis=0, concat_axis=1, tiled=True),
        lax.all_to_all(grad_output, "chan", split_axis=0, concat_axis=1, tiled=True),
    )
    input_rows = moved_inputs.astype(jnp.float32)
    output_rows = moved_grads.astype(jnp.float32)
    span_len = input_rows.shape[1]
    log_rate = log_rates(pole_values)
    end_state, start_adjoint = boundary_terms(input_rows, output_rows, pole_values, block_len)
    span_step = jnp.exp(log_rate * span_len)
    identity = (jnp.ones_like(end_state), jnp.zeros_like(end_state))
    state_in = carried_in((span_step, end_state), "len", link_pairs, identity, False)[1]
    adjoint_after = carried_in((span_step, start_adjoint), "len", link_pairs, identity, True)[1]
    input_grad, residue_raw, pole_raw = grouped_pass(
        input_rows, output_rows, pole_values, residue_values, state_in, adjoint_after, block_len
    )
    residue_raw, pole_raw = lax.psum((residue_raw, pole_raw), "len")
    rounded = input_grad.astype(jnp.bfloat16)
    rounded = lax.all_to_all(rounded, "chan", split_axis=1, concat_axis=0, tiled=True)
    residue_grad, pole_grad = scale_grads(residue_raw, pole_raw, pole_values, token_total)
    return (rounded, residue_grad, pole_grad)


def solution(mesh):
    in_specs = (
        P(None, ("len", "chan")),
        P(None, ("len", "chan")),
        P("chan", None),
        P("chan", None),
    )
    out_specs = (P(None, ("len", "chan")), P("chan", None), P("chan", None))
    return jax.shard_map(body, mesh=mesh, in_specs=in_specs, out_specs=out_specs, check_vma=False)
```

profile of v0, /device:TPU:32, one launch (start us, length us, event | category | flops | bytes accessed | tf_op | source)
XLA Modules:
  0.0 392.3 jit_solution(9397961765772920786)
XLA Ops:
  0.6 8.6 %all-to-all-start.1 = ((bf16[16,128,128]{2,1,0:T(8,128)(2,1)}), bf16[16,128,128]{2,1,0:T(8,128)(2,1)S(1)}, u32[]{:S(2)}, u32[]{:S(2)}) async-start(bf16[16,128,128]{2,1,0:T(8,128)(2,1)} %bitcast.151), calls=%async_computation.1 | async-start | bytes 1048576 | tf_op jit(solution)/shard_map/all_to_all | solution.py:144
  11.8 24.2 %all-gather = f32[2048,16]{0,1:T(8,128)S(1)} all-gather(f32[128,16]{0,1:T(8,128)S(1)} %get-tuple-element.480), channel_id=2, replica_groups=mesh['len'=16,'chan'=16] {'len'}, dimensions={0}, use_global_device_ids=true | all-gather | bytes 139264 | tf_op jit(solution)/shard_map/all_gather | solution.py:17
  36.0 7.2 %all-to-all-start = ((bf16[16,128,128]{2,1,0:T(8,128)(2,1)}), bf16[16,128,128]{2,1,0:T(8,128)(2,1)S(1)}, u32[]{:S(2)}, u32[]{:S(2)}) async-start(bf16[16,128,128]{2,1,0:T(8,128)(2,1)} %bitcast.152), calls=%async_computation | async-start | bytes 1048576 | tf_op jit(solution)/shard_map/all_to_all | solution.py:145
  44.6 24.1 %all-gather.2 = f32[2048,16]{1,0:T(8,128)S(1)} all-gather(f32[128,16]{1,0:T(8,128)S(1)} %fusion.40), channel_id=4, replica_groups=mesh['len'=16,'chan'=16] {'len'}, dimensions={0}, use_global_device_ids=true | all-gather | bytes 139264 | tf_op jit(solution)/shard_map/all_gather | solution.py:17
  71.2 22.9 %all-gather.1 = f32[2048,16]{1,0:T(8,128)S(1)} all-gather(f32[128,16]{1,0:T(8,128)S(1)} %fusion.39), channel_id=3, replica_groups=mesh['len'=16,'chan'=16] {'len'}, dimensions={0}, use_global_device_ids=true | all-gather | bytes 139264 | tf_op jit(solution)/shard_map/all_gather | solution.py:17
  97.0 212.5 %while.44 = (s32[]{:T(128)}, bf16[8,16,16,128]{3,2,1,0:T(8,128)(2,1)}, f32[8,16,16]{2,1,0:T(8,128)S(1)}, f32[8,16,16]{2,1,0:T(8,128)S(1)}, f32[8,16,16]{2,1,0:T(...) while((s32[]{:T(128)}, ...), condition=%wide.region_8.9_spmd, body=%wide.region_6.8_spmd.sunk | while | flops 1629722368 | bytes 39761692 | solution.py:104
  105.2 1.9 slice.362
  107.1 3.1 copy.122
  110.9 6.2 %multiply_reduce_fusion.2 = (f32[16,16]{1,0:T(8,128)S(1)}, f32[16,16,16,128]{3,2,1,0:T(8,128)S(1)}, f32[16,16,16,128]{3,2,1,0:T(8,128)S(1)}) fusion(f32[16,16,16,127]{3,2,1,0:T(8,128)S(1)} %bitcast.136, f32[16,16,16]{2,1,0:T(8,128)S(1)} %copy.123, f32[16,16,128]{2,1,0:T(8,128)S(1)} %get-tuple-element.627, f32[16,16,16,128]{3,2,1,0:T(8,128)} %copy-done, ...), kind=kLoop, calls=%fused_computation.4.clone.1 | loop fusion | flops 4194048 | bytes 10896384 | tf_op jit(solution)/shard_map/while/body/eval_jaxpr/reduce_sum | solution.py:60
  118.1 3.1 fusion.113
  131.8 1.9 slice.362
  133.7 3.1 copy.122
  137.5 6.2 %multiply_reduce_fusion.2 = (f32[16,16]{1,0:T(8,128)S(1)}, f32[16,16,16,128]{3,2,1,0:T(8,128)S(1)}, f32[16,16,16,128]{3,2,1,0:T(8,128)S(1)}) fusion(f32[16,16,16,127]{3,2,1,0:T(8,128)S(1)} %bitcast.136, f32[16,16,16]{2,1,0:T(8,128)S(1)} %copy.123, f32[16,16,128]{2,1,0:T(8,128)S(1)} %get-tuple-element.627, f32[16,16,16,128]{3,2,1,0:T(8,128)} %copy-done, ...), kind=kLoop, calls=%fused_computation.4.clone.1 | loop fusion | flops 4194048 | bytes 10896384 | tf_op jit(solution)/shard_map/while/body/eval_jaxpr/reduce_sum | solution.py:60
  144.7 3.1 fusion.113
  147.8 1.7 fusion.115
  158.3 1.9 slice.362
  160.2 3.1 copy.122
  164.0 6.2 %multiply_reduce_fusion.2 = (f32[16,16]{1,0:T(8,128)S(1)}, f32[16,16,16,128]{3,2,1,0:T(8,128)S(1)}, f32[16,16,16,128]{3,2,1,0:T(8,128)S(1)}) fusion(f32[16,16,16,127]{3,2,1,0:T(8,128)S(1)} %bitcast.136, f32[16,16,16]{2,1,0:T(8,128)S(1)} %copy.123, f32[16,16,128]{2,1,0:T(8,128)S(1)} %get-tuple-element.627, f32[16,16,16,128]{3,2,1,0:T(8,128)} %copy-done, ...), kind=kLoop, calls=%fused_computation.4.clone.1 | loop fusion | flops 4194048 | bytes 10896384 | tf_op jit(solution)/shard_map/while/body/eval_jaxpr/reduce_sum | solution.py:60
  171.2 3.1 fusion.113
  174.4 1.7 fusion.115
  184.9 1.9 slice.362
  186.8 3.1 copy.122
  190.6 6.2 %multiply_reduce_fusion.2 = (f32[16,16]{1,0:T(8,128)S(1)}, f32[16,16,16,128]{3,2,1,0:T(8,128)S(1)}, f32[16,16,16,128]{3,2,1,0:T(8,128)S(1)}) fusion(f32[16,16,16,127]{3,2,1,0:T(8,128)S(1)} %bitcast.136, f32[16,16,16]{2,1,0:T(8,128)S(1)} %copy.123, f32[16,16,128]{2,1,0:T(8,128)S(1)} %get-tuple-element.627, f32[16,16,16,128]{3,2,1,0:T(8,128)} %copy-done, ...), kind=kLoop, calls=%fused_computation.4.clone.1 | loop fusion | flops 4194048 | bytes 10896384 | tf_op jit(solution)/shard_map/while/body/eval_jaxpr/reduce_sum | solution.py:60
  197.8 3.1 fusion.113
  200.9 1.7 fusion.115
  211.4 1.9 slice.362
  213.4 3.1 copy.122
  217.2 6.2 %multiply_reduce_fusion.2 = (f32[16,16]{1,0:T(8,128)S(1)}, f32[16,16,16,128]{3,2,1,0:T(8,128)S(1)}, f32[16,16,16,128]{3,2,1,0:T(8,128)S(1)}) fusion(f32[16,16,16,127]{3,2,1,0:T(8,128)S(1)} %bitcast.136, f32[16,16,16]{2,1,0:T(8,128)S(1)} %copy.123, f32[16,16,128]{2,1,0:T(8,128)S(1)} %get-tuple-element.627, f32[16,16,16,128]{3,2,1,0:T(8,128)} %copy-done, ...), kind=kLoop, calls=%fused_computation.4.clone.1 | loop fusion | flops 4194048 | bytes 10896384 | tf_op jit(solution)/shard_map/while/body/eval_jaxpr/reduce_sum | solution.py:60
  224.3 3.1 fusion.113
  227.5 1.7 fusion.115
  238.0 1.9 slice.362
  239.9 3.1 copy.122
  243.7 6.2 %multiply_reduce_fusion.2 = (f32[16,16]{1,0:T(8,128)S(1)}, f32[16,16,16,128]{3,2,1,0:T(8,128)S(1)}, f32[16,16,16,128]{3,2,1,0:T(8,128)S(1)}) fusion(f32[16,16,16,127]{3,2,1,0:T(8,128)S(1)} %bitcast.136, f32[16,16,16]{2,1,0:T(8,128)S(1)} %copy.123, f32[16,16,128]{2,1,0:T(8,128)S(1)} %get-tuple-element.627, f32[16,16,16,128]{3,2,1,0:T(8,128)} %copy-done, ...), kind=kLoop, calls=%fused_computation.4.clone.1 | loop fusion | flops 4194048 | bytes 10896384 | tf_op jit(solution)/shard_map/while/body/eval_jaxpr/reduce_sum | solution.py:60
  250.9 3.1 fusion.113
  254.0 1.7 fusion.115
  264.6 1.9 slice.362
  266.5 3.1 copy.122
  270.3 6.2 %multiply_reduce_fusion.2 = (f32[16,16]{1,0:T(8,128)S(1)}, f32[16,16,16,128]{3,2,1,0:T(8,128)S(1)}, f32[16,16,16,128]{3,2,1,0:T(8,128)S(1)}) fusion(f32[16,16,16,127]{3,2,1,0:T(8,128)S(1)} %bitcast.136, f32[16,16,16]{2,1,0:T(8,128)S(1)} %copy.123, f32[16,16,128]{2,1,0:T(8,128)S(1)} %get-tuple-element.627, f32[16,16,16,128]{3,2,1,0:T(8,128)} %copy-done, ...), kind=kLoop, calls=%fused_computation.4.clone.1 | loop fusion | flops 4194048 | bytes 10896384 | tf_op jit(solution)/shard_map/while/body/eval_jaxpr/reduce_sum | solution.py:60
  277.5 3.1 fusion.113
  280.6 1.7 fusion.115
  291.1 1.9 slice.362
  293.0 3.1 copy.122
  296.8 6.2 %multiply_reduce_fusion.2 = (f32[16,16]{1,0:T(8,128)S(1)}, f32[16,16,16,128]{3,2,1,0:T(8,128)S(1)}, f32[16,16,16,128]{3,2,1,0:T(8,128)S(1)}) fusion(f32[16,16,16,127]{3,2,1,0:T(8,128)S(1)} %bitcast.136, f32[16,16,16]{2,1,0:T(8,128)S(1)} %copy.123, f32[16,16,128]{2,1,0:T(8,128)S(1)} %get-tuple-element.627, f32[16,16,16,128]{3,2,1,0:T(8,128)} %copy-done, ...), kind=kLoop, calls=%fused_computation.4.clone.1 | loop fusion | flops 4194048 | bytes 10896384 | tf_op jit(solution)/shard_map/while/body/eval_jaxpr/reduce_sum | solution.py:60
  304.0 3.1 fusion.113
  307.2 1.7 fusion.115
  309.5 2.0 copy.82
  311.5 7.2 %all-to-all-start.2 = ((bf16[128,16,128]{2,0,1:T(8,128)(2,1)}), bf16[128,16,128]{2,0,1:T(8,128)(2,1)S(1)}, u32[]{:S(2)}, u32[]{:S(2)}) async-start(bf16[128,16,128]{2,0,1:T(8,128)(2,1)} %copy.82), calls=%async_computation.2 | async-start | bytes 1048576 | tf_op jit(solution)/shard_map/all_to_all | solution.py:161
  318.8 72.1 %all-reduce.17 = (f32[128,16]{0,1:T(8,128)S(1)}, f32[128,16]{0,1:T(8,128)S(1)}) all-reduce(f32[128,16]{0,1:T(8,128)S(1)} %copy.98, f32[128,16]{0,1:T(8,128)S(1)} %copy.99), channel_id=1, replica_groups=mesh['len'=16,'chan'=16] {'len'}, use_global_device_ids=true, to_apply=%region_9.10 | all-reduce | flops 4096 | bytes 32768 | tf_op jit(solution)/shard_map/psum | solution.py:159
  (659 shorter events, 92.9 us)
Async XLA Ops:
  0.6 35.4 %all-to-all-start.1 = ((bf16[16,128,128]{2,1,0:T(8,128)(2,1)}), bf16[16,128,128]{2,1,0:T(8,128)(2,1)S(1)}, u32[]{:S(2)}, u32[]{:S(2)}) async-start(bf16[16,128,128]{2,1,0:T(8,128)(2,1)} %bitcast.151), calls=%async_computation.1 | async-start | bytes 1048576 | tf_op jit(solution)/shard_map/all_to_all | solution.py:144
  36.0 33.8 %all-to-all-start = ((bf16[16,128,128]{2,1,0:T(8,128)(2,1)}), bf16[16,128,128]{2,1,0:T(8,128)(2,1)S(1)}, u32[]{:S(2)}, u32[]{:S(2)}) async-start(bf16[16,128,128]{2,1,0:T(8,128)(2,1)} %bitcast.152), calls=%async_computation | async-start | bytes 1048576 | tf_op jit(solution)/shard_map/all_to_all | solution.py:145
  97.0 1.0 copy-start.1
  99.2 1.3 copy-start
  118.1 5.5 %copy-start.2 = (f32[8,16,16,128]{3,2,1,0:T(8,128)S(1)}, f32[8,16,16,128]{3,2,1,0:T(8,128)}, u32[]{:S(2)}) copy-start(f32[8,16,16,128]{3,2,1,0:T(8,128)} %copy-done.1) | copy-start | bytes 3145732 | tf_op jit(solution)/shard_map/while
  123.6 1.0 copy-start.1
  125.8 1.3 copy-start
  144.7 5.5 %copy-start.2 = (f32[8,16,16,128]{3,2,1,0:T(8,128)S(1)}, f32[8,16,16,128]{3,2,1,0:T(8,128)}, u32[]{:S(2)}) copy-start(f32[8,16,16,128]{3,2,1,0:T(8,128)} %copy-done.1) | copy-start | bytes 3145732 | tf_op jit(solution)/shard_map/while
  150.2 1.0 copy-start.1
  152.3 1.3 copy-start
  171.2 5.5 %copy-start.2 = (f32[8,16,16,128]{3,2,1,0:T(8,128)S(1)}, f32[8,16,16,128]{3,2,1,0:T(8,128)}, u32[]{:S(2)}) copy-start(f32[8,16,16,128]{3,2,1,0:T(8,128)} %copy-done.1) | copy-start | bytes 3145732 | tf_op jit(solution)/shard_map/while
  176.7 1.0 copy-start.1
  178.9 1.3 copy-start
  197.8 5.5 %copy-start.2 = (f32[8,16,16,128]{3,2,1,0:T(8,128)S(1)}, f32[8,16,16,128]{3,2,1,0:T(8,128)}, u32[]{:S(2)}) copy-start(f32[8,16,16,128]{3,2,1,0:T(8,128)} %copy-done.1) | copy-start | bytes 3145732 | tf_op jit(solution)/shard_map/while
  203.3 1.0 copy-start.1
  205.5 1.3 copy-start
  224.3 5.5 %copy-start.2 = (f32[8,16,16,128]{3,2,1,0:T(8,128)S(1)}, f32[8,16,16,128]{3,2,1,0:T(8,128)}, u32[]{:S(2)}) copy-start(f32[8,16,16,128]{3,2,1,0:T(8,128)} %copy-done.1) | copy-start | bytes 3145732 | tf_op jit(solution)/shard_map/while
  229.8 1.0 copy-start.1
  232.0 1.3 copy-start
  250.9 5.5 %copy-start.2 = (f32[8,16,16,128]{3,2,1,0:T(8,128)S(1)}, f32[8,16,16,128]{3,2,1,0:T(8,128)}, u32[]{:S(2)}) copy-start(f32[8,16,16,128]{3,2,1,0:T(8,128)} %copy-done.1) | copy-start | bytes 3145732 | tf_op jit(solution)/shard_map/while
  256.4 1.0 copy-start.1
  258.6 1.3 copy-start
  277.5 5.5 %copy-start.2 = (f32[8,16,16,128]{3,2,1,0:T(8,128)S(1)}, f32[8,16,16,128]{3,2,1,0:T(8,128)}, u32[]{:S(2)}) copy-start(f32[8,16,16,128]{3,2,1,0:T(8,128)} %copy-done.1) | copy-start | bytes 3145732 | tf_op jit(solution)/shard_map/while
  283.0 1.0 copy-start.1
  285.1 1.3 copy-start
  304.0 5.5 %copy-start.2 = (f32[8,16,16,128]{3,2,1,0:T(8,128)S(1)}, f32[8,16,16,128]{3,2,1,0:T(8,128)}, u32[]{:S(2)}) copy-start(f32[8,16,16,128]{3,2,1,0:T(8,128)} %copy-done.1) | copy-start | bytes 3145732 | tf_op jit(solution)/shard_map/while
  309.5 81.4 %copy-start.3 = (f32[128,16]{0,1:T(8,128)S(1)}, f32[128,16]{0,1:T(8,128)}, u32[]{:S(2)}) copy-start(f32[128,16]{0,1:T(8,128)} %param.12) | copy-start | bytes 24580
  311.5 80.0 %all-to-all-start.2 = ((bf16[128,16,128]{2,0,1:T(8,128)(2,1)}), bf16[128,16,128]{2,0,1:T(8,128)(2,1)S(1)}, u32[]{:S(2)}, u32[]{:S(2)}) async-start(bf16[128,16,128]{2,0,1:T(8,128)(2,1)} %copy.82), calls=%async_computation.2 | async-start | bytes 1048576 | tf_op jit(solution)/shard_map/all_to_all | solution.py:161
where the time goes:
time: 394 us; the launch traced here: 392 us
  blocking collectives  143 us (36%)
  local copies, waits for them, and re-layouts  103 us (26%)
  matrix products  60 us (15%)
  other arithmetic  57.8 us (15%)
  starting transfers between devices  23 us (6%)
  loops' own time  4.76 us (1%)
    psum x1, blocking collectives, body(): residue_raw, pole_raw = lax.psum((residue_raw, pole_raw), 'len')  72.1 us
    all_gather x3, blocking collectives, carried_in(): everything = jax.tree.map(lambda part: lax.all_gather(part, axis), shard)  71.2 us
    reduce_sum x8, other arithmetic, finish_span(): pole_raw = residue_values * jnp.sum(adjoint * previous, axis=(2, 3))  49.9 us
    slice x16, local copies, waits for them, and re-layouts, finish_span(): intra_state[:, :, :-1, -1]  40.1 us
    dot_general x8, matrix products, finish_span(): jnp.einsum('cpnt,cnt->cp', state_full, output_blocks, precision=PRECISE)  25 us
    while x48, local copies, waits for them, and re-layouts  16.2 us
    slice x16, local copies, waits for them, and re-layouts, finish_span(): intra_adjoint[:, :, 1:, 0]  14.1 us
    dot_general x8, matrix products, finish_span(): jnp.einsum('cp,cpnt->cnt', residue_values, adjoint, precision=PRECISE)  13.6 us
  transfers between devices with their start and end apart: 3, of which 0 were waited for; matrix products, arithmetic and copies ran while one was open for 1% of the time, Pallas kernels for 0%

commit v1 on v0

v1 whole, which is shorter than its diff:
```python
import functools
import math

import jax
import jax.numpy as jnp
from jax import lax
from jax.experimental import pallas as pl
from jax.experimental.pallas import tpu as pltpu
from jax.sharding import PartitionSpec as P

ROWS = 8
GROUP = 8
F32 = jnp.float32
VMEM = pl.BlockSpec(memory_space=pltpu.VMEM)


def identity_matrix(size):
    rows = lax.broadcasted_iota(jnp.int32, (size, size), 0)
    cols = lax.broadcasted_iota(jnp.int32, (size, size), 1)
    return (rows == cols).astype(F32).astype(jnp.bfloat16)


def flip(eye, tile):
    return lax.dot_general(eye, tile, (((1,), (1,)), ((), ())), preferred_element_type=F32)


def flip_blocks(src_ref, dst_ref):
    blocks, chans, block_len = src_ref.shape
    eye = identity_matrix(block_len)
    for n in range(blocks):
        dst_ref[pl.ds(n, block_len, stride=blocks), :] = flip(eye, src_ref[n])


def log_rates(poles):
    return jnp.log1p(-(1.0 - poles))


def spread(table, p):
    return jnp.broadcast_to(table[p : p + 1, :], (ROWS, table.shape[1]))


def cleared(ref, count):
    ref[:ROWS, :] = jnp.zeros((ROWS, ref.shape[1]), F32)
    return (ref[:ROWS, :],) * count


def block_rows(ref, n, blocks, modes):
    return ref[pl.ds(n, modes, stride=blocks), :]


def ends_kernel(blocks, spans, g_ref, pole_ref, res_ref, gt_ref, coef_ref, h_ref, hs_ref, pad_ref):
    modes = pole_ref.shape[1]
    chans = pole_ref.shape[0]
    block_len = g_ref.shape[2]
    pad_ref[:, :modes] = pole_ref[...]
    pad_ref[:, modes : 2 * modes] = res_ref[...]
    coef_ref[...] = pad_ref[...].T[: 2 * modes, :]
    lam = coef_ref[:modes, :]
    flip_blocks(g_ref, gt_ref)
    empty = cleared(h_ref, modes)
    for half in range(blocks // ROWS):
        wide = [spread(lam, p) for p in range(modes)]

        def step(i, held):
            at = pl.multiple_of((block_len - 1 - i) * blocks + half * ROWS, ROWS)
            g = gt_ref[pl.ds(at, ROWS), :]
            return tuple(l * a + g for l, a in zip(wide, held))

        ends = lax.fori_loop(0, block_len, step, empty, unroll=8)
        for p in range(modes):
            h_ref[p * blocks + half * ROWS : p * blocks + half * ROWS + ROWS, :] = ends[p]
    block_step = jnp.exp(block_len * log_rates(lam))
    total = block_rows(h_ref, blocks - 1, blocks, modes)
    for n in range(blocks - 2, -1, -1):
        total = block_step * total + block_rows(h_ref, n, blocks, modes)
    for span in range(spans):
        hs_ref[span] = total


def input_grad_kernel(blocks, spans, gt_ref, coef_ref, h_ref, got_ref, out_ref, next_ref, flat_ref):
    modes = coef_ref.shape[0] // 2
    chans = coef_ref.shape[1]
    block_len = gt_ref.shape[0] // blocks
    lam = coef_ref[:modes, :]
    res = coef_ref[modes:, :]
    rate = log_rates(lam)
    block_step = jnp.exp(block_len * rate)
    span_step = jnp.exp((blocks * block_len) * rate)
    place = lax.axis_index("len")
    total = jnp.zeros((modes, chans), F32)
    for span in range(spans - 1, 0, -1):
        total = jnp.where(span > place, span_step * total + got_ref[span], total)
    for n in range(blocks - 1, -1, -1):
        next_ref[pl.ds(n, modes, stride=blocks), :] = total
        total = block_step * total + block_rows(h_ref, n, blocks, modes)
    for half in range(blocks // ROWS):
        wide = [spread(lam, p) for p in range(modes)]
        gain = [spread(res, p) for p in range(modes)]
        start = tuple(
            next_ref[p * blocks + half * ROWS : p * blocks + half * ROWS + ROWS, :]
            for p in range(modes)
        )

        def step(i, held):
            at = pl.multiple_of((block_len - 1 - i) * blocks + half * ROWS, ROWS)
            g = gt_ref[pl.ds(at, ROWS), :]
            held = tuple(l * a + g for l, a in zip(wide, held))
            terms = [r * a for r, a in zip(gain, held)]
            while len(terms) > 1:
                terms = [a + b for a, b in zip(terms[::2], terms[1::2])]
            flat_ref[pl.ds(at, ROWS), :] = terms[0]
            return held

        lax.fori_loop(0, block_len, step, start, unroll=4)
    eye = identity_matrix(chans)
    for n in range(blocks):
        tile = flat_ref[pl.ds(n, block_len, stride=blocks), :].astype(jnp.bfloat16)
        out_ref[n] = flip(eye, tile).astype(jnp.bfloat16)


def sums_kernel(
    blocks, spans, x_ref, gt_ref, coef_ref, h_ref, pay_ref, xt_ref, s_ref, d_ref, r_ref, q_ref, t_ref, zero_ref
):
    modes = coef_ref.shape[0] // 2
    chans = coef_ref.shape[1]
    block_len = gt_ref.shape[0] // blocks
    lam = coef_ref[:modes, :]
    flip_blocks(x_ref, xt_ref)
    empty = cleared(zero_ref, GROUP)
    for half in range(blocks // ROWS):
        for first in range(0, modes, GROUP):
            wide = [spread(lam, first + k) for k in range(GROUP)]

            def ahead(i, held):
                at = pl.multiple_of(i * blocks + half * ROWS, ROWS)
                g = gt_ref[pl.ds(at, ROWS), :]
                x = xt_ref[pl.ds(at, ROWS), :]
                state, slope, res_sum, pole_sum = held
                slope = tuple(l * d + s for l, d, s in zip(wide, slope, state))
                state = tuple(l * s + x for l, s in zip(wide, state))
                res_sum = tuple(r + g * s for r, s in zip(res_sum, state))
                pole_sum = tuple(q + g * d for q, d in zip(pole_sum, slope))
                return (state, slope, res_sum, pole_sum)

            results = lax.fori_loop(0, block_len, ahead, (empty,) * 4, unroll=4)

            def back(i, held):
                at = pl.multiple_of((block_len - 1 - i) * blocks + half * ROWS, ROWS)
                g = gt_ref[pl.ds(at, ROWS), :]
                adjoint, weighted = held
                adjoint = tuple(l * a + g for l, a in zip(wide, adjoint))
                weighted = tuple(l * q + a for l, q, a in zip(wide, weighted, adjoint))
                return (adjoint, weighted)

            weighted = lax.fori_loop(0, block_len, back, (empty,) * 2, unroll=4)[1]
            for k in range(GROUP):
                rows = slice(
                    (first + k) * blocks + half * ROWS, (first + k) * blocks + half * ROWS + ROWS
                )
                s_ref[rows, :] = results[0][k]
                d_ref[rows, :] = results[1][k]
                r_ref[rows, :] = results[2][k]
                q_ref[rows, :] = results[3][k]
                t_ref[rows, :] = weighted[k]
    rate = log_rates(lam)
    block_step = jnp.exp(block_len * rate)
    block_slope = block_len * jnp.exp((block_len - 1) * rate)
    rows_of = lambda ref, n: block_rows(ref, n, blocks, modes)
    state = jnp.zeros((modes, chans), F32)
    slope = state
    res_sum = state
    pole_sum = state
    for n in range(blocks):
        after = lam * rows_of(h_ref, n)
        res_sum = res_sum + (rows_of(r_ref, n) + state * after)
        pole_sum = pole_sum + (rows_of(q_ref, n) + slope * after + state * rows_of(t_ref, n))
        slope = block_step * slope + block_slope * state + rows_of(d_ref, n)
        state = block_step * state + rows_of(s_ref, n)
    total = jnp.zeros((modes, chans), F32)
    weighted = total
    for n in range(blocks - 1, -1, -1):
        weighted = block_step * (weighted + block_len * total) + rows_of(t_ref, n)
        total = block_step * total + rows_of(h_ref, n)
    for span in range(spans):
        for k, item in enumerate((state, slope, res_sum, pole_sum, weighted)):
            pay_ref[span, k * modes : (k + 1) * modes, :] = item


def finish_kernel(spans, span_len, pay_ref, got_ref, coef_ref, res_out, pole_out, pad_ref):
    modes = coef_ref.shape[0] // 2
    lam = coef_ref[:modes, :]
    res = coef_ref[modes:, :]
    rate = log_rates(lam)
    span_step = jnp.exp(span_len * rate)
    span_slope = span_len * jnp.exp((span_len - 1) * rate)
    state = jnp.zeros(lam.shape, F32)
    slope = state
    res_sum = state
    pole_sum = state
    for span in range(spans):
        ends, slopes, res_part, pole_part, weighted = [
            pay_ref[span, k * modes : (k + 1) * modes, :] for k in range(5)
        ]
        after = lam * got_ref[span]
        res_sum = res_sum + (res_part + state * after)
        pole_sum = pole_sum + (pole_part + slope * after + state * weighted)
        slope = span_step * slope + span_slope * state + slopes
        state = span_step * state + ends
    width = (1.0 - lam) * (1.0 + lam)
    scale = 1.0 / math.sqrt(spans * span_len)
    pad_ref[:modes, :] = res_sum * jnp.sqrt(width) * scale
    pad_ref[modes : 2 * modes, :] = res * pole_sum * width * scale
    turned = pad_ref[...].T
    res_out[...] = turned[:, :modes]
    pole_out[...] = turned[:, modes : 2 * modes]


def call(kernel, out_shape, in_count, scratch, name, flops):
    single = not isinstance(out_shape, (tuple, list))
    return pl.pallas_call(
        kernel,
        out_shape=out_shape,
        in_specs=[VMEM] * in_count,
        out_specs=VMEM if single else [VMEM] * len(out_shape),
        scratch_shapes=scratch,
        compiler_params=pltpu.CompilerParams(vmem_limit_bytes=32 * 1024 * 1024),
        cost_estimate=pl.CostEstimate(flops=flops, bytes_accessed=2**20, transcendentals=0),
        name=name,
    )


def swap(part, axis):
    return lax.all_to_all(part, axis, split_axis=0, concat_axis=0, tiled=True)


def body(inputs, grad_output, pole_values, residue_values):
    spans = lax.axis_size("len")
    blocks = lax.axis_size("chan")
    chans, modes = pole_values.shape
    block_len = inputs.shape[1]
    flat = blocks * block_len
    held = modes * blocks
    work = chans * flat * modes
    shape = lambda *dims: jax.ShapeDtypeStruct(dims, F32)
    scratch = lambda *dims: pltpu.VMEM(dims, F32)
    moved_grads = swap(grad_output.reshape(blocks, chans, block_len), "chan")
    moved_inputs = swap(inputs.reshape(blocks, chans, block_len), "chan")
    flat_grads, coef, ends, span_ends = call(
        functools.partial(ends_kernel, blocks, spans),
        (shape(flat, chans), shape(2 * modes, chans), shape(held, chans), shape(spans, modes, chans)),
        3,
        [scratch(chans, chans)],
        "block_ends",
        2 * work,
    )(moved_grads, pole_values, residue_values)
    all_ends = swap(span_ends, "len")
    rounded = call(
        functools.partial(input_grad_kernel, blocks, spans),
        jax.ShapeDtypeStruct((blocks, chans, block_len), jnp.bfloat16),
        4,
        [scratch(held, chans), scratch(flat, chans)],
        "input_grad",
        4 * work,
    )(flat_grads, coef, ends, all_ends)
    input_grad = swap(rounded, "chan").reshape(blocks * chans, block_len)
    pay = call(
        functools.partial(sums_kernel, blocks, spans),
        shape(spans, 5 * modes, chans),
        4,
        [scratch(flat, chans)] + [scratch(held, chans)] * 5 + [scratch(ROWS, chans)],
        "mode_sums",
        12 * work,
    )(moved_inputs, flat_grads, coef, ends)
    all_pay = swap(pay, "len")
    residue_grad, pole_grad = call(
        functools.partial(finish_kernel, spans, flat),
        (shape(chans, modes), shape(chans, modes)),
        3,
        [scratch(chans, chans)],
        "finish",
        work // 100,
    )(all_pay, all_ends, coef)
    return (input_grad, residue_grad, pole_grad)


def solution(mesh):
    in_specs = (
        P(None, ("len", "chan")),
        P(None, ("len", "chan")),
        P("chan", None),
        P("chan", None),
    )
    out_specs = (P(None, ("len", "chan")), P("chan", None), P("chan", None))
    return jax.shard_map(body, mesh=mesh, in_specs=in_specs, out_specs=out_specs, check_vma=False)
```

time: 394 us -> 108 us (0.27)
  the two profiles are of different devices: /device:TPU:32 before, /device:TPU:1 now
where the time goes in v1:
time: 108 us; the launch traced here: 107 us
  waiting for transfers between devices  38.9 us (36%)
  blocking collectives  27.3 us (25%)
  starting transfers between devices  21.1 us (20%)
  Pallas kernels  16.4 us (15%)
  local copies, waits for them, and re-layouts  2.93 us (3%)
    all_to_all x4, waiting for transfers between devices, swap(): return lax.all_to_all(part, axis, split_axis=0, concat_axis=0, tiled=True)  38.9 us
    all_to_all x1, blocking collectives, swap(): return lax.all_to_all(part, axis, split_axis=0, concat_axis=0, tiled=True)  27.3 us
    all_to_all x4, starting transfers between devices, swap(): return lax.all_to_all(part, axis, split_axis=0, concat_axis=0, tiled=True)  21.1 us
    pallas_call x1, Pallas kernels, body(): call(functools.partial(sums_kernel, blocks, spans), shape(spans, 5 * mode...  9.82 us
    pallas_call x1, Pallas kernels, body(): call(functools.partial(input_grad_kernel, blocks, spans), jax.ShapeDtypeS...  3.81 us
    unnamed x9, local copies, waits for them, and re-layouts  2.93 us
    pallas_call x1, Pallas kernels, body(): call(functools.partial(ends_kernel, blocks, spans), (shape(flat, chans),...  2.49 us
  transfers between devices with their start and end apart: 4, of which 3 were waited for; matrix products, arithmetic and copies ran while one was open for 1% of the time, Pallas kernels for 15%

profile of v1, /device:TPU:1, one launch (start us, length us, event | category | flops | bytes accessed | tf_op | source)
XLA Modules:
  0.0 107.2 jit_solution(2558978871929450706)
XLA Ops:
  0.6 27.3 %all_to_all.25.g_ref = bf16[16,128,128]{2,1,0:T(8,128)(2,1)S(1)} all-to-all(bf16[16,128,128]{2,1,0:T(8,128)(2,1)} %bitcast.4), channel_id=1, replica_groups=mesh['len'=16,'chan'=16] {'chan'}, dimensions={0} | all-to-all | bytes 1048576 | tf_op jit(solution)/shard_map/all_to_all | solution.py:233
  27.9 0.0 copy-start
  27.9 3.6 %all-to-all-start.3 = ((bf16[16,128,128]{2,1,0:T(8,128)(2,1)}), bf16[16,128,128]{2,1,0:T(8,128)(2,1)S(1)}, u32[]{:S(2)}, u32[]{:S(2)}) async-start(bf16[16,128,128]{2,1,0:T(8,128)(2,1)} %bitcast.2), calls=%async_computation.3 | async-start | bytes 1048576 | tf_op jit(solution)/shard_map/all_to_all | solution.py:233
  31.5 0.0 copy-done
  31.6 0.0 copy-start.1
  31.6 0.1 copy.7.pole_ref
  31.7 0.6 copy-done.1
  32.3 0.1 copy.8.res_ref
  32.4 2.5 %block_ends.1 = (f32[2048,128]{1,0:T(8,128)S(1)}, f32[32,128]{1,0:T(8,128)S(1)}, f32[256,128]{1,0:T(8,128)S(1)}, f32[16,16,128]{2,1,0:T(8,128)}) custom-call(bf16[16,128,128]{2,1,0:T(8,128)(2,1)S(1)} %all_to_all.25.g_ref, f32[128,16]{1,0:T(8,128)S(1)} %copy.7.pole_ref, f32[128,16]{1,0:T(8,128)S(1)} %copy.8.res_ref), custom_call_target="tpu_custom_call" | custom-call | flops 8388608 | bytes 1048576 | tf_op jit(solution)/shard_map/block_ends/pallas_call | solution.py:248
  34.8 13.4 %all-to-all-done.3.x_ref = bf16[16,128,128]{2,1,0:T(8,128)(2,1)S(1)} async-done(((bf16[16,128,128]{2,1,0:T(8,128)(2,1)}), bf16[16,128,128]{2,1,0:T(8,128)(2,1)S(1)}, u32[]{:S(2)}, u32[]{:S(2)}) %all-to-all-start.3) | async-done | bytes 524320 | tf_op jit(solution)/shard_map/all_to_all | solution.py:233
  48.2 6.8 %all-to-all-start.1 = ((f32[16,16,128]{2,1,0:T(8,128)}), f32[16,16,128]{2,1,0:T(8,128)S(1)}, u32[]{:S(2)}, u32[]{:S(2)}) async-start(f32[16,16,128]{2,1,0:T(8,128)} %get-tuple-element.12), calls=%async_computation.1 | async-start | bytes 262144 | tf_op jit(solution)/shard_map/all_to_all | solution.py:233
  55.0 9.8 %mode_sums.1 = f32[16,80,128]{2,1,0:T(8,128)} custom-call(bf16[16,128,128]{2,1,0:T(8,128)(2,1)S(1)} %all-to-all-done.3.x_ref, f32[2048,128]{1,0:T(8,128)S(1)} %get-tuple-element.9.gt_ref, f32[32,128]{1,0:T(8,128)S(1)} %get-tuple-element.10.coef_ref, f32[256,128]{1,0:T(8,128)S(1)} %get-tuple-element.11.h_ref), custom_call_target="tpu_custom_call" | custom-call | flops 50331648 | bytes 1048576 | tf_op jit(solution)/shard_map/mode_sums/pallas_call | solution.py:266
  64.8 0.0 all-to-all-done.1.got_ref
  64.8 6.7 %all-to-all-start.4 = ((f32[16,80,128]{2,1,0:T(8,128)}), f32[16,80,128]{2,1,0:T(8,128)S(1)}, u32[]{:S(2)}, u32[]{:S(2)}) async-start(f32[16,80,128]{2,1,0:T(8,128)} %mode_sums.1), calls=%async_computation.4 | async-start | bytes 1310720 | tf_op jit(solution)/shard_map/all_to_all | solution.py:233
  71.5 3.8 %input_grad.1 = bf16[16,128,128]{2,1,0:T(8,128)(2,1)} custom-call(f32[2048,128]{1,0:T(8,128)S(1)} %get-tuple-element.9.gt_ref, f32[32,128]{1,0:T(8,128)S(1)} %get-tuple-element.10.coef_ref, f32[256,128]{1,0:T(8,128)S(1)} %get-tuple-element.11.h_ref, f32[16,16,128]{2,1,0:T(8,128)S(1)} %all-to-all-done.1.got_ref), custom_call_target="tpu_custom_call" | custom-call | flops 16777216 | bytes 1048576 | tf_op jit(solution)/shard_map/input_grad/pallas_call | solution.py:257
  75.3 9.7 %all-to-all-done.4.pay_ref = f32[16,80,128]{2,1,0:T(8,128)S(1)} async-done(((f32[16,80,128]{2,1,0:T(8,128)}), f32[16,80,128]{2,1,0:T(8,128)S(1)}, u32[]{:S(2)}, u32[]{:S(2)}) %all-to-all-start.4) | async-done | bytes 655392 | tf_op jit(solution)/shard_map/all_to_all | solution.py:233
  85.0 4.1 %all-to-all-start.2 = ((bf16[16,128,128]{2,1,0:T(8,128)(2,1)}), bf16[16,128,128]{2,1,0:T(8,128)(2,1)S(1)}, u32[]{:S(2)}, u32[]{:S(2)}) async-start(bf16[16,128,128]{2,1,0:T(8,128)(2,1)} %input_grad.1), calls=%async_computation.2 | async-start | bytes 1048576 | tf_op jit(solution)/shard_map/all_to_all | solution.py:233
  89.1 0.3 finish.1
  89.4 0.7 copy.9
  90.0 0.7 copy.10
  90.7 15.7 %all-to-all-done.2 = bf16[16,128,128]{2,1,0:T(8,128)(2,1)S(1)} async-done(((bf16[16,128,128]{2,1,0:T(8,128)(2,1)}), bf16[16,128,128]{2,1,0:T(8,128)(2,1)S(1)}, u32[]{:S(2)}, u32[]{:S(2)}) %all-to-all-start.2) | async-done | bytes 524320 | tf_op jit(solution)/shard_map/all_to_all | solution.py:233
  106.4 0.8 copy.12
Async XLA Ops:
  27.9 3.6 %copy-start = (f32[128,16]{0,1:T(8,128)S(1)}, f32[128,16]{0,1:T(8,128)}, u32[]{:S(2)}) copy-start(f32[128,16]{0,1:T(8,128)} %param.6) | copy-start | bytes 24580
  27.9 20.3 %all-to-all-start.3 = ((bf16[16,128,128]{2,1,0:T(8,128)(2,1)}), bf16[16,128,128]{2,1,0:T(8,128)(2,1)S(1)}, u32[]{:S(2)}, u32[]{:S(2)}) async-start(bf16[16,128,128]{2,1,0:T(8,128)(2,1)} %bitcast.2), calls=%async_computation.3 | async-start | bytes 1048576 | tf_op jit(solution)/shard_map/all_to_all | solution.py:233
  31.6 0.7 copy-start.1
  48.2 16.6 %all-to-all-start.1 = ((f32[16,16,128]{2,1,0:T(8,128)}), f32[16,16,128]{2,1,0:T(8,128)S(1)}, u32[]{:S(2)}, u32[]{:S(2)}) async-start(f32[16,16,128]{2,1,0:T(8,128)} %get-tuple-element.12), calls=%async_computation.1 | async-start | bytes 262144 | tf_op jit(solution)/shard_map/all_to_all | solution.py:233
  64.8 20.2 %all-to-all-start.4 = ((f32[16,80,128]{2,1,0:T(8,128)}), f32[16,80,128]{2,1,0:T(8,128)S(1)}, u32[]{:S(2)}, u32[]{:S(2)}) async-start(f32[16,80,128]{2,1,0:T(8,128)} %mode_sums.1), calls=%async_computation.4 | async-start | bytes 1310720 | tf_op jit(solution)/shard_map/all_to_all | solution.py:233
  85.0 21.4 %all-to-all-start.2 = ((bf16[16,128,128]{2,1,0:T(8,128)(2,1)}), bf16[16,128,128]{2,1,0:T(8,128)(2,1)S(1)}, u32[]{:S(2)}, u32[]{:S(2)}) async-start(bf16[16,128,128]{2,1,0:T(8,128)(2,1)} %input_grad.1), calls=%async_computation.2 | async-start | bytes 1048576 | tf_op jit(solution)/shard_map/all_to_all | solution.py:233

commit v2 on v1

v2 whole, which is shorter than its diff:
```python
import functools
import math

import jax
import jax.numpy as jnp
from jax import lax
from jax.experimental import pallas as pl
from jax.experimental.pallas import tpu as pltpu
from jax.sharding import PartitionSpec as P

ROWS = 8
GROUP = 8
F32 = jnp.float32
VMEM = pl.BlockSpec(memory_space=pltpu.VMEM)


def identity_matrix(size):
    rows = lax.broadcasted_iota(jnp.int32, (size, size), 0)
    cols = lax.broadcasted_iota(jnp.int32, (size, size), 1)
    return (rows == cols).astype(F32).astype(jnp.bfloat16)


def flip(eye, tile):
    return lax.dot_general(eye, tile, (((1,), (1,)), ((), ())), preferred_element_type=F32)


def flip_blocks(src_ref, dst_ref):
    blocks, _, block_len = src_ref.shape
    eye = identity_matrix(block_len)
    for n in range(blocks):
        dst_ref[pl.ds(n, block_len, stride=blocks), :] = flip(eye, src_ref[n])


def log_rates(poles):
    return jnp.log1p(-(1.0 - poles))


def spread(ref, p):
    return jnp.broadcast_to(ref[p : p + 1, :], (ROWS, ref.shape[1]))


def cleared(ref, count):
    ref[:ROWS, :] = jnp.zeros((ROWS, ref.shape[1]), F32)
    return (ref[:ROWS, :],) * count


def block_rows(ref, n, blocks, modes):
    return ref[pl.ds(n, modes, stride=blocks), :]


def ends_kernel(blocks, moved_ref, lam_ref, gt_ref, h_ref, head_ref):
    modes = lam_ref.shape[0]
    block_len = moved_ref.shape[2]
    flip_blocks(moved_ref, gt_ref)
    empty = cleared(h_ref, modes)
    for half in range(blocks // ROWS):
        wide = [spread(lam_ref, p) for p in range(modes)]

        def back(i, held):
            at = pl.multiple_of((block_len - 1 - i) * blocks + half * ROWS, ROWS)
            g = gt_ref[pl.ds(at, ROWS), :]
            return tuple(l * a + g for l, a in zip(wide, held))

        ends = lax.fori_loop(0, block_len, back, empty, unroll=8)
        for p in range(modes):
            at = p * blocks + half * ROWS
            h_ref[at : at + ROWS, :] = ends[p]
    step = jnp.exp(block_len * log_rates(lam_ref[...]))
    head_ref[...] = folded(step, [block_rows(h_ref, n, blocks, modes) for n in range(blocks)])


def folded(step, heads):
    total = heads[-1]
    for head in heads[-2::-1]:
        total = step * total + head
    return total


def weighted_kernel(blocks, gt_ref, lam_ref, t_ref):
    modes = lam_ref.shape[0]
    block_len = gt_ref.shape[0] // blocks
    empty = cleared(t_ref, GROUP)
    for half in range(blocks // ROWS):
        for first in range(0, modes, GROUP):
            wide = [spread(lam_ref, first + k) for k in range(GROUP)]

            def back(i, held):
                at = pl.multiple_of((block_len - 1 - i) * blocks + half * ROWS, ROWS)
                g = gt_ref[pl.ds(at, ROWS), :]
                adjoint, weighted = held
                adjoint = tuple(l * a + g for l, a in zip(wide, adjoint))
                weighted = tuple(l * q + a for l, q, a in zip(wide, weighted, adjoint))
                return (adjoint, weighted)

            weighted = lax.fori_loop(0, block_len, back, (empty,) * 2, unroll=8)[1]
            for k in range(GROUP):
                at = (first + k) * blocks + half * ROWS
                t_ref[at : at + ROWS, :] = weighted[k]


def near_kernel(span_len, *refs):
    *parts, lam_ref, _, all_ref, near_ref, group_ref = refs
    count = len(parts)
    place = lax.rem(lax.axis_index("len"), count)
    heads = ordered(parts, place, all_ref)
    step = jnp.exp(span_len * log_rates(lam_ref[...]))
    group_ref[...] = folded(step, heads)
    near_ref[...] = folded_after(step, heads, place)


def folded_after(step, heads, place):
    total = jnp.zeros(step.shape, F32)
    for i in range(len(heads) - 1, 0, -1):
        total = jnp.where(i > place, step * total + heads[i], total)
    return total


def input_grad_kernel(blocks, inner, outer, *refs):
    *parts, near_ref, gt_ref, lam_ref, res_ref, h_ref, _, out_ref, all_ref, next_ref, flat_ref = refs
    modes, chans = lam_ref.shape
    block_len = gt_ref.shape[0] // blocks
    span_len = blocks * block_len
    rate = log_rates(lam_ref[...])
    block_step = jnp.exp(block_len * rate)
    place = lax.axis_index("len")
    at_inner = lax.rem(place, inner)
    at_outer = lax.div(place, inner)
    heads = ordered(parts, at_outer, all_ref)
    far = folded_after(jnp.exp((inner * span_len) * rate), heads, at_outer)
    reach = (span_len * (inner - 1 - at_inner)).astype(F32)
    total = near_ref[...] + jnp.exp(reach * rate) * far
    for n in range(blocks - 1, -1, -1):
        next_ref[pl.ds(n, modes, stride=blocks), :] = total
        total = block_step * total + block_rows(h_ref, n, blocks, modes)
    for half in range(blocks // ROWS):
        wide = [spread(lam_ref, p) for p in range(modes)]
        gain = [spread(res_ref, p) for p in range(modes)]
        start = tuple(
            next_ref[p * blocks + half * ROWS : p * blocks + half * ROWS + ROWS, :]
            for p in range(modes)
        )

        def step(i, held):
            at = pl.multiple_of((block_len - 1 - i) * blocks + half * ROWS, ROWS)
            g = gt_ref[pl.ds(at, ROWS), :]
            held = tuple(l * a + g for l, a in zip(wide, held))
            terms = [r * a for r, a in zip(gain, held)]
            while len(terms) > 1:
                terms = [a + b for a, b in zip(terms[::2], terms[1::2])]
            flat_ref[pl.ds(at, ROWS), :] = terms[0]
            return held

        lax.fori_loop(0, block_len, step, start, unroll=4)
    eye = identity_matrix(chans)
    for n in range(blocks):
        tile = flat_ref[pl.ds(n, block_len, stride=blocks), :].astype(jnp.bfloat16)
        out_ref[n] = flip(eye, tile).astype(jnp.bfloat16)


def mode_sums(first, blocks, x_ref, gt_ref, lam_ref, h_ref, t_ref, parts_refs):
    block_len = gt_ref.shape[0] // blocks
    lam = lam_ref[first : first + GROUP, :]
    empty = cleared(parts_refs[0], GROUP)
    wide = [spread(lam_ref, first + k) for k in range(GROUP)]
    for half in range(blocks // ROWS):

        def ahead(i, held):
            at = pl.multiple_of(i * blocks + half * ROWS, ROWS)
            g = gt_ref[pl.ds(at, ROWS), :]
            x = x_ref[pl.ds(at, ROWS), :]
            state, slope, res_sum, pole_sum = held
            slope = tuple(l * d + s for l, d, s in zip(wide, slope, state))
            state = tuple(l * s + x for l, s in zip(wide, state))
            res_sum = tuple(r + g * s for r, s in zip(res_sum, state))
            pole_sum = tuple(q + g * d for q, d in zip(pole_sum, slope))
            return (state, slope, res_sum, pole_sum)

        results = lax.fori_loop(0, block_len, ahead, (empty,) * 4, unroll=8)
        for k in range(GROUP):
            at = k * blocks + half * ROWS
            for ref, result in zip(parts_refs, results):
                ref[at : at + ROWS, :] = result[k]
    rate = log_rates(lam)
    block_step = jnp.exp(block_len * rate)
    block_slope = block_len * jnp.exp((block_len - 1) * rate)
    own = lambda ref, n: ref[pl.ds(n, GROUP, stride=blocks), :]
    of_all = lambda ref, n: ref[pl.ds(first * blocks + n, GROUP, stride=blocks), :]
    s_ref, d_ref, r_ref, q_ref = parts_refs
    state, slope, res_sum, pole_sum, total, weighted = [jnp.zeros(lam.shape, F32)] * 6
    for n in range(blocks):
        after = lam * of_all(h_ref, n)
        res_sum = res_sum + (own(r_ref, n) + state * after)
        pole_sum = pole_sum + (own(q_ref, n) + slope * after + state * of_all(t_ref, n))
        slope = block_step * slope + block_slope * state + own(d_ref, n)
        state = block_step * state + own(s_ref, n)
    for n in range(blocks - 1, -1, -1):
        weighted = block_step * (weighted + block_len * total) + of_all(t_ref, n)
        total = block_step * total + of_all(h_ref, n)
    return state, slope, res_sum, pole_sum, weighted


def sums_first_kernel(blocks, moved_ref, gt_ref, lam_ref, h_ref, t_ref, xt_ref, pay_ref, *parts):
    flip_blocks(moved_ref, xt_ref)
    for k, item in enumerate(mode_sums(0, blocks, xt_ref, gt_ref, lam_ref, h_ref, t_ref, parts)):
        pay_ref[k * GROUP : (k + 1) * GROUP, :] = item


def sums_rest_kernel(blocks, xt_ref, gt_ref, lam_ref, h_ref, t_ref, first_ref, _, pay_ref, *parts):
    modes = lam_ref.shape[0]
    for k in range(5):
        pay_ref[k * modes : k * modes + GROUP, :] = first_ref[k * GROUP : (k + 1) * GROUP, :]
    for first in range(GROUP, modes, GROUP):
        items = mode_sums(first, blocks, xt_ref, gt_ref, lam_ref, h_ref, t_ref, parts)
        for k, item in enumerate(items):
            pay_ref[k * modes + first : k * modes + first + GROUP, :] = item


def ordered(refs, place, slots_ref):
    count = len(refs)
    for s, ref in enumerate(refs):
        slots_ref[lax.rem(place + count - s, count)] = ref[...]
    return [slots_ref[i] for i in range(count)]


def joined(lam, length, parts, heads):
    modes = lam.shape[0]
    rate = log_rates(lam)
    step = jnp.exp(length * rate)
    slope_step = length * jnp.exp((length - 1) * rate)
    state, slope, res_sum, pole_sum = [jnp.zeros(lam.shape, F32)] * 4
    tables = [[part[k * modes : (k + 1) * modes, :] for k in range(5)] for part in parts]
    for (ends, slopes, res_part, pole_part, weighted), head in zip(tables, heads):
        after = lam * head
        res_sum = res_sum + (res_part + state * after)
        pole_sum = pole_sum + (pole_part + slope * after + state * weighted)
        slope = step * slope + slope_step * state + slopes
        state = step * state + ends
    total = jnp.zeros(lam.shape, F32)
    weighted = total
    for table, head in zip(tables[::-1], heads[::-1]):
        weighted = step * (weighted + length * total) + table[4]
        total = step * total + head
    return state, slope, res_sum, pole_sum, weighted


def join_kernel(span_len, *refs):
    *parts, heads_ref, lam_ref, pay_ref, slots_ref = refs
    modes = lam_ref.shape[0]
    count = len(parts)
    parts = ordered(parts, lax.rem(lax.axis_index("len"), count), slots_ref)
    heads = [heads_ref[i] for i in range(count)]
    for k, item in enumerate(joined(lam_ref[...], span_len, parts, heads)):
        pay_ref[k * modes : (k + 1) * modes, :] = item


def finish_kernel(inner, group_len, *refs):
    *parts, heads_ref, lam_ref, res_ref, res_out, pole_out, slots_ref = refs
    count = len(parts)
    lam = lam_ref[...]
    parts = ordered(parts, lax.div(lax.axis_index("len"), inner), slots_ref)
    heads = [heads_ref[i] for i in range(count)]
    _, _, res_sum, pole_sum, _ = joined(lam, group_len, parts, heads)
    width = (1.0 - lam) * (1.0 + lam)
    scale = 1.0 / math.sqrt(count * group_len)
    res_out[...] = res_sum * jnp.sqrt(width) * scale
    pole_out[...] = res_ref[...] * pole_sum * width * scale


def call(kernel, out_shape, in_count, scratch, name, flops):
    single = not isinstance(out_shape, (tuple, list))
    return pl.pallas_call(
        kernel,
        out_shape=out_shape,
        in_specs=[VMEM] * in_count,
        out_specs=VMEM if single else [VMEM] * len(out_shape),
        scratch_shapes=scratch,
        compiler_params=pltpu.CompilerParams(vmem_limit_bytes=32 * 1024 * 1024),
        cost_estimate=pl.CostEstimate(flops=flops, bytes_accessed=2**20, transcendentals=0),
        name=name,
    )


def swap(part, axis):
    return lax.all_to_all(part, axis, split_axis=0, concat_axis=0, tiled=True)


def rotated(part, count, stride, spans):
    size = count * stride
    hop = lambda i, s: (i // size) * size + (i % size + s * stride) % size
    return [
        lax.ppermute(part, "len", [(i, hop(i, s)) for i in range(spans)]) for s in range(1, count)
    ]


def body(inputs, grad_output, pole_values, residue_values):
    spans = lax.axis_size("len")
    blocks = lax.axis_size("chan")
    inner = math.isqrt(spans)
    outer = spans // inner
    chans, modes = pole_values.shape
    block_len = inputs.shape[1]
    flat = blocks * block_len
    held = modes * blocks
    work = chans * flat * modes
    shape = lambda *dims: jax.ShapeDtypeStruct(dims, F32)
    scratch = lambda *dims: pltpu.VMEM(dims, F32)
    cut = lambda part: part.reshape(blocks, chans, block_len)
    table = shape(modes, chans)
    poles = pole_values.T
    residues = residue_values.T
    moved_grads = swap(cut(grad_output), "chan")
    moved_inputs = swap(cut(inputs), "chan")
    flat_grads, ends, head = call(
        functools.partial(ends_kernel, blocks),
        (shape(flat, chans), shape(held, chans), table),
        2,
        [],
        "block_ends",
        2 * work,
    )(moved_grads, poles)
    weighted = call(
        functools.partial(weighted_kernel, blocks),
        shape(held, chans),
        2,
        [],
        "weighted",
        4 * work,
    )(flat_grads, poles)
    heads, near, group_head = call(
        functools.partial(near_kernel, flat),
        (shape(inner, modes, chans), table, table),
        inner + 2,
        [],
        "near",
        work // 100,
    )(head, *rotated(head, inner, 1, spans), poles, weighted)
    flat_inputs, first_pay = call(
        functools.partial(sums_first_kernel, blocks),
        (shape(flat, chans), shape(5 * GROUP, chans)),
        5,
        [scratch(GROUP * blocks, chans)] * 4,
        "sums_first",
        4 * work,
    )(moved_inputs, flat_grads, poles, ends, weighted)
    rounded, group_heads = call(
        functools.partial(input_grad_kernel, blocks, inner, outer),
        (jax.ShapeDtypeStruct((blocks, chans, block_len), jnp.bfloat16), shape(outer, modes, chans)),
        outer + 6,
        [scratch(held, chans), scratch(flat, chans)],
        "input_grad",
        4 * work,
    )(
        group_head,
        *rotated(group_head, outer, inner, spans),
        near,
        flat_grads,
        poles,
        residues,
        ends,
        first_pay,
    )
    input_grad = swap(rounded, "chan").reshape(blocks * chans, block_len)
    pay = call(
        functools.partial(sums_rest_kernel, blocks),
        shape(5 * modes, chans),
        7,
        [scratch(GROUP * blocks, chans)] * 4,
        "sums_rest",
        4 * work,
    )(flat_inputs, flat_grads, poles, ends, weighted, first_pay, group_heads)
    group_pay = call(
        functools.partial(join_kernel, flat),
        shape(5 * modes, chans),
        inner + 2,
        [scratch(inner, 5 * modes, chans)],
        "join",
        work // 100,
    )(pay, *rotated(pay, inner, 1, spans), heads, poles)
    residue_grad, pole_grad = call(
        functools.partial(finish_kernel, inner, inner * flat),
        (table, table),
        outer + 3,
        [scratch(outer, 5 * modes, chans)],
        "finish",
        work // 100,
    )(group_pay, *rotated(group_pay, outer, inner, spans), group_heads, poles, residues)
    return (input_grad, residue_grad.T, pole_grad.T)


def solution(mesh):
    in_specs = (
        P(None, ("len", "chan")),
        P(None, ("len", "chan")),
        P("chan", None),
        P("chan", None),
    )
    out_specs = (P(None, ("len", "chan")), P("chan", None), P("chan", None))
    return jax.shard_map(body, mesh=mesh, in_specs=in_specs, out_specs=out_specs, check_vma=False)
```

time: 108 us -> 81.2 us (0.75)
  waiting for transfers between devices: 38.9 us -> 13.3 us
  starting transfers between devices: 21.1 us -> 23.1 us
  Pallas kernels: 16.4 us -> 14.4 us
    all_to_all x4 -> x2, waiting for transfers between devices: 38.9 us -> 3.88 us  [swap(): return lax.all_to_all(part, axis, split_axis=0, concat_axis=0, tiled=True)]
    ppermute x0 -> x12, starting transfers between devices: none -> 13.8 us  [rotated(): lax.ppermute(part, 'len', [(i, hop(i, s)) for i in range(spans)])]
    all_to_all x4 -> x2, starting transfers between devices: 21.1 us -> 9.27 us  [swap(): return lax.all_to_all(part, axis, split_axis=0, concat_axis=0, tiled=True)]
    ppermute x0 -> x12, waiting for transfers between devices: none -> 9.37 us  [rotated(): lax.ppermute(part, 'len', [(i, hop(i, s)) for i in range(spans)])]
    pallas_call x4 -> x8, Pallas kernels: 16.4 us -> 14.4 us  [the longest x1 3.78 us: body(): call(functools.partial(input_grad_kernel, blocks, inner, outer), (jax.Sha...]
    unnamed x9 -> x5, local copies, waits for them, and re-layouts: 2.93 us -> 1.88 us
  transfers between devices with their start and end apart: 4 -> 14, of which waited for: 3 -> 9; matrix products, arithmetic and copies ran while one was open for 1% -> 0% of each run, Pallas kernels for 15% -> 13%
where the time goes in v2:
time: 81.2 us; the launch traced here: 80.6 us
  blocking collectives  27.3 us (34%)
  starting transfers between devices  23.1 us (28%)
  Pallas kernels  14.4 us (18%)
  waiting for transfers between devices  13.3 us (16%)
  local copies, waits for them, and re-layouts  1.88 us (2%)
    all_to_all x1, blocking collectives, swap(): return lax.all_to_all(part, axis, split_axis=0, concat_axis=0, tiled=True)  27.3 us
    ppermute x12, starting transfers between devices, rotated(): lax.ppermute(part, 'len', [(i, hop(i, s)) for i in range(spans)])  13.8 us
    ppermute x12, waiting for transfers between devices, rotated(): lax.ppermute(part, 'len', [(i, hop(i, s)) for i in range(spans)])  9.37 us
    all_to_all x2, starting transfers between devices, swap(): return lax.all_to_all(part, axis, split_axis=0, concat_axis=0, tiled=True)  9.27 us
    all_to_all x2, waiting for transfers between devices, swap(): return lax.all_to_all(part, axis, split_axis=0, concat_axis=0, tiled=True)  3.88 us
    pallas_call x1, Pallas kernels, body(): call(functools.partial(input_grad_kernel, blocks, inner, outer), (jax.Sha...  3.78 us
    pallas_call x1, Pallas kernels, body(): call(functools.partial(sums_first_kernel, blocks), (shape(flat, chans), s...  3.17 us
    pallas_call x1, Pallas kernels, body(): call(functools.partial(sums_rest_kernel, blocks), shape(5 * modes, chans)...  2.6 us
  transfers between devices with their start and end apart: 14, of which 9 were waited for; matrix products, arithmetic and copies ran while one was open for 0% of the time, Pallas kernels for 13%

profile of v2, /device:TPU:1, one launch (start us, length us, event | category | flops | bytes accessed | tf_op | source)
XLA Modules:
  0.0 80.6 jit_solution(1251499420424383286)
XLA Ops:
  0.6 27.3 %all_to_all.15.moved_ref = bf16[16,128,128]{2,1,0:T(8,128)(2,1)S(1)} all-to-all(bf16[16,128,128]{2,1,0:T(8,128)(2,1)} %bitcast.17), channel_id=1, replica_groups=mesh['len'=16,'chan'=16] {'chan'}, dimensions={0} | all-to-all | bytes 1048576 | tf_op jit(solution)/shard_map/all_to_all | solution.py:284
  27.9 0.0 copy-start
  27.9 3.6 %all-to-all-start.1 = ((bf16[16,128,128]{2,1,0:T(8,128)(2,1)}), bf16[16,128,128]{2,1,0:T(8,128)(2,1)S(1)}, u32[]{:S(2)}, u32[]{:S(2)}) async-start(bf16[16,128,128]{2,1,0:T(8,128)(2,1)} %bitcast.3), calls=%async_computation.1 | async-start | bytes 1048576 | tf_op jit(solution)/shard_map/all_to_all | solution.py:284
  31.5 0.0 copy-done
  31.6 1.8 %block_ends.1 = (f32[2048,128]{1,0:T(8,128)S(1)}, f32[256,128]{1,0:T(8,128)S(1)}, f32[16,128]{1,0:T(8,128)S(1)}) custom-call(bf16[16,128,128]{2,1,0:T(8,128)(2,1)S(1)} %all_to_all.15.moved_ref, f32[16,128]{1,0:T(8,128)S(1)} %bitcast.7), custom_call_target="tpu_custom_call" | custom-call | flops 8388608 | bytes 1048576 | tf_op jit(solution)/shard_map/block_ends/pallas_call | solution.py:313
  33.4 2.6 %collective-permute-start.2 = (f32[16,128]{1,0:T(8,128)S(1)}, f32[16,128]{1,0:T(8,128)S(1)}, u32[]{:S(2)}, u32[]{:S(2)}) collective-permute-start(f32[16,128]{1,0:T(8,128)S(1)} %get-tuple-element.15.refs_0_), channel_id=1, source_target_pairs={{0,48},{16,0},{32,16},{48,32},{64,112},{80,64},{96,80},{112,96},{1... | collective-permute-start | bytes 24584 | tf_op jit(solution)/shard_map/ppermute | solution.py:291
  35.9 0.5 collective-permute-start.1
  36.4 0.6 collective-permute-start
  37.1 2.3 %weighted.1.refs_5_.t_ref = f32[256,128]{1,0:T(8,128)S(1)} custom-call(f32[2048,128]{1,0:T(8,128)S(1)} %get-tuple-element.16.gt_ref.refs_5_, f32[16,128]{1,0:T(8,128)S(1)} %bitcast.8), custom_call_target="tpu_custom_call" | custom-call | flops 16777216 | bytes 1048576 | tf_op jit(solution)/shard_map/weighted/pallas_call | solution.py:321
  39.4 0.0 collective-permute-done.2.refs_3_
  39.4 0.9 %collective-permute-done.1.refs_2_ = f32[16,128]{1,0:T(8,128)S(1)} collective-permute-done((f32[16,128]{1,0:T(8,128)S(1)}, f32[16,128]{1,0:T(8,128)S(1)}, u32[]{:S(2)}, u32[]{:S(2)}) %collective-permute-start.1) | collective-permute-done | bytes 8224 | tf_op jit(solution)/shard_map/ppermute | solution.py:291
  40.2 0.2 collective-permute-done.refs_1_
  40.5 2.8 %collective-permute-start.5 = (f32[16,128]{1,0:T(8,128)S(1)}, f32[16,128]{1,0:T(8,128)S(1)}, u32[]{:S(2)}, u32[]{:S(2)}) collective-permute-start(f32[16,128]{1,0:T(8,128)S(1)} %get-tuple-element.17.refs_0_), channel_id=1, source_target_pairs={{0,192},{16,208},{32,224},{48,240},{64,0},{80,16},{96,32},{112,48}... | collective-permute-start | bytes 24584 | tf_op jit(solution)/shard_map/ppermute | solution.py:291
  43.3 0.3 collective-permute-start.4
  43.7 0.7 collective-permute-start.3
  44.4 3.9 %all-to-all-done.1.moved_ref = bf16[16,128,128]{2,1,0:T(8,128)(2,1)S(1)} async-done(((bf16[16,128,128]{2,1,0:T(8,128)(2,1)}), bf16[16,128,128]{2,1,0:T(8,128)(2,1)S(1)}, u32[]{:S(2)}, u32[]{:S(2)}) %all-to-all-start.1) | async-done | bytes 524320 | tf_op jit(solution)/shard_map/all_to_all | solution.py:284
  48.2 0.0 copy-start.1
  48.3 3.2 %sums_first.1 = (f32[2048,128]{1,0:T(8,128)S(1)}, f32[40,128]{1,0:T(8,128)S(1)}) custom-call(bf16[16,128,128]{2,1,0:T(8,128)(2,1)S(1)} %all-to-all-done.1.moved_ref, f32[2048,128]{1,0:T(8,128)S(1)} %get-tuple-element.16.gt_ref.refs_5_, f32[16,128]{1,0:T(8,128)S(1)} %bitcast.10, f32[256,128]{1,0:T(8,128)S(1)} %get-tuple-element.19.h_ref.refs_8_, ...), custom_call_target="tpu_custom_call" | custom-call | flops 16777216 | bytes 1048576 | tf_op jit(solution)/shard_map/sums_first/pallas_call | solution.py:337
  51.4 0.0 collective-permute-done.5.refs_3_
  51.4 0.0 collective-permute-done.4.refs_2_
  51.4 0.0 collective-permute-done.3.refs_1_
  51.4 0.0 copy-done.1
  51.5 3.8 %input_grad.1 = (bf16[16,128,128]{2,1,0:T(8,128)(2,1)}, f32[4,16,128]{2,1,0:T(8,128)S(1)}) custom-call(f32[16,128]{1,0:T(8,128)S(1)} %get-tuple-element.17.refs_0_, f32[16,128]{1,0:T(8,128)S(1)} %collective-permute-done.3.refs_1_, f32[16,128]{1,0:T(8,128)S(1)} %collective-permute-done.4.refs_2_, f32[16,128]{1,0:T(8,128)S(1)} %collective-permute-done.5.refs_3_, ...), custom_call_target="tpu_custom_call" | custom-call | flops 16777216 | bytes 1048576 | tf_op jit(solution)/shard_map/input_grad/pallas_call | solution.py:345
  55.2 5.7 %all-to-all-start.2 = ((bf16[16,128,128]{2,1,0:T(8,128)(2,1)}), bf16[16,128,128]{2,1,0:T(8,128)(2,1)}, u32[]{:S(2)}, u32[]{:S(2)}) async-start(bf16[16,128,128]{2,1,0:T(8,128)(2,1)} %get-tuple-element.21), calls=%async_computation.2 | async-start | bytes 1048576 | tf_op jit(solution)/shard_map/all_to_all | solution.py:284
  60.9 2.6 %sums_rest.1.refs_0_ = f32[80,128]{1,0:T(8,128)S(1)} custom-call(f32[2048,128]{1,0:T(8,128)S(1)} %get-tuple-element.22.xt_ref, f32[2048,128]{1,0:T(8,128)S(1)} %get-tuple-element.16.gt_ref.refs_5_, f32[16,128]{1,0:T(8,128)S(1)} %bitcast.12, f32[256,128]{1,0:T(8,128)S(1)} %get-tuple-element.19.h_ref.refs_8_, f32[256,128]{1,0:T(8,128)S(1)} %weighted.1.refs_5_.t_ref, ...), custom_call_target="tpu_custom_call" | custom-call | flops 16777216 | bytes 1048576 | tf_op jit(solution)/shard_map/sums_rest/pallas_call | solution.py:363
  63.5 1.0 %collective-permute-start.8 = (f32[80,128]{1,0:T(8,128)S(1)}, f32[80,128]{1,0:T(8,128)S(1)}, u32[]{:S(2)}, u32[]{:S(2)}) collective-permute-start(f32[80,128]{1,0:T(8,128)S(1)} %sums_rest.1.refs_0_), channel_id=1, source_target_pairs={{0,48},{16,0},{32,16},{48,32},{64,112},{80,64},{96,80},{112,96},{1... | collective-permute-start | bytes 122888 | tf_op jit(solution)/shard_map/ppermute | solution.py:291
  64.6 0.7 collective-permute-start.7
  65.2 0.4 collective-permute-start.6
  65.7 1.1 %collective-permute-done.8.refs_3_ = f32[80,128]{1,0:T(8,128)S(1)} collective-permute-done((f32[80,128]{1,0:T(8,128)S(1)}, f32[80,128]{1,0:T(8,128)S(1)}, u32[]{:S(2)}, u32[]{:S(2)}) %collective-permute-start.8) | collective-permute-done | bytes 40992 | tf_op jit(solution)/shard_map/ppermute | solution.py:291
  66.8 2.6 %collective-permute-done.7.refs_2_ = f32[80,128]{1,0:T(8,128)S(1)} collective-permute-done((f32[80,128]{1,0:T(8,128)S(1)}, f32[80,128]{1,0:T(8,128)S(1)}, u32[]{:S(2)}, u32[]{:S(2)}) %collective-permute-start.7) | collective-permute-done | bytes 40992 | tf_op jit(solution)/shard_map/ppermute | solution.py:291
  69.4 0.8 collective-permute-done.6.refs_1_
  70.2 0.1 join.1.refs_0_
  70.3 3.1 %collective-permute-start.11 = (f32[80,128]{1,0:T(8,128)S(1)}, f32[80,128]{1,0:T(8,128)S(1)}, u32[]{:S(2)}, u32[]{:S(2)}) collective-permute-start(f32[80,128]{1,0:T(8,128)S(1)} %join.1.refs_0_), channel_id=1, source_target_pairs={{0,192},{16,208},{32,224},{48,240},{64,0},{80,16},{96,32},{112,48}... | collective-permute-start | bytes 122888 | tf_op jit(solution)/shard_map/ppermute | solution.py:291
  73.3 0.3 collective-permute-start.10
  73.6 0.8 collective-permute-start.9
  74.4 0.1 collective-permute-done.11.refs_3_
  74.4 3.4 %collective-permute-done.10.refs_2_ = f32[80,128]{1,0:T(8,128)S(1)} collective-permute-done((f32[80,128]{1,0:T(8,128)S(1)}, f32[80,128]{1,0:T(8,128)S(1)}, u32[]{:S(2)}, u32[]{:S(2)}) %collective-permute-start.10) | collective-permute-done | bytes 40992 | tf_op jit(solution)/shard_map/ppermute | solution.py:291
  77.8 0.3 collective-permute-done.9.refs_1_
  78.1 0.6 finish.1
  78.7 0.0 all-to-all-done.2
  78.8 1.9 %copy.8 = bf16[2048,128]{1,0:T(8,128)(2,1)} copy(bf16[2048,128]{1,0:T(8,128)(2,1)} %bitcast.4) | data formatting | bytes 1048576
  (1 shorter events, 0.0 us)
Async XLA Ops:
  27.9 3.6 %copy-start = (f32[128,16]{0,1:T(8,128)S(1)}, f32[128,16]{0,1:T(8,128)}, u32[]{:S(2)}) copy-start(f32[128,16]{0,1:T(8,128)} %param.6) | copy-start | bytes 24580
  27.9 20.3 %all-to-all-start.1 = ((bf16[16,128,128]{2,1,0:T(8,128)(2,1)}), bf16[16,128,128]{2,1,0:T(8,128)(2,1)S(1)}, u32[]{:S(2)}, u32[]{:S(2)}) async-start(bf16[16,128,128]{2,1,0:T(8,128)(2,1)} %bitcast.3), calls=%async_computation.1 | async-start | bytes 1048576 | tf_op jit(solution)/shard_map/all_to_all | solution.py:284
  33.4 6.0 %collective-permute-start.2 = (f32[16,128]{1,0:T(8,128)S(1)}, f32[16,128]{1,0:T(8,128)S(1)}, u32[]{:S(2)}, u32[]{:S(2)}) collective-permute-start(f32[16,128]{1,0:T(8,128)S(1)} %get-tuple-element.15.refs_0_), channel_id=1, source_target_pairs={{0,48},{16,0},{32,16},{48,32},{64,112},{80,64},{96,80},{112,96},{1... | collective-permute-start | bytes 24584 | tf_op jit(solution)/shard_map/ppermute | solution.py:291
  35.9 4.3 %collective-permute-start.1 = (f32[16,128]{1,0:T(8,128)S(1)}, f32[16,128]{1,0:T(8,128)S(1)}, u32[]{:S(2)}, u32[]{:S(2)}) collective-permute-start(f32[16,128]{1,0:T(8,128)S(1)} %get-tuple-element.15.refs_0_), channel_id=1, source_target_pairs={{0,32},{16,48},{32,0},{48,16},{64,96},{80,112},{96,64},{112,80},{1... | collective-permute-start | bytes 24584 | tf_op jit(solution)/shard_map/ppermute | solution.py:291
  36.4 4.0 %collective-permute-start = (f32[16,128]{1,0:T(8,128)S(1)}, f32[16,128]{1,0:T(8,128)S(1)}, u32[]{:S(2)}, u32[]{:S(2)}) collective-permute-start(f32[16,128]{1,0:T(8,128)S(1)} %get-tuple-element.15.refs_0_), channel_id=1, source_target_pairs={{0,16},{16,32},{32,48},{48,0},{64,80},{80,96},{96,112},{112,64},{1... | collective-permute-start | bytes 24584 | tf_op jit(solution)/shard_map/ppermute | solution.py:291
  40.5 10.9 %collective-permute-start.5 = (f32[16,128]{1,0:T(8,128)S(1)}, f32[16,128]{1,0:T(8,128)S(1)}, u32[]{:S(2)}, u32[]{:S(2)}) collective-permute-start(f32[16,128]{1,0:T(8,128)S(1)} %get-tuple-element.17.refs_0_), channel_id=1, source_target_pairs={{0,192},{16,208},{32,224},{48,240},{64,0},{80,16},{96,32},{112,48}... | collective-permute-start | bytes 24584 | tf_op jit(solution)/shard_map/ppermute | solution.py:291
  43.3 8.1 %collective-permute-start.4 = (f32[16,128]{1,0:T(8,128)S(1)}, f32[16,128]{1,0:T(8,128)S(1)}, u32[]{:S(2)}, u32[]{:S(2)}) collective-permute-start(f32[16,128]{1,0:T(8,128)S(1)} %get-tuple-element.17.refs_0_), channel_id=1, source_target_pairs={{0,128},{16,144},{32,160},{48,176},{64,192},{80,208},{96,224},{112... | collective-permute-start | bytes 24584 | tf_op jit(solution)/shard_map/ppermute | solution.py:291
  43.7 7.8 %collective-permute-start.3 = (f32[16,128]{1,0:T(8,128)S(1)}, f32[16,128]{1,0:T(8,128)S(1)}, u32[]{:S(2)}, u32[]{:S(2)}) collective-permute-start(f32[16,128]{1,0:T(8,128)S(1)} %get-tuple-element.17.refs_0_), channel_id=1, source_target_pairs={{0,64},{16,80},{32,96},{48,112},{64,128},{80,144},{96,160},{112,17... | collective-permute-start | bytes 24584 | tf_op jit(solution)/shard_map/ppermute | solution.py:291
  48.2 3.2 %copy-start.1 = (f32[128,16]{0,1:T(8,128)S(1)}, f32[128,16]{0,1:T(8,128)}, u32[]{:S(2)}) copy-start(f32[128,16]{0,1:T(8,128)} %param.7) | copy-start | bytes 24580
  55.2 23.5 %all-to-all-start.2 = ((bf16[16,128,128]{2,1,0:T(8,128)(2,1)}), bf16[16,128,128]{2,1,0:T(8,128)(2,1)}, u32[]{:S(2)}, u32[]{:S(2)}) async-start(bf16[16,128,128]{2,1,0:T(8,128)(2,1)} %get-tuple-element.21), calls=%async_computation.2 | async-start | bytes 1048576 | tf_op jit(solution)/shard_map/all_to_all | solution.py:284
  63.5 3.3 %collective-permute-start.8 = (f32[80,128]{1,0:T(8,128)S(1)}, f32[80,128]{1,0:T(8,128)S(1)}, u32[]{:S(2)}, u32[]{:S(2)}) collective-permute-start(f32[80,128]{1,0:T(8,128)S(1)} %sums_rest.1.refs_0_), channel_id=1, source_target_pairs={{0,48},{16,0},{32,16},{48,32},{64,112},{80,64},{96,80},{112,96},{1... | collective-permute-start | bytes 122888 | tf_op jit(solution)/shard_map/ppermute | solution.py:291
  64.6 4.9 %collective-permute-start.7 = (f32[80,128]{1,0:T(8,128)S(1)}, f32[80,128]{1,0:T(8,128)S(1)}, u32[]{:S(2)}, u32[]{:S(2)}) collective-permute-start(f32[80,128]{1,0:T(8,128)S(1)} %sums_rest.1.refs_0_), channel_id=1, source_target_pairs={{0,32},{16,48},{32,0},{48,16},{64,96},{80,112},{96,64},{112,80},{1... | collective-permute-start | bytes 122888 | tf_op jit(solution)/shard_map/ppermute | solution.py:291
  65.2 5.0 %collective-permute-start.6 = (f32[80,128]{1,0:T(8,128)S(1)}, f32[80,128]{1,0:T(8,128)S(1)}, u32[]{:S(2)}, u32[]{:S(2)}) collective-permute-start(f32[80,128]{1,0:T(8,128)S(1)} %sums_rest.1.refs_0_), channel_id=1, source_target_pairs={{0,16},{16,32},{32,48},{48,0},{64,80},{80,96},{96,112},{112,64},{1... | collective-permute-start | bytes 122888 | tf_op jit(solution)/shard_map/ppermute | solution.py:291
  70.3 4.2 %collective-permute-start.11 = (f32[80,128]{1,0:T(8,128)S(1)}, f32[80,128]{1,0:T(8,128)S(1)}, u32[]{:S(2)}, u32[]{:S(2)}) collective-permute-start(f32[80,128]{1,0:T(8,128)S(1)} %join.1.refs_0_), channel_id=1, source_target_pairs={{0,192},{16,208},{32,224},{48,240},{64,0},{80,16},{96,32},{112,48}... | collective-permute-start | bytes 122888 | tf_op jit(solution)/shard_map/ppermute | solution.py:291
  73.3 4.5 %collective-permute-start.10 = (f32[80,128]{1,0:T(8,128)S(1)}, f32[80,128]{1,0:T(8,128)S(1)}, u32[]{:S(2)}, u32[]{:S(2)}) collective-permute-start(f32[80,128]{1,0:T(8,128)S(1)} %join.1.refs_0_), channel_id=1, source_target_pairs={{0,128},{16,144},{32,160},{48,176},{64,192},{80,208},{96,224},{112... | collective-permute-start | bytes 122888 | tf_op jit(solution)/shard_map/ppermute | solution.py:291
  73.6 4.5 %collective-permute-start.9 = (f32[80,128]{1,0:T(8,128)S(1)}, f32[80,128]{1,0:T(8,128)S(1)}, u32[]{:S(2)}, u32[]{:S(2)}) collective-permute-start(f32[80,128]{1,0:T(8,128)S(1)} %join.1.refs_0_), channel_id=1, source_target_pairs={{0,64},{16,80},{32,96},{48,112},{64,128},{80,144},{96,160},{112,17... | collective-permute-start | bytes 122888 | tf_op jit(solution)/shard_map/ppermute | solution.py:291

commit v3 on v2

--- a/solution.py
+++ b/solution.py
@@ -48,7 +48,7 @@
     return ref[pl.ds(n, modes, stride=blocks), :]
 
 
-def ends_kernel(blocks, moved_ref, lam_ref, gt_ref, h_ref, head_ref):
+def ends_kernel(blocks, spans, moved_ref, lam_ref, gt_ref, h_ref, head_ref):
     modes = lam_ref.shape[0]
     block_len = moved_ref.shape[2]
     flip_blocks(moved_ref, gt_ref)
@@ -66,7 +66,9 @@
             at = p * blocks + half * ROWS
             h_ref[at : at + ROWS, :] = ends[p]
     step = jnp.exp(block_len * log_rates(lam_ref[...]))
-    head_ref[...] = folded(step, [block_rows(h_ref, n, blocks, modes) for n in range(blocks)])
+    head = folded(step, [block_rows(h_ref, n, blocks, modes) for n in range(blocks)])
+    for span in range(spans):
+        head_ref[span] = head
 
 
 def folded(step, heads):
@@ -98,16 +100,6 @@
                 t_ref[at : at + ROWS, :] = weighted[k]
 
 
-def near_kernel(span_len, *refs):
-    *parts, lam_ref, _, all_ref, near_ref, group_ref = refs
-    count = len(parts)
-    place = lax.rem(lax.axis_index("len"), count)
-    heads = ordered(parts, place, all_ref)
-    step = jnp.exp(span_len * log_rates(lam_ref[...]))
-    group_ref[...] = folded(step, heads)
-    near_ref[...] = folded_after(step, heads, place)
-
-
 def folded_after(step, heads, place):
     total = jnp.zeros(step.shape, F32)
     for i in range(len(heads) - 1, 0, -1):
@@ -115,20 +107,15 @@
     return total
 
 
-def input_grad_kernel(blocks, inner, outer, *refs):
-    *parts, near_ref, gt_ref, lam_ref, res_ref, h_ref, _, out_ref, all_ref, next_ref, flat_ref = refs
+def input_grad_kernel(
+    blocks, spans, heads_ref, gt_ref, lam_ref, res_ref, h_ref, _, out_ref, next_ref, flat_ref
+):
     modes, chans = lam_ref.shape
     block_len = gt_ref.shape[0] // blocks
-    span_len = blocks * block_len
     rate = log_rates(lam_ref[...])
     block_step = jnp.exp(block_len * rate)
-    place = lax.axis_index("len")
-    at_inner = lax.rem(place, inner)
-    at_outer = lax.div(place, inner)
-    heads = ordered(parts, at_outer, all_ref)
-    far = folded_after(jnp.exp((inner * span_len) * rate), heads, at_outer)
-    reach = (span_len * (inner - 1 - at_inner)).astype(F32)
-    total = near_ref[...] + jnp.exp(reach * rate) * far
+    span_step = jnp.exp((blocks * block_len) * rate)
+    total = folded_after(span_step, [heads_ref[i] for i in range(spans)], lax.axis_index("len"))
     for n in range(blocks - 1, -1, -1):
         next_ref[pl.ds(n, modes, stride=blocks), :] = total
         total = block_step * total + block_rows(h_ref, n, blocks, modes)
@@ -199,17 +186,19 @@
     return state, slope, res_sum, pole_sum, weighted
 
 
-def sums_first_kernel(blocks, moved_ref, gt_ref, lam_ref, h_ref, t_ref, xt_ref, pay_ref, *parts):
+def sums_kernel(blocks, shifts, *refs):
+    pieces, refs = refs[: len(shifts) + 1], refs[len(shifts) + 1 :]
+    gt_ref, lam_ref, h_ref, t_ref, pay_ref, moved_ref, xt_ref, *parts = refs
+    modes = lam_ref.shape[0]
+    chips = blocks // 2
+    place = lax.axis_index("chan")
+    chip, core = lax.div(place, 2), lax.rem(place, 2)
+    for s, ref in zip((0, *shifts), pieces):
+        source = 2 * lax.rem(chip + chips - s, chips)
+        moved_ref[source + core] = ref[0]
+        moved_ref[source + 1 - core] = ref[1]
     flip_blocks(moved_ref, xt_ref)
-    for k, item in enumerate(mode_sums(0, blocks, xt_ref, gt_ref, lam_ref, h_ref, t_ref, parts)):
-        pay_ref[k * GROUP : (k + 1) * GROUP, :] = item
-
-
-def sums_rest_kernel(blocks, xt_ref, gt_ref, lam_ref, h_ref, t_ref, first_ref, _, pay_ref, *parts):
-    modes = lam_ref.shape[0]
-    for k in range(5):
-        pay_ref[k * modes : k * modes + GROUP, :] = first_ref[k * GROUP : (k + 1) * GROUP, :]
-    for first in range(GROUP, modes, GROUP):
+    for first in range(0, modes, GROUP):
         items = mode_sums(first, blocks, xt_ref, gt_ref, lam_ref, h_ref, t_ref, parts)
         for k, item in enumerate(items):
             pay_ref[k * modes + first : k * modes + first + GROUP, :] = item
@@ -247,26 +236,30 @@
     *parts, heads_ref, lam_ref, pay_ref, slots_ref = refs
     modes = lam_ref.shape[0]
     count = len(parts)
-    parts = ordered(parts, lax.rem(lax.axis_index("len"), count), slots_ref)
-    heads = [heads_ref[i] for i in range(count)]
+    place = lax.axis_index("len")
+    parts = ordered(parts, lax.rem(place, count), slots_ref)
+    heads = [heads_ref[place - lax.rem(place, count) + i] for i in range(count)]
     for k, item in enumerate(joined(lam_ref[...], span_len, parts, heads)):
         pay_ref[k * modes : (k + 1) * modes, :] = item
 
 
-def finish_kernel(inner, group_len, *refs):
+def finish_kernel(inner, span_len, *refs):
     *parts, heads_ref, lam_ref, res_ref, res_out, pole_out, slots_ref = refs
     count = len(parts)
     lam = lam_ref[...]
+    step = jnp.exp(span_len * log_rates(lam))
     parts = ordered(parts, lax.div(lax.axis_index("len"), inner), slots_ref)
-    heads = [heads_ref[i] for i in range(count)]
-    _, _, res_sum, pole_sum, _ = joined(lam, group_len, parts, heads)
+    heads = [
+        folded(step, [heads_ref[g * inner + i] for i in range(inner)]) for g in range(count)
+    ]
+    _, _, res_sum, pole_sum, _ = joined(lam, inner * span_len, parts, heads)
     width = (1.0 - lam) * (1.0 + lam)
-    scale = 1.0 / math.sqrt(count * group_len)
+    scale = 1.0 / math.sqrt(count * inner * span_len)
     res_out[...] = res_sum * jnp.sqrt(width) * scale
     pole_out[...] = res_ref[...] * pole_sum * width * scale
 
 
-def call(kernel, out_shape, in_count, scratch, name, flops):
+def call(kernel, out_shape, in_count, scratch, name, flops, mebibytes=32):
     single = not isinstance(out_shape, (tuple, list))
     return pl.pallas_call(
         kernel,
@@ -274,7 +267,7 @@
         in_specs=[VMEM] * in_count,
         out_specs=VMEM if single else [VMEM] * len(out_shape),
         scratch_shapes=scratch,
-        compiler_params=pltpu.CompilerParams(vmem_limit_bytes=32 * 1024 * 1024),
+        compiler_params=pltpu.CompilerParams(vmem_limit_bytes=mebibytes * 2**20),
         cost_estimate=pl.CostEstimate(flops=flops, bytes_accessed=2**20, transcendentals=0),
         name=name,
     )
@@ -290,6 +283,20 @@
     return [
         lax.ppermute(part, "len", [(i, hop(i, s)) for i in range(spans)]) for s in range(1, count)
     ]
+
+
+def moved_pieces(part, blocks, shifts):
+    chips = blocks // 2
+    place = lax.axis_index("chan")
+    chip, core = place // 2, place % 2
+    got = lax.ppermute(part, "chan", [(i, i ^ 1) for i in range(blocks)])
+    halves = [half.reshape(chips, 2, *half.shape[1:]) for half in (part, got)]
+    block = lambda half, s: lax.dynamic_slice(
+        half, ((chip + s) % chips, core, 0, 0), (1, 1, *half.shape[2:])
+    )[0]
+    at = lambda s: jnp.concatenate([block(half, s) for half in halves])
+    ring = lambda s: [(i, (i + 2 * s) % blocks) for i in range(blocks)]
+    return [at(0)] + [lax.ppermute(at(s), "chan", ring(s)) for s in shifts]
 
 
 def body(inputs, grad_output, pole_values, residue_values):
@@ -309,15 +316,17 @@
     poles = pole_values.T
     residues = residue_values.T
     moved_grads = swap(cut(grad_output), "chan")
-    moved_inputs = swap(cut(inputs), "chan")
+    shifts = sorted(range(1, blocks // 2), key=lambda s: -min(s, blocks // 2 - s))
+    pieces = moved_pieces(cut(inputs), blocks, shifts)
     flat_grads, ends, head = call(
-        functools.partial(ends_kernel, blocks),
-        (shape(flat, chans), shape(held, chans), table),
+        functools.partial(ends_kernel, blocks, spans),
+        (shape(flat, chans), shape(held, chans), shape(spans, modes, chans)),
         2,
         [],
         "block_ends",
         2 * work,
     )(moved_grads, poles)
+    heads = swap(head, "len")
     weighted = call(
         functools.partial(weighted_kernel, blocks),
         shape(held, chans),
@@ -326,48 +335,24 @@
         "weighted",
         4 * work,
     )(flat_grads, poles)
-    heads, near, group_head = call(
-        functools.partial(near_kernel, flat),
-        (shape(inner, modes, chans), table, table),
-        inner + 2,
-        [],
-        "near",
-        work // 100,
-    )(head, *rotated(head, inner, 1, spans), poles, weighted)
-    flat_inputs, first_pay = call(
-        functools.partial(sums_first_kernel, blocks),
-        (shape(flat, chans), shape(5 * GROUP, chans)),
-        5,
-        [scratch(GROUP * blocks, chans)] * 4,
-        "sums_first",
-        4 * work,
-    )(moved_inputs, flat_grads, poles, ends, weighted)
-    rounded, group_heads = call(
-        functools.partial(input_grad_kernel, blocks, inner, outer),
-        (jax.ShapeDtypeStruct((blocks, chans, block_len), jnp.bfloat16), shape(outer, modes, chans)),
-        outer + 6,
+    pay = call(
+        functools.partial(sums_kernel, blocks, shifts),
+        shape(5 * modes, chans),
+        len(pieces) + 4,
+        [pltpu.VMEM((blocks, chans, block_len), jnp.bfloat16), scratch(flat, chans)]
+        + [scratch(GROUP * blocks, chans)] * 4,
+        "mode_sums",
+        8 * work,
+    )(*pieces, flat_grads, poles, ends, weighted)
+    rounded = call(
+        functools.partial(input_grad_kernel, blocks, spans),
+        jax.ShapeDtypeStruct((blocks, chans, block_len), jnp.bfloat16),
+        6,
         [scratch(held, chans), scratch(flat, chans)],
         "input_grad",
         4 * work,
-    )(
-        group_head,
-        *rotated(group_head, outer, inner, spans),
-        near,
-        flat_grads,
-        poles,
-        residues,
-        ends,
-        first_pay,
-    )
+    )(heads, flat_grads, poles, residues, ends, pay)
     input_grad = swap(rounded, "chan").reshape(blocks * chans, block_len)
-    pay = call(
-        functools.partial(sums_rest_kernel, blocks),
-        shape(5 * modes, chans),
-        7,
-        [scratch(GROUP * blocks, chans)] * 4,
-        "sums_rest",
-        4 * work,
-    )(flat_inputs, flat_grads, poles, ends, weighted, first_pay, group_heads)
     group_pay = call(
         functools.partial(join_kernel, flat),
         shape(5 * modes, chans),
@@ -377,13 +362,13 @@
         work // 100,
     )(pay, *rotated(pay, inner, 1, spans), heads, poles)
     residue_grad, pole_grad = call(
-        functools.partial(finish_kernel, inner, inner * flat),
+        functools.partial(finish_kernel, inner, flat),
         (table, table),
         outer + 3,
         [scratch(outer, 5 * modes, chans)],
         "finish",
         work // 100,
-    )(group_pay, *rotated(group_pay, outer, inner, spans), group_heads, poles, residues)
+    )(group_pay, *rotated(group_pay, outer, inner, spans), heads, poles, residues)
     return (input_grad, residue_grad.T, pole_grad.T)
 
 

time: 81.2 us -> 77.4 us (0.953)
  starting transfers between devices: 23.1 us -> 50.8 us
  blocking collectives: 27.3 us -> 0 us
  waiting for transfers between devices: 13.3 us -> 9.33 us
  local copies, waits for them, and re-layouts: 1.88 us -> 0.89 us
    all_to_all x1 -> x0, blocking collectives: 27.3 us -> none  [swap(): return lax.all_to_all(part, axis, split_axis=0, concat_axis=0, tiled=True)]
    ppermute x0 -> x8, starting transfers between devices: none -> 19.8 us  [the longest x7 16.5 us: moved_pieces(): return [at(0)] + [lax.ppermute(at(s), 'chan', ring(s)) for s in shifts]]
    all_to_all x2 -> x3, starting transfers between devices: 9.27 us -> 21.3 us  [swap(): return lax.all_to_all(part, axis, split_axis=0, concat_axis=0, tiled=True)]
    ppermute x12 -> x6, waiting for transfers between devices: 9.37 us -> 3.94 us  [rotated(): lax.ppermute(part, 'len', [(i, hop(i, s)) for i in range(spans)])]
    ppermute x12 -> x6, starting transfers between devices: 13.8 us -> 9.77 us  [rotated(): lax.ppermute(part, 'len', [(i, hop(i, s)) for i in range(spans)])]
    all_to_all x2 -> x3, waiting for transfers between devices: 3.88 us -> 5.37 us  [swap(): return lax.all_to_all(part, axis, split_axis=0, concat_axis=0, tiled=True)]
    unnamed x5 -> x7, local copies, waits for them, and re-layouts: 1.88 us -> 0.81 us
    pallas_call x6 -> x4, Pallas kernels: 12 us -> 12.8 us  [the longest x1 5.83 us: body(): call(functools.partial(sums_kernel, blocks, shifts), shape(5 * modes, cha...]
  transfers between devices with their start and end apart: 14 -> 17, of which waited for: 9 -> 6; matrix products, arithmetic and copies ran while one was open for 0% -> 0% of each run, Pallas kernels for 13% -> 15%
where the time goes in v3:
time: 77.4 us; the launch traced here: 77 us
  starting transfers between devices  50.8 us (66%)
  Pallas kernels  15.1 us (20%)
  waiting for transfers between devices  9.33 us (12%)
  local copies, waits for them, and re-layouts  0.89 us (1%)
  between operations  0.8 us (1%)
    all_to_all x3, starting transfers between devices, swap(): return lax.all_to_all(part, axis, split_axis=0, concat_axis=0, tiled=True)  21.3 us
    ppermute x7, starting transfers between devices, moved_pieces(): return [at(0)] + [lax.ppermute(at(s), 'chan', ring(s)) for s in shifts]  16.5 us
    ppermute x6, starting transfers between devices, rotated(): lax.ppermute(part, 'len', [(i, hop(i, s)) for i in range(spans)])  9.77 us
    pallas_call x1, Pallas kernels, body(): call(functools.partial(sums_kernel, blocks, shifts), shape(5 * modes, cha...  5.83 us
    all_to_all x3, waiting for transfers between devices, swap(): return lax.all_to_all(part, axis, split_axis=0, concat_axis=0, tiled=True)  5.37 us
    ppermute x6, waiting for transfers between devices, rotated(): lax.ppermute(part, 'len', [(i, hop(i, s)) for i in range(spans)])  3.94 us
    pallas_call x1, Pallas kernels, body(): call(functools.partial(input_grad_kernel, blocks, spans), jax.ShapeDtypeS...  3.8 us
    ppermute x1, starting transfers between devices, moved_pieces(): got = lax.ppermute(part, 'chan', [(i, i ^ 1) for i in range(blocks)])  3.33 us
  transfers between devices with their start and end apart: 17, of which 6 were waited for; matrix products, arithmetic and copies ran while one was open for 0% of the time, Pallas kernels for 15%

profile of v3, /device:TPU:1, one launch (start us, length us, event | category | flops | bytes accessed | tf_op | source)
XLA Modules:
  0.0 77.0 jit_solution(9600156591080297269)
XLA Ops:
  0.6 3.3 %collective-permute-start = (bf16[16,128,128]{2,1,0:T(8,128)(2,1)}, bf16[16,128,128]{2,1,0:T(8,128)(2,1)S(1)}, u32[]{:S(2)}, u32[]{:S(2)}) collective-permute-start(bf16[16,128,128]{2,1,0:T(8,128)(2,1)} %bitcast.51), channel_id=1, source_target_pairs={{0,1},{1,0},{2,3},{3,2},{4,5},{5,4},{6,7},{7,6},{8,9},{9,8},{10,11... | collective-permute-start | bytes 1572872 | tf_op jit(solution)/shard_map/ppermute | solution.py:292
  4.0 0.0 copy-start.2
  4.0 7.0 %all-to-all-start = ((bf16[16,128,128]{2,1,0:T(8,128)(2,1)}), bf16[16,128,128]{2,1,0:T(8,128)(2,1)S(1)}, u32[]{:S(2)}, u32[]{:S(2)}) async-start(bf16[16,128,128]{2,1,0:T(8,128)(2,1)} %bitcast.50), calls=%async_computation | async-start | bytes 1048576 | tf_op jit(solution)/shard_map/all_to_all | solution.py:277
  10.9 0.0 copy-done.2
  11.0 0.0 collective-permute-done
  11.1 5.4 %collective-permute-start.1 = (bf16[2,128,128]{2,1,0:T(8,128)(2,1)S(1)}, bf16[2,128,128]{2,1,0:T(8,128)(2,1)S(1)}, u32[]{:S(2)}, u32[]{:S(2)}) collective-permute-start(bf16[2,128,128]{2,1,0:T(8,128)(2,1)S(1)} %pad_maximum_fusion.1), channel_id=1, source_target_pairs={{0,8},{1,9},{2,10},{3,11},{4,12},{5,13},{6,14},{7,15},{8,0},{9,1},... | collective-permute-start | bytes 196616 | tf_op jit(solution)/shard_map/ppermute | solution.py:299
  16.5 0.4 collective-permute-start.2
  16.8 4.3 %collective-permute-start.3 = (bf16[2,128,128]{2,1,0:T(8,128)(2,1)S(1)}, bf16[2,128,128]{2,1,0:T(8,128)(2,1)S(1)}, u32[]{:S(2)}, u32[]{:S(2)}) collective-permute-start(bf16[2,128,128]{2,1,0:T(8,128)(2,1)S(1)} %pad_maximum_fusion.3), channel_id=1, source_target_pairs={{0,10},{1,11},{2,12},{3,13},{4,14},{5,15},{6,0},{7,1},{8,2},{9,3},... | collective-permute-start | bytes 196616 | tf_op jit(solution)/shard_map/ppermute | solution.py:299
  21.1 0.4 collective-permute-start.4
  21.5 3.4 %collective-permute-start.5 = (bf16[2,128,128]{2,1,0:T(8,128)(2,1)S(1)}, bf16[2,128,128]{2,1,0:T(8,128)(2,1)S(1)}, u32[]{:S(2)}, u32[]{:S(2)}) collective-permute-start(bf16[2,128,128]{2,1,0:T(8,128)(2,1)S(1)} %pad_maximum_fusion.5), channel_id=1, source_target_pairs={{0,12},{1,13},{2,14},{3,15},{4,0},{5,1},{6,2},{7,3},{8,4},{9,5},{1... | collective-permute-start | bytes 196616 | tf_op jit(solution)/shard_map/ppermute | solution.py:299
  24.8 0.0 copy-start
  24.8 2.5 %all-to-all-done.moved_ref = bf16[16,128,128]{2,1,0:T(8,128)(2,1)S(1)} async-done(((bf16[16,128,128]{2,1,0:T(8,128)(2,1)}), bf16[16,128,128]{2,1,0:T(8,128)(2,1)S(1)}, u32[]{:S(2)}, u32[]{:S(2)}) %all-to-all-start) | async-done | bytes 524320 | tf_op jit(solution)/shard_map/all_to_all | solution.py:277
  27.3 0.0 copy-done
  27.3 2.5 %block_ends.1 = (f32[2048,128]{1,0:T(8,128)S(1)}, f32[256,128]{1,0:T(8,128)S(1)}, f32[16,16,128]{2,1,0:T(8,128)}) custom-call(bf16[16,128,128]{2,1,0:T(8,128)(2,1)S(1)} %all-to-all-done.moved_ref, f32[16,128]{1,0:T(8,128)S(1)} %bitcast.41), custom_call_target="tpu_custom_call" | custom-call | flops 8388608 | bytes 1048576 | tf_op jit(solution)/shard_map/block_ends/pallas_call | solution.py:321
  29.8 6.8 %all-to-all-start.1 = ((f32[16,16,128]{2,1,0:T(8,128)}), f32[16,16,128]{2,1,0:T(8,128)S(1)}, u32[]{:S(2)}, u32[]{:S(2)}) async-start(f32[16,16,128]{2,1,0:T(8,128)} %get-tuple-element.8), calls=%async_computation.1 | async-start | bytes 262144 | tf_op jit(solution)/shard_map/all_to_all | solution.py:277
  36.6 0.0 collective-permute-done.1.refs_1_
  36.6 0.1 collective-permute-start.6
  36.7 0.0 collective-permute-done.2.refs_2_
  36.7 2.7 %collective-permute-start.7 = (bf16[2,128,128]{2,1,0:T(8,128)(2,1)S(1)}, bf16[2,128,128]{2,1,0:T(8,128)(2,1)S(1)}, u32[]{:S(2)}, u32[]{:S(2)}) collective-permute-start(bf16[2,128,128]{2,1,0:T(8,128)(2,1)S(1)} %pad_maximum_fusion.7), channel_id=1, source_target_pairs={{0,14},{1,15},{2,0},{3,1},{4,2},{5,3},{6,4},{7,5},{8,6},{9,7},{10,... | collective-permute-start | bytes 196616 | tf_op jit(solution)/shard_map/ppermute | solution.py:299
  39.4 2.3 %weighted.1.refs_11_ = f32[256,128]{1,0:T(8,128)S(1)} custom-call(f32[2048,128]{1,0:T(8,128)S(1)} %get-tuple-element.9.gt_ref.refs_8_, f32[16,128]{1,0:T(8,128)S(1)} %bitcast.42), custom_call_target="tpu_custom_call" | custom-call | flops 16777216 | bytes 1048576 | tf_op jit(solution)/shard_map/weighted/pallas_call | solution.py:330
  41.6 0.0 collective-permute-done.3.refs_3_
  41.7 0.0 collective-permute-done.4.refs_4_
  41.7 0.0 collective-permute-done.5.refs_5_
  41.7 0.0 collective-permute-done.6.refs_6_
  41.7 0.0 collective-permute-done.7.refs_7_
  41.7 0.0 copy-start.1
  41.7 5.8 %mode_sums.1._.refs_0_ = f32[80,128]{1,0:T(8,128)S(1)} custom-call(bf16[2,128,128]{2,1,0:T(8,128)(2,1)S(1)} %pad_maximum_fusion.refs_0_, bf16[2,128,128]{2,1,0:T(8,128)(2,1)S(1)} %collective-permute-done.1.refs_1_, bf16[2,128,128]{2,1,0:T(8,128)(2,1)S(1)} %collective-permute-done.2.refs_2_, bf16[2,128,128]{2,1,0:T(8,128)(2,1)S(1)} %collective-permute-done.3.refs_3_, ...), custom_call_target="tpu_custom_call" | custom-call | flops 33554432 | bytes 1048576 | tf_op jit(solution)/shard_map/mode_sums/pallas_call | solution.py:338
  47.5 0.0 all-to-all-done.1.heads_ref.refs_4_
  47.5 0.0 copy-done.1
  47.6 3.8 %input_grad.1 = bf16[16,128,128]{2,1,0:T(8,128)(2,1)} custom-call(f32[16,16,128]{2,1,0:T(8,128)S(1)} %all-to-all-done.1.heads_ref.refs_4_, f32[2048,128]{1,0:T(8,128)S(1)} %get-tuple-element.9.gt_ref.refs_8_, f32[16,128]{1,0:T(8,128)S(1)} %bitcast.44, f32[16,128]{1,0:T(8,128)S(1)} %bitcast.47, f32[256,128]{1,0:T(8,128)S(1)} %get-tuple-element.10.refs_10_.h_ref, ...), custom_call_target="tpu_custom_call" | custom-call | flops 16777216 | bytes 1048576 | tf_op jit(solution)/shard_map/input_grad/pallas_call | solution.py:347
  51.4 7.5 %all-to-all-start.2 = ((bf16[16,128,128]{2,1,0:T(8,128)(2,1)}), bf16[16,128,128]{2,1,0:T(8,128)(2,1)S(1)}, u32[]{:S(2)}, u32[]{:S(2)}) async-start(bf16[16,128,128]{2,1,0:T(8,128)(2,1)} %input_grad.1), calls=%async_computation.2 | async-start | bytes 1048576 | tf_op jit(solution)/shard_map/all_to_all | solution.py:277
  58.9 1.4 %collective-permute-start.8 = (f32[80,128]{1,0:T(8,128)S(1)}, f32[80,128]{1,0:T(8,128)S(1)}, u32[]{:S(2)}, u32[]{:S(2)}) collective-permute-start(f32[80,128]{1,0:T(8,128)S(1)} %mode_sums.1._.refs_0_), channel_id=1, source_target_pairs={{0,16},{16,32},{32,48},{48,0},{64,80},{80,96},{96,112},{112,64},{1... | collective-permute-start | bytes 122888 | tf_op jit(solution)/shard_map/ppermute | solution.py:284
  60.2 2.4 %collective-permute-start.9 = (f32[80,128]{1,0:T(8,128)S(1)}, f32[80,128]{1,0:T(8,128)S(1)}, u32[]{:S(2)}, u32[]{:S(2)}) collective-permute-start(f32[80,128]{1,0:T(8,128)S(1)} %mode_sums.1._.refs_0_), channel_id=1, source_target_pairs={{0,32},{16,48},{32,0},{48,16},{64,96},{80,112},{96,64},{112,80},{1... | collective-permute-start | bytes 122888 | tf_op jit(solution)/shard_map/ppermute | solution.py:284
  62.6 1.2 %collective-permute-start.10 = (f32[80,128]{1,0:T(8,128)S(1)}, f32[80,128]{1,0:T(8,128)S(1)}, u32[]{:S(2)}, u32[]{:S(2)}) collective-permute-start(f32[80,128]{1,0:T(8,128)S(1)} %mode_sums.1._.refs_0_), channel_id=1, source_target_pairs={{0,48},{16,0},{32,16},{48,32},{64,112},{80,64},{96,80},{112,96},{1... | collective-permute-start | bytes 122888 | tf_op jit(solution)/shard_map/ppermute | solution.py:284
  63.8 0.0 collective-permute-done.8.refs_1_
  63.8 1.4 %collective-permute-done.9.refs_2_ = f32[80,128]{1,0:T(8,128)S(1)} collective-permute-done((f32[80,128]{1,0:T(8,128)S(1)}, f32[80,128]{1,0:T(8,128)S(1)}, u32[]{:S(2)}, u32[]{:S(2)}) %collective-permute-start.9) | collective-permute-done | bytes 40992 | tf_op jit(solution)/shard_map/ppermute | solution.py:284
  65.3 0.5 collective-permute-done.10.refs_3_
  65.8 0.1 join.1.refs_0_
  65.8 1.3 %collective-permute-start.11 = (f32[80,128]{1,0:T(8,128)S(1)}, f32[80,128]{1,0:T(8,128)S(1)}, u32[]{:S(2)}, u32[]{:S(2)}) collective-permute-start(f32[80,128]{1,0:T(8,128)S(1)} %join.1.refs_0_), channel_id=1, source_target_pairs={{0,64},{16,80},{32,96},{48,112},{64,128},{80,144},{96,160},{112,17... | collective-permute-start | bytes 122888 | tf_op jit(solution)/shard_map/ppermute | solution.py:284
  67.1 2.4 %collective-permute-start.12 = (f32[80,128]{1,0:T(8,128)S(1)}, f32[80,128]{1,0:T(8,128)S(1)}, u32[]{:S(2)}, u32[]{:S(2)}) collective-permute-start(f32[80,128]{1,0:T(8,128)S(1)} %join.1.refs_0_), channel_id=1, source_target_pairs={{0,128},{16,144},{32,160},{48,176},{64,192},{80,208},{96,224},{112... | collective-permute-start | bytes 122888 | tf_op jit(solution)/shard_map/ppermute | solution.py:284
  69.5 1.2 %collective-permute-start.13 = (f32[80,128]{1,0:T(8,128)S(1)}, f32[80,128]{1,0:T(8,128)S(1)}, u32[]{:S(2)}, u32[]{:S(2)}) collective-permute-start(f32[80,128]{1,0:T(8,128)S(1)} %join.1.refs_0_), channel_id=1, source_target_pairs={{0,192},{16,208},{32,224},{48,240},{64,0},{80,16},{96,32},{112,48}... | collective-permute-start | bytes 122888 | tf_op jit(solution)/shard_map/ppermute | solution.py:284
  70.7 0.0 collective-permute-done.11.refs_1_
  70.7 0.8 %collective-permute-done.12.refs_2_ = f32[80,128]{1,0:T(8,128)S(1)} collective-permute-done((f32[80,128]{1,0:T(8,128)S(1)}, f32[80,128]{1,0:T(8,128)S(1)}, u32[]{:S(2)}, u32[]{:S(2)}) %collective-permute-start.12) | collective-permute-done | bytes 40992 | tf_op jit(solution)/shard_map/ppermute | solution.py:284
  71.5 1.1 %collective-permute-done.13.refs_3_ = f32[80,128]{1,0:T(8,128)S(1)} collective-permute-done((f32[80,128]{1,0:T(8,128)S(1)}, f32[80,128]{1,0:T(8,128)S(1)}, u32[]{:S(2)}, u32[]{:S(2)}) %collective-permute-start.13) | collective-permute-done | bytes 40992 | tf_op jit(solution)/shard_map/ppermute | solution.py:284
  72.7 0.7 finish.1
  73.3 2.9 %all-to-all-done.2 = bf16[16,128,128]{2,1,0:T(8,128)(2,1)S(1)} async-done(((bf16[16,128,128]{2,1,0:T(8,128)(2,1)}), bf16[16,128,128]{2,1,0:T(8,128)(2,1)S(1)}, u32[]{:S(2)}, u32[]{:S(2)}) %all-to-all-start.2) | async-done | bytes 524320 | tf_op jit(solution)/shard_map/all_to_all | solution.py:277
  76.2 0.8 %copy.8 = bf16[2048,128]{1,0:T(8,128)(2,1)} copy(bf16[2048,128]{1,0:T(8,128)(2,1)S(1)} %bitcast.49) | data formatting | bytes 1048576
  (10 shorter events, 0.1 us)
Async XLA Ops:
  0.6 10.4 %collective-permute-start = (bf16[16,128,128]{2,1,0:T(8,128)(2,1)}, bf16[16,128,128]{2,1,0:T(8,128)(2,1)S(1)}, u32[]{:S(2)}, u32[]{:S(2)}) collective-permute-start(bf16[16,128,128]{2,1,0:T(8,128)(2,1)} %bitcast.51), channel_id=1, source_target_pairs={{0,1},{1,0},{2,3},{3,2},{4,5},{5,4},{6,7},{7,6},{8,9},{9,8},{10,11... | collective-permute-start | bytes 1572872 | tf_op jit(solution)/shard_map/ppermute | solution.py:292
  4.0 7.0 %copy-start.2 = (bf16[2048,128]{1,0:T(8,128)(2,1)S(1)}, bf16[2048,128]{1,0:T(8,128)(2,1)}, u32[]{:S(2)}) copy-start(bf16[2048,128]{1,0:T(8,128)(2,1)} %param.4) | copy-start | bytes 1572868
  4.0 23.4 %all-to-all-start = ((bf16[16,128,128]{2,1,0:T(8,128)(2,1)}), bf16[16,128,128]{2,1,0:T(8,128)(2,1)S(1)}, u32[]{:S(2)}, u32[]{:S(2)}) async-start(bf16[16,128,128]{2,1,0:T(8,128)(2,1)} %bitcast.50), calls=%async_computation | async-start | bytes 1048576 | tf_op jit(solution)/shard_map/all_to_all | solution.py:277
  11.1 25.5 %collective-permute-start.1 = (bf16[2,128,128]{2,1,0:T(8,128)(2,1)S(1)}, bf16[2,128,128]{2,1,0:T(8,128)(2,1)S(1)}, u32[]{:S(2)}, u32[]{:S(2)}) collective-permute-start(bf16[2,128,128]{2,1,0:T(8,128)(2,1)S(1)} %pad_maximum_fusion.1), channel_id=1, source_target_pairs={{0,8},{1,9},{2,10},{3,11},{4,12},{5,13},{6,14},{7,15},{8,0},{9,1},... | collective-permute-start | bytes 196616 | tf_op jit(solution)/shard_map/ppermute | solution.py:299
  16.5 20.2 %collective-permute-start.2 = (bf16[2,128,128]{2,1,0:T(8,128)(2,1)S(1)}, bf16[2,128,128]{2,1,0:T(8,128)(2,1)S(1)}, u32[]{:S(2)}, u32[]{:S(2)}) collective-permute-start(bf16[2,128,128]{2,1,0:T(8,128)(2,1)S(1)} %pad_maximum_fusion.2), channel_id=1, source_target_pairs={{0,6},{1,7},{2,8},{3,9},{4,10},{5,11},{6,12},{7,13},{8,14},{9,15},... | collective-permute-start | bytes 196616 | tf_op jit(solution)/shard_map/ppermute | solution.py:299
  16.8 24.8 %collective-permute-start.3 = (bf16[2,128,128]{2,1,0:T(8,128)(2,1)S(1)}, bf16[2,128,128]{2,1,0:T(8,128)(2,1)S(1)}, u32[]{:S(2)}, u32[]{:S(2)}) collective-permute-start(bf16[2,128,128]{2,1,0:T(8,128)(2,1)S(1)} %pad_maximum_fusion.3), channel_id=1, source_target_pairs={{0,10},{1,11},{2,12},{3,13},{4,14},{5,15},{6,0},{7,1},{8,2},{9,3},... | collective-permute-start | bytes 196616 | tf_op jit(solution)/shard_map/ppermute | solution.py:299
  21.1 20.6 %collective-permute-start.4 = (bf16[2,128,128]{2,1,0:T(8,128)(2,1)S(1)}, bf16[2,128,128]{2,1,0:T(8,128)(2,1)S(1)}, u32[]{:S(2)}, u32[]{:S(2)}) collective-permute-start(bf16[2,128,128]{2,1,0:T(8,128)(2,1)S(1)} %pad_maximum_fusion.4), channel_id=1, source_target_pairs={{0,4},{1,5},{2,6},{3,7},{4,8},{5,9},{6,10},{7,11},{8,12},{9,13},{1... | collective-permute-start | bytes 196616 | tf_op jit(solution)/shard_map/ppermute | solution.py:299
  21.5 20.2 %collective-permute-start.5 = (bf16[2,128,128]{2,1,0:T(8,128)(2,1)S(1)}, bf16[2,128,128]{2,1,0:T(8,128)(2,1)S(1)}, u32[]{:S(2)}, u32[]{:S(2)}) collective-permute-start(bf16[2,128,128]{2,1,0:T(8,128)(2,1)S(1)} %pad_maximum_fusion.5), channel_id=1, source_target_pairs={{0,12},{1,13},{2,14},{3,15},{4,0},{5,1},{6,2},{7,3},{8,4},{9,5},{1... | collective-permute-start | bytes 196616 | tf_op jit(solution)/shard_map/ppermute | solution.py:299
  24.8 2.5 %copy-start = (f32[128,16]{0,1:T(8,128)S(1)}, f32[128,16]{0,1:T(8,128)}, u32[]{:S(2)}) copy-start(f32[128,16]{0,1:T(8,128)} %param.6) | copy-start | bytes 24580
  29.8 17.7 %all-to-all-start.1 = ((f32[16,16,128]{2,1,0:T(8,128)}), f32[16,16,128]{2,1,0:T(8,128)S(1)}, u32[]{:S(2)}, u32[]{:S(2)}) async-start(f32[16,16,128]{2,1,0:T(8,128)} %get-tuple-element.8), calls=%async_computation.1 | async-start | bytes 262144 | tf_op jit(solution)/shard_map/all_to_all | solution.py:277
  36.6 5.1 %collective-permute-start.6 = (bf16[2,128,128]{2,1,0:T(8,128)(2,1)S(1)}, bf16[2,128,128]{2,1,0:T(8,128)(2,1)S(1)}, u32[]{:S(2)}, u32[]{:S(2)}) collective-permute-start(bf16[2,128,128]{2,1,0:T(8,128)(2,1)S(1)} %pad_maximum_fusion.6), channel_id=1, source_target_pairs={{0,2},{1,3},{2,4},{3,5},{4,6},{5,7},{6,8},{7,9},{8,10},{9,11},{10,... | collective-permute-start | bytes 196616 | tf_op jit(solution)/shard_map/ppermute | solution.py:299
  36.7 5.0 %collective-permute-start.7 = (bf16[2,128,128]{2,1,0:T(8,128)(2,1)S(1)}, bf16[2,128,128]{2,1,0:T(8,128)(2,1)S(1)}, u32[]{:S(2)}, u32[]{:S(2)}) collective-permute-start(bf16[2,128,128]{2,1,0:T(8,128)(2,1)S(1)} %pad_maximum_fusion.7), channel_id=1, source_target_pairs={{0,14},{1,15},{2,0},{3,1},{4,2},{5,3},{6,4},{7,5},{8,6},{9,7},{10,... | collective-permute-start | bytes 196616 | tf_op jit(solution)/shard_map/ppermute | solution.py:299
  41.7 5.9 %copy-start.1 = (f32[128,16]{0,1:T(8,128)S(1)}, f32[128,16]{0,1:T(8,128)}, u32[]{:S(2)}) copy-start(f32[128,16]{0,1:T(8,128)} %param.7) | copy-start | bytes 24580
  51.4 24.8 %all-to-all-start.2 = ((bf16[16,128,128]{2,1,0:T(8,128)(2,1)}), bf16[16,128,128]{2,1,0:T(8,128)(2,1)S(1)}, u32[]{:S(2)}, u32[]{:S(2)}) async-start(bf16[16,128,128]{2,1,0:T(8,128)(2,1)} %input_grad.1), calls=%async_computation.2 | async-start | bytes 1048576 | tf_op jit(solution)/shard_map/all_to_all | solution.py:277
  58.9 4.9 %collective-permute-start.8 = (f32[80,128]{1,0:T(8,128)S(1)}, f32[80,128]{1,0:T(8,128)S(1)}, u32[]{:S(2)}, u32[]{:S(2)}) collective-permute-start(f32[80,128]{1,0:T(8,128)S(1)} %mode_sums.1._.refs_0_), channel_id=1, source_target_pairs={{0,16},{16,32},{32,48},{48,0},{64,80},{80,96},{96,112},{112,64},{1... | collective-permute-start | bytes 122888 | tf_op jit(solution)/shard_map/ppermute | solution.py:284
  60.2 5.0 %collective-permute-start.9 = (f32[80,128]{1,0:T(8,128)S(1)}, f32[80,128]{1,0:T(8,128)S(1)}, u32[]{:S(2)}, u32[]{:S(2)}) collective-permute-start(f32[80,128]{1,0:T(8,128)S(1)} %mode_sums.1._.refs_0_), channel_id=1, source_target_pairs={{0,32},{16,48},{32,0},{48,16},{64,96},{80,112},{96,64},{112,80},{1... | collective-permute-start | bytes 122888 | tf_op jit(solution)/shard_map/ppermute | solution.py:284
  62.6 3.1 %collective-permute-start.10 = (f32[80,128]{1,0:T(8,128)S(1)}, f32[80,128]{1,0:T(8,128)S(1)}, u32[]{:S(2)}, u32[]{:S(2)}) collective-permute-start(f32[80,128]{1,0:T(8,128)S(1)} %mode_sums.1._.refs_0_), channel_id=1, source_target_pairs={{0,48},{16,0},{32,16},{48,32},{64,112},{80,64},{96,80},{112,96},{1... | collective-permute-start | bytes 122888 | tf_op jit(solution)/shard_map/ppermute | solution.py:284
  65.8 4.8 %collective-permute-start.11 = (f32[80,128]{1,0:T(8,128)S(1)}, f32[80,128]{1,0:T(8,128)S(1)}, u32[]{:S(2)}, u32[]{:S(2)}) collective-permute-start(f32[80,128]{1,0:T(8,128)S(1)} %join.1.refs_0_), channel_id=1, source_target_pairs={{0,64},{16,80},{32,96},{48,112},{64,128},{80,144},{96,160},{112,17... | collective-permute-start | bytes 122888 | tf_op jit(solution)/shard_map/ppermute | solution.py:284
  67.1 4.4 %collective-permute-start.12 = (f32[80,128]{1,0:T(8,128)S(1)}, f32[80,128]{1,0:T(8,128)S(1)}, u32[]{:S(2)}, u32[]{:S(2)}) collective-permute-start(f32[80,128]{1,0:T(8,128)S(1)} %join.1.refs_0_), channel_id=1, source_target_pairs={{0,128},{16,144},{32,160},{48,176},{64,192},{80,208},{96,224},{112... | collective-permute-start | bytes 122888 | tf_op jit(solution)/shard_map/ppermute | solution.py:284
  69.5 3.1 %collective-permute-start.13 = (f32[80,128]{1,0:T(8,128)S(1)}, f32[80,128]{1,0:T(8,128)S(1)}, u32[]{:S(2)}, u32[]{:S(2)}) collective-permute-start(f32[80,128]{1,0:T(8,128)S(1)} %join.1.refs_0_), channel_id=1, source_target_pairs={{0,192},{16,208},{32,224},{48,240},{64,0},{80,16},{96,32},{112,48}... | collective-permute-start | bytes 122888 | tf_op jit(solution)/shard_map/ppermute | solution.py:284

commit v4 on v3

--- a/solution.py
+++ b/solution.py
@@ -10,33 +10,19 @@
 
 ROWS = 8
 GROUP = 8
+STEP = 8
 F32 = jnp.float32
 VMEM = pl.BlockSpec(memory_space=pltpu.VMEM)
 
 
-def identity_matrix(size):
-    rows = lax.broadcasted_iota(jnp.int32, (size, size), 0)
-    cols = lax.broadcasted_iota(jnp.int32, (size, size), 1)
-    return (rows == cols).astype(F32).astype(jnp.bfloat16)
-
-
-def flip(eye, tile):
-    return lax.dot_general(eye, tile, (((1,), (1,)), ((), ())), preferred_element_type=F32)
-
-
 def flip_blocks(src_ref, dst_ref):
     blocks, _, block_len = src_ref.shape
-    eye = identity_matrix(block_len)
     for n in range(blocks):
-        dst_ref[pl.ds(n, block_len, stride=blocks), :] = flip(eye, src_ref[n])
+        dst_ref[pl.ds(n, block_len, stride=blocks), :] = src_ref[n].astype(F32).T
 
 
 def log_rates(poles):
     return jnp.log1p(-(1.0 - poles))
-
-
-def spread(ref, p):
-    return jnp.broadcast_to(ref[p : p + 1, :], (ROWS, ref.shape[1]))
 
 
 def cleared(ref, count):
@@ -48,24 +34,48 @@
     return ref[pl.ds(n, modes, stride=blocks), :]
 
 
+def horner(rate, terms):
+    total = terms[-1]
+    for term in terms[-2::-1]:
+        total = rate * total + term
+    return total
+
+
+def step_rows(ref, j, blocks, half):
+    at = lambda i: pl.multiple_of((j * STEP + i) * blocks + half * ROWS, ROWS)
+    return [ref[pl.ds(at(i), ROWS), :] for i in range(STEP)]
+
+
+def wide_rows(table, first, count):
+    return [jnp.broadcast_to(table[p : p + 1, :], (ROWS, table.shape[1])) for p in range(first, first + count)]
+
+
+def put(ref, blocks, half, first, rows):
+    for k, row in enumerate(rows):
+        at = (first + k) * blocks + half * ROWS
+        ref[at : at + ROWS, :] = row
+
+
 def ends_kernel(blocks, spans, moved_ref, lam_ref, gt_ref, h_ref, head_ref):
     modes = lam_ref.shape[0]
     block_len = moved_ref.shape[2]
+    steps = block_len // STEP
     flip_blocks(moved_ref, gt_ref)
+    lam = lam_ref[...]
+    rate = log_rates(lam)
+    wide = wide_rows(lam, 0, modes)
+    jump = wide_rows(jnp.exp(STEP * rate), 0, modes)
     empty = cleared(h_ref, modes)
     for half in range(blocks // ROWS):
-        wide = [spread(lam_ref, p) for p in range(modes)]
 
         def back(i, held):
-            at = pl.multiple_of((block_len - 1 - i) * blocks + half * ROWS, ROWS)
-            g = gt_ref[pl.ds(at, ROWS), :]
-            return tuple(l * a + g for l, a in zip(wide, held))
-
-        ends = lax.fori_loop(0, block_len, back, empty, unroll=8)
-        for p in range(modes):
-            at = p * blocks + half * ROWS
-            h_ref[at : at + ROWS, :] = ends[p]
-    step = jnp.exp(block_len * log_rates(lam_ref[...]))
+            j = steps - 1 - i
+            g = step_rows(gt_ref, j, blocks, half)
+            sums = [horner(l, g) for l in wide]
+            return tuple(l * a + h for l, a, h in zip(jump, held, sums))
+
+        put(h_ref, blocks, half, 0, lax.fori_loop(0, steps, back, empty, unroll=4))
+    step = jnp.exp(block_len * rate)
     head = folded(step, [block_rows(h_ref, n, blocks, modes) for n in range(blocks)])
     for span in range(spans):
         head_ref[span] = head
@@ -84,7 +94,7 @@
     empty = cleared(t_ref, GROUP)
     for half in range(blocks // ROWS):
         for first in range(0, modes, GROUP):
-            wide = [spread(lam_ref, first + k) for k in range(GROUP)]
+            wide = wide_rows(lam_ref[...], first, GROUP)
 
             def back(i, held):
                 at = pl.multiple_of((block_len - 1 - i) * blocks + half * ROWS, ROWS)
@@ -120,8 +130,8 @@
         next_ref[pl.ds(n, modes, stride=blocks), :] = total
         total = block_step * total + block_rows(h_ref, n, blocks, modes)
     for half in range(blocks // ROWS):
-        wide = [spread(lam_ref, p) for p in range(modes)]
-        gain = [spread(res_ref, p) for p in range(modes)]
+        wide = wide_rows(lam_ref[...], 0, modes)
+        gain = wide_rows(res_ref[...], 0, modes)
         start = tuple(
             next_ref[p * blocks + half * ROWS : p * blocks + half * ROWS + ROWS, :]
             for p in range(modes)
@@ -138,17 +148,15 @@
             return held
 
         lax.fori_loop(0, block_len, step, start, unroll=4)
-    eye = identity_matrix(chans)
     for n in range(blocks):
-        tile = flat_ref[pl.ds(n, block_len, stride=blocks), :].astype(jnp.bfloat16)
-        out_ref[n] = flip(eye, tile).astype(jnp.bfloat16)
+        out_ref[n] = flat_ref[pl.ds(n, block_len, stride=blocks), :].T.astype(jnp.bfloat16)
 
 
 def mode_sums(first, blocks, x_ref, gt_ref, lam_ref, h_ref, t_ref, parts_refs):
     block_len = gt_ref.shape[0] // blocks
     lam = lam_ref[first : first + GROUP, :]
     empty = cleared(parts_refs[0], GROUP)
-    wide = [spread(lam_ref, first + k) for k in range(GROUP)]
+    wide = wide_rows(lam, 0, GROUP)
     for half in range(blocks // ROWS):
 
         def ahead(i, held):

time: 77.4 us -> 76.8 us (level)
  transfers between devices with their start and end apart: 17 -> 17, of which waited for: 6 -> 6; matrix products, arithmetic and copies ran while one was open for 0% -> 0% of each run, Pallas kernels for 15% -> 14%
where the time goes in v4:
time: 76.8 us; the launch traced here: 76.4 us
  starting transfers between devices  50.8 us (66%)
  Pallas kernels  14.5 us (19%)
  waiting for transfers between devices  9.33 us (12%)
  local copies, waits for them, and re-layouts  0.89 us (1%)
  between operations  0.8 us (1%)
    all_to_all x3, starting transfers between devices, swap(): return lax.all_to_all(part, axis, split_axis=0, concat_axis=0, tiled=True)  21.3 us
    ppermute x7, starting transfers between devices, moved_pieces(): return [at(0)] + [lax.ppermute(at(s), 'chan', ring(s)) for s in shifts]  16.5 us
    ppermute x6, starting transfers between devices, rotated(): lax.ppermute(part, 'len', [(i, hop(i, s)) for i in range(spans)])  9.77 us
    pallas_call x1, Pallas kernels, body(): call(functools.partial(sums_kernel, blocks, shifts), shape(5 * modes, cha...  5.61 us
    all_to_all x3, waiting for transfers between devices, swap(): return lax.all_to_all(part, axis, split_axis=0, concat_axis=0, tiled=True)  5.38 us
    ppermute x6, waiting for transfers between devices, rotated(): lax.ppermute(part, 'len', [(i, hop(i, s)) for i in range(spans)])  3.93 us
    pallas_call x1, Pallas kernels, body(): call(functools.partial(input_grad_kernel, blocks, spans), jax.ShapeDtypeS...  3.65 us
    ppermute x1, starting transfers between devices, moved_pieces(): got = lax.ppermute(part, 'chan', [(i, i ^ 1) for i in range(blocks)])  3.33 us
  transfers between devices with their start and end apart: 17, of which 6 were waited for; matrix products, arithmetic and copies ran while one was open for 0% of the time, Pallas kernels for 14%

profile of v4, /device:TPU:1, one launch (start us, length us, event | category | flops | bytes accessed | tf_op | source)
XLA Modules:
  0.0 76.4 jit_solution(13377051815836435859)
XLA Ops:
  0.6 3.3 %collective-permute-start = (bf16[16,128,128]{2,1,0:T(8,128)(2,1)}, bf16[16,128,128]{2,1,0:T(8,128)(2,1)S(1)}, u32[]{:S(2)}, u32[]{:S(2)}) collective-permute-start(bf16[16,128,128]{2,1,0:T(8,128)(2,1)} %bitcast.51), channel_id=1, source_target_pairs={{0,1},{1,0},{2,3},{3,2},{4,5},{5,4},{6,7},{7,6},{8,9},{9,8},{10,11... | collective-permute-start | bytes 1572872 | tf_op jit(solution)/shard_map/ppermute | solution.py:300
  4.0 0.0 copy-start.2
  4.0 7.0 %all-to-all-start = ((bf16[16,128,128]{2,1,0:T(8,128)(2,1)}), bf16[16,128,128]{2,1,0:T(8,128)(2,1)S(1)}, u32[]{:S(2)}, u32[]{:S(2)}) async-start(bf16[16,128,128]{2,1,0:T(8,128)(2,1)} %bitcast.50), calls=%async_computation | async-start | bytes 1048576 | tf_op jit(solution)/shard_map/all_to_all | solution.py:285
  10.9 0.0 copy-done.2
  11.0 0.0 collective-permute-done
  11.1 5.4 %collective-permute-start.1 = (bf16[2,128,128]{2,1,0:T(8,128)(2,1)S(1)}, bf16[2,128,128]{2,1,0:T(8,128)(2,1)S(1)}, u32[]{:S(2)}, u32[]{:S(2)}) collective-permute-start(bf16[2,128,128]{2,1,0:T(8,128)(2,1)S(1)} %pad_maximum_fusion.1), channel_id=1, source_target_pairs={{0,8},{1,9},{2,10},{3,11},{4,12},{5,13},{6,14},{7,15},{8,0},{9,1},... | collective-permute-start | bytes 196616 | tf_op jit(solution)/shard_map/ppermute | solution.py:307
  16.5 0.4 collective-permute-start.2
  16.8 4.3 %collective-permute-start.3 = (bf16[2,128,128]{2,1,0:T(8,128)(2,1)S(1)}, bf16[2,128,128]{2,1,0:T(8,128)(2,1)S(1)}, u32[]{:S(2)}, u32[]{:S(2)}) collective-permute-start(bf16[2,128,128]{2,1,0:T(8,128)(2,1)S(1)} %pad_maximum_fusion.3), channel_id=1, source_target_pairs={{0,10},{1,11},{2,12},{3,13},{4,14},{5,15},{6,0},{7,1},{8,2},{9,3},... | collective-permute-start | bytes 196616 | tf_op jit(solution)/shard_map/ppermute | solution.py:307
  21.1 0.4 collective-permute-start.4
  21.5 3.4 %collective-permute-start.5 = (bf16[2,128,128]{2,1,0:T(8,128)(2,1)S(1)}, bf16[2,128,128]{2,1,0:T(8,128)(2,1)S(1)}, u32[]{:S(2)}, u32[]{:S(2)}) collective-permute-start(bf16[2,128,128]{2,1,0:T(8,128)(2,1)S(1)} %pad_maximum_fusion.5), channel_id=1, source_target_pairs={{0,12},{1,13},{2,14},{3,15},{4,0},{5,1},{6,2},{7,3},{8,4},{9,5},{1... | collective-permute-start | bytes 196616 | tf_op jit(solution)/shard_map/ppermute | solution.py:307
  24.8 0.0 copy-start
  24.8 2.5 %all-to-all-done.moved_ref = bf16[16,128,128]{2,1,0:T(8,128)(2,1)S(1)} async-done(((bf16[16,128,128]{2,1,0:T(8,128)(2,1)}), bf16[16,128,128]{2,1,0:T(8,128)(2,1)S(1)}, u32[]{:S(2)}, u32[]{:S(2)}) %all-to-all-start) | async-done | bytes 524320 | tf_op jit(solution)/shard_map/all_to_all | solution.py:285
  27.3 0.0 copy-done
  27.3 2.2 %block_ends.1 = (f32[2048,128]{1,0:T(8,128)S(1)}, f32[256,128]{1,0:T(8,128)S(1)}, f32[16,16,128]{2,1,0:T(8,128)}) custom-call(bf16[16,128,128]{2,1,0:T(8,128)(2,1)S(1)} %all-to-all-done.moved_ref, f32[16,128]{1,0:T(8,128)S(1)} %bitcast.41), custom_call_target="tpu_custom_call" | custom-call | flops 8388608 | bytes 1048576 | tf_op jit(solution)/shard_map/block_ends/pallas_call | solution.py:329
  29.5 6.8 %all-to-all-start.1 = ((f32[16,16,128]{2,1,0:T(8,128)}), f32[16,16,128]{2,1,0:T(8,128)S(1)}, u32[]{:S(2)}, u32[]{:S(2)}) async-start(f32[16,16,128]{2,1,0:T(8,128)} %get-tuple-element.8), calls=%async_computation.1 | async-start | bytes 262144 | tf_op jit(solution)/shard_map/all_to_all | solution.py:285
  36.3 0.0 collective-permute-done.1.refs_1_
  36.3 0.1 collective-permute-start.6
  36.4 0.0 collective-permute-done.2.refs_2_
  36.4 2.7 %collective-permute-start.7 = (bf16[2,128,128]{2,1,0:T(8,128)(2,1)S(1)}, bf16[2,128,128]{2,1,0:T(8,128)(2,1)S(1)}, u32[]{:S(2)}, u32[]{:S(2)}) collective-permute-start(bf16[2,128,128]{2,1,0:T(8,128)(2,1)S(1)} %pad_maximum_fusion.7), channel_id=1, source_target_pairs={{0,14},{1,15},{2,0},{3,1},{4,2},{5,3},{6,4},{7,5},{8,6},{9,7},{10,... | collective-permute-start | bytes 196616 | tf_op jit(solution)/shard_map/ppermute | solution.py:307
  39.1 2.3 %weighted.1.refs_11_ = f32[256,128]{1,0:T(8,128)S(1)} custom-call(f32[2048,128]{1,0:T(8,128)S(1)} %get-tuple-element.9.gt_ref.refs_8_, f32[16,128]{1,0:T(8,128)S(1)} %bitcast.42), custom_call_target="tpu_custom_call" | custom-call | flops 16777216 | bytes 1048576 | tf_op jit(solution)/shard_map/weighted/pallas_call | solution.py:338
  41.4 0.0 collective-permute-done.3.refs_3_
  41.4 0.0 collective-permute-done.4.refs_4_
  41.4 0.0 collective-permute-done.5.refs_5_
  41.4 0.0 collective-permute-done.6.refs_6_
  41.4 0.0 collective-permute-done.7.refs_7_
  41.4 0.0 copy-start.1
  41.5 5.6 %mode_sums.1._.refs_0_ = f32[80,128]{1,0:T(8,128)S(1)} custom-call(bf16[2,128,128]{2,1,0:T(8,128)(2,1)S(1)} %pad_maximum_fusion.refs_0_, bf16[2,128,128]{2,1,0:T(8,128)(2,1)S(1)} %collective-permute-done.1.refs_1_, bf16[2,128,128]{2,1,0:T(8,128)(2,1)S(1)} %collective-permute-done.2.refs_2_, bf16[2,128,128]{2,1,0:T(8,128)(2,1)S(1)} %collective-permute-done.3.refs_3_, ...), custom_call_target="tpu_custom_call" | custom-call | flops 33554432 | bytes 1048576 | tf_op jit(solution)/shard_map/mode_sums/pallas_call | solution.py:346
  47.1 0.0 all-to-all-done.1.heads_ref.refs_4_
  47.1 0.0 copy-done.1
  47.1 3.7 %input_grad.1 = bf16[16,128,128]{2,1,0:T(8,128)(2,1)} custom-call(f32[16,16,128]{2,1,0:T(8,128)S(1)} %all-to-all-done.1.heads_ref.refs_4_, f32[2048,128]{1,0:T(8,128)S(1)} %get-tuple-element.9.gt_ref.refs_8_, f32[16,128]{1,0:T(8,128)S(1)} %bitcast.44, f32[16,128]{1,0:T(8,128)S(1)} %bitcast.47, f32[256,128]{1,0:T(8,128)S(1)} %get-tuple-element.10.refs_10_.h_ref, ...), custom_call_target="tpu_custom_call" | custom-call | flops 16777216 | bytes 1048576 | tf_op jit(solution)/shard_map/input_grad/pallas_call | solution.py:355
  50.7 7.5 %all-to-all-start.2 = ((bf16[16,128,128]{2,1,0:T(8,128)(2,1)}), bf16[16,128,128]{2,1,0:T(8,128)(2,1)S(1)}, u32[]{:S(2)}, u32[]{:S(2)}) async-start(bf16[16,128,128]{2,1,0:T(8,128)(2,1)} %input_grad.1), calls=%async_computation.2 | async-start | bytes 1048576 | tf_op jit(solution)/shard_map/all_to_all | solution.py:285
  58.3 1.4 %collective-permute-start.8 = (f32[80,128]{1,0:T(8,128)S(1)}, f32[80,128]{1,0:T(8,128)S(1)}, u32[]{:S(2)}, u32[]{:S(2)}) collective-permute-start(f32[80,128]{1,0:T(8,128)S(1)} %mode_sums.1._.refs_0_), channel_id=1, source_target_pairs={{0,16},{16,32},{32,48},{48,0},{64,80},{80,96},{96,112},{112,64},{1... | collective-permute-start | bytes 122888 | tf_op jit(solution)/shard_map/ppermute | solution.py:292
  59.6 2.4 %collective-permute-start.9 = (f32[80,128]{1,0:T(8,128)S(1)}, f32[80,128]{1,0:T(8,128)S(1)}, u32[]{:S(2)}, u32[]{:S(2)}) collective-permute-start(f32[80,128]{1,0:T(8,128)S(1)} %mode_sums.1._.refs_0_), channel_id=1, source_target_pairs={{0,32},{16,48},{32,0},{48,16},{64,96},{80,112},{96,64},{112,80},{1... | collective-permute-start | bytes 122888 | tf_op jit(solution)/shard_map/ppermute | solution.py:292
  62.0 1.2 %collective-permute-start.10 = (f32[80,128]{1,0:T(8,128)S(1)}, f32[80,128]{1,0:T(8,128)S(1)}, u32[]{:S(2)}, u32[]{:S(2)}) collective-permute-start(f32[80,128]{1,0:T(8,128)S(1)} %mode_sums.1._.refs_0_), channel_id=1, source_target_pairs={{0,48},{16,0},{32,16},{48,32},{64,112},{80,64},{96,80},{112,96},{1... | collective-permute-start | bytes 122888 | tf_op jit(solution)/shard_map/ppermute | solution.py:292
  63.2 0.0 collective-permute-done.8.refs_1_
  63.2 1.4 %collective-permute-done.9.refs_2_ = f32[80,128]{1,0:T(8,128)S(1)} collective-permute-done((f32[80,128]{1,0:T(8,128)S(1)}, f32[80,128]{1,0:T(8,128)S(1)}, u32[]{:S(2)}, u32[]{:S(2)}) %collective-permute-start.9) | collective-permute-done | bytes 40992 | tf_op jit(solution)/shard_map/ppermute | solution.py:292
  64.7 0.5 collective-permute-done.10.refs_3_
  65.2 0.1 join.1.refs_0_
  65.2 1.3 %collective-permute-start.11 = (f32[80,128]{1,0:T(8,128)S(1)}, f32[80,128]{1,0:T(8,128)S(1)}, u32[]{:S(2)}, u32[]{:S(2)}) collective-permute-start(f32[80,128]{1,0:T(8,128)S(1)} %join.1.refs_0_), channel_id=1, source_target_pairs={{0,64},{16,80},{32,96},{48,112},{64,128},{80,144},{96,160},{112,17... | collective-permute-start | bytes 122888 | tf_op jit(solution)/shard_map/ppermute | solution.py:292
  66.5 2.4 %collective-permute-start.12 = (f32[80,128]{1,0:T(8,128)S(1)}, f32[80,128]{1,0:T(8,128)S(1)}, u32[]{:S(2)}, u32[]{:S(2)}) collective-permute-start(f32[80,128]{1,0:T(8,128)S(1)} %join.1.refs_0_), channel_id=1, source_target_pairs={{0,128},{16,144},{32,160},{48,176},{64,192},{80,208},{96,224},{112... | collective-permute-start | bytes 122888 | tf_op jit(solution)/shard_map/ppermute | solution.py:292
  68.9 1.2 %collective-permute-start.13 = (f32[80,128]{1,0:T(8,128)S(1)}, f32[80,128]{1,0:T(8,128)S(1)}, u32[]{:S(2)}, u32[]{:S(2)}) collective-permute-start(f32[80,128]{1,0:T(8,128)S(1)} %join.1.refs_0_), channel_id=1, source_target_pairs={{0,192},{16,208},{32,224},{48,240},{64,0},{80,16},{96,32},{112,48}... | collective-permute-start | bytes 122888 | tf_op jit(solution)/shard_map/ppermute | solution.py:292
  70.1 0.0 collective-permute-done.11.refs_1_
  70.1 0.8 %collective-permute-done.12.refs_2_ = f32[80,128]{1,0:T(8,128)S(1)} collective-permute-done((f32[80,128]{1,0:T(8,128)S(1)}, f32[80,128]{1,0:T(8,128)S(1)}, u32[]{:S(2)}, u32[]{:S(2)}) %collective-permute-start.12) | collective-permute-done | bytes 40992 | tf_op jit(solution)/shard_map/ppermute | solution.py:292
  70.9 1.1 %collective-permute-done.13.refs_3_ = f32[80,128]{1,0:T(8,128)S(1)} collective-permute-done((f32[80,128]{1,0:T(8,128)S(1)}, f32[80,128]{1,0:T(8,128)S(1)}, u32[]{:S(2)}, u32[]{:S(2)}) %collective-permute-start.13) | collective-permute-done | bytes 40992 | tf_op jit(solution)/shard_map/ppermute | solution.py:292
  72.0 0.7 finish.1
  72.7 2.9 %all-to-all-done.2 = bf16[16,128,128]{2,1,0:T(8,128)(2,1)S(1)} async-done(((bf16[16,128,128]{2,1,0:T(8,128)(2,1)}), bf16[16,128,128]{2,1,0:T(8,128)(2,1)S(1)}, u32[]{:S(2)}, u32[]{:S(2)}) %all-to-all-start.2) | async-done | bytes 524320 | tf_op jit(solution)/shard_map/all_to_all | solution.py:285
  75.6 0.8 %copy.8 = bf16[2048,128]{1,0:T(8,128)(2,1)} copy(bf16[2048,128]{1,0:T(8,128)(2,1)S(1)} %bitcast.49) | data formatting | bytes 1048576
  (10 shorter events, 0.1 us)
Async XLA Ops:
  0.6 10.4 %collective-permute-start = (bf16[16,128,128]{2,1,0:T(8,128)(2,1)}, bf16[16,128,128]{2,1,0:T(8,128)(2,1)S(1)}, u32[]{:S(2)}, u32[]{:S(2)}) collective-permute-start(bf16[16,128,128]{2,1,0:T(8,128)(2,1)} %bitcast.51), channel_id=1, source_target_pairs={{0,1},{1,0},{2,3},{3,2},{4,5},{5,4},{6,7},{7,6},{8,9},{9,8},{10,11... | collective-permute-start | bytes 1572872 | tf_op jit(solution)/shard_map/ppermute | solution.py:300
  4.0 7.0 %copy-start.2 = (bf16[2048,128]{1,0:T(8,128)(2,1)S(1)}, bf16[2048,128]{1,0:T(8,128)(2,1)}, u32[]{:S(2)}) copy-start(bf16[2048,128]{1,0:T(8,128)(2,1)} %param.4) | copy-start | bytes 1572868
  4.0 23.4 %all-to-all-start = ((bf16[16,128,128]{2,1,0:T(8,128)(2,1)}), bf16[16,128,128]{2,1,0:T(8,128)(2,1)S(1)}, u32[]{:S(2)}, u32[]{:S(2)}) async-start(bf16[16,128,128]{2,1,0:T(8,128)(2,1)} %bitcast.50), calls=%async_computation | async-start | bytes 1048576 | tf_op jit(solution)/shard_map/all_to_all | solution.py:285
  11.1 25.2 %collective-permute-start.1 = (bf16[2,128,128]{2,1,0:T(8,128)(2,1)S(1)}, bf16[2,128,128]{2,1,0:T(8,128)(2,1)S(1)}, u32[]{:S(2)}, u32[]{:S(2)}) collective-permute-start(bf16[2,128,128]{2,1,0:T(8,128)(2,1)S(1)} %pad_maximum_fusion.1), channel_id=1, source_target_pairs={{0,8},{1,9},{2,10},{3,11},{4,12},{5,13},{6,14},{7,15},{8,0},{9,1},... | collective-permute-start | bytes 196616 | tf_op jit(solution)/shard_map/ppermute | solution.py:307
  16.5 20.0 %collective-permute-start.2 = (bf16[2,128,128]{2,1,0:T(8,128)(2,1)S(1)}, bf16[2,128,128]{2,1,0:T(8,128)(2,1)S(1)}, u32[]{:S(2)}, u32[]{:S(2)}) collective-permute-start(bf16[2,128,128]{2,1,0:T(8,128)(2,1)S(1)} %pad_maximum_fusion.2), channel_id=1, source_target_pairs={{0,6},{1,7},{2,8},{3,9},{4,10},{5,11},{6,12},{7,13},{8,14},{9,15},... | collective-permute-start | bytes 196616 | tf_op jit(solution)/shard_map/ppermute | solution.py:307
  16.8 24.6 %collective-permute-start.3 = (bf16[2,128,128]{2,1,0:T(8,128)(2,1)S(1)}, bf16[2,128,128]{2,1,0:T(8,128)(2,1)S(1)}, u32[]{:S(2)}, u32[]{:S(2)}) collective-permute-start(bf16[2,128,128]{2,1,0:T(8,128)(2,1)S(1)} %pad_maximum_fusion.3), channel_id=1, source_target_pairs={{0,10},{1,11},{2,12},{3,13},{4,14},{5,15},{6,0},{7,1},{8,2},{9,3},... | collective-permute-start | bytes 196616 | tf_op jit(solution)/shard_map/ppermute | solution.py:307
  21.1 20.3 %collective-permute-start.4 = (bf16[2,128,128]{2,1,0:T(8,128)(2,1)S(1)}, bf16[2,128,128]{2,1,0:T(8,128)(2,1)S(1)}, u32[]{:S(2)}, u32[]{:S(2)}) collective-permute-start(bf16[2,128,128]{2,1,0:T(8,128)(2,1)S(1)} %pad_maximum_fusion.4), channel_id=1, source_target_pairs={{0,4},{1,5},{2,6},{3,7},{4,8},{5,9},{6,10},{7,11},{8,12},{9,13},{1... | collective-permute-start | bytes 196616 | tf_op jit(solution)/shard_map/ppermute | solution.py:307
  21.5 19.9 %collective-permute-start.5 = (bf16[2,128,128]{2,1,0:T(8,128)(2,1)S(1)}, bf16[2,128,128]{2,1,0:T(8,128)(2,1)S(1)}, u32[]{:S(2)}, u32[]{:S(2)}) collective-permute-start(bf16[2,128,128]{2,1,0:T(8,128)(2,1)S(1)} %pad_maximum_fusion.5), channel_id=1, source_target_pairs={{0,12},{1,13},{2,14},{3,15},{4,0},{5,1},{6,2},{7,3},{8,4},{9,5},{1... | collective-permute-start | bytes 196616 | tf_op jit(solution)/shard_map/ppermute | solution.py:307
  24.8 2.5 %copy-start = (f32[128,16]{0,1:T(8,128)S(1)}, f32[128,16]{0,1:T(8,128)}, u32[]{:S(2)}) copy-start(f32[128,16]{0,1:T(8,128)} %param.6) | copy-start | bytes 24580
  29.5 17.5 %all-to-all-start.1 = ((f32[16,16,128]{2,1,0:T(8,128)}), f32[16,16,128]{2,1,0:T(8,128)S(1)}, u32[]{:S(2)}, u32[]{:S(2)}) async-start(f32[16,16,128]{2,1,0:T(8,128)} %get-tuple-element.8), calls=%async_computation.1 | async-start | bytes 262144 | tf_op jit(solution)/shard_map/all_to_all | solution.py:285
  36.3 5.1 %collective-permute-start.6 = (bf16[2,128,128]{2,1,0:T(8,128)(2,1)S(1)}, bf16[2,128,128]{2,1,0:T(8,128)(2,1)S(1)}, u32[]{:S(2)}, u32[]{:S(2)}) collective-permute-start(bf16[2,128,128]{2,1,0:T(8,128)(2,1)S(1)} %pad_maximum_fusion.6), channel_id=1, source_target_pairs={{0,2},{1,3},{2,4},{3,5},{4,6},{5,7},{6,8},{7,9},{8,10},{9,11},{10,... | collective-permute-start | bytes 196616 | tf_op jit(solution)/shard_map/ppermute | solution.py:307
  36.4 5.0 %collective-permute-start.7 = (bf16[2,128,128]{2,1,0:T(8,128)(2,1)S(1)}, bf16[2,128,128]{2,1,0:T(8,128)(2,1)S(1)}, u32[]{:S(2)}, u32[]{:S(2)}) collective-permute-start(bf16[2,128,128]{2,1,0:T(8,128)(2,1)S(1)} %pad_maximum_fusion.7), channel_id=1, source_target_pairs={{0,14},{1,15},{2,0},{3,1},{4,2},{5,3},{6,4},{7,5},{8,6},{9,7},{10,... | collective-permute-start | bytes 196616 | tf_op jit(solution)/shard_map/ppermute | solution.py:307
  41.4 5.6 %copy-start.1 = (f32[128,16]{0,1:T(8,128)S(1)}, f32[128,16]{0,1:T(8,128)}, u32[]{:S(2)}) copy-start(f32[128,16]{0,1:T(8,128)} %param.7) | copy-start | bytes 24580
  50.7 24.9 %all-to-all-start.2 = ((bf16[16,128,128]{2,1,0:T(8,128)(2,1)}), bf16[16,128,128]{2,1,0:T(8,128)(2,1)S(1)}, u32[]{:S(2)}, u32[]{:S(2)}) async-start(bf16[16,128,128]{2,1,0:T(8,128)(2,1)} %input_grad.1), calls=%async_computation.2 | async-start | bytes 1048576 | tf_op jit(solution)/shard_map/all_to_all | solution.py:285
  58.3 4.9 %collective-permute-start.8 = (f32[80,128]{1,0:T(8,128)S(1)}, f32[80,128]{1,0:T(8,128)S(1)}, u32[]{:S(2)}, u32[]{:S(2)}) collective-permute-start(f32[80,128]{1,0:T(8,128)S(1)} %mode_sums.1._.refs_0_), channel_id=1, source_target_pairs={{0,16},{16,32},{32,48},{48,0},{64,80},{80,96},{96,112},{112,64},{1... | collective-permute-start | bytes 122888 | tf_op jit(solution)/shard_map/ppermute | solution.py:292
  59.6 5.0 %collective-permute-start.9 = (f32[80,128]{1,0:T(8,128)S(1)}, f32[80,128]{1,0:T(8,128)S(1)}, u32[]{:S(2)}, u32[]{:S(2)}) collective-permute-start(f32[80,128]{1,0:T(8,128)S(1)} %mode_sums.1._.refs_0_), channel_id=1, source_target_pairs={{0,32},{16,48},{32,0},{48,16},{64,96},{80,112},{96,64},{112,80},{1... | collective-permute-start | bytes 122888 | tf_op jit(solution)/shard_map/ppermute | solution.py:292
  62.0 3.1 %collective-permute-start.10 = (f32[80,128]{1,0:T(8,128)S(1)}, f32[80,128]{1,0:T(8,128)S(1)}, u32[]{:S(2)}, u32[]{:S(2)}) collective-permute-start(f32[80,128]{1,0:T(8,128)S(1)} %mode_sums.1._.refs_0_), channel_id=1, source_target_pairs={{0,48},{16,0},{32,16},{48,32},{64,112},{80,64},{96,80},{112,96},{1... | collective-permute-start | bytes 122888 | tf_op jit(solution)/shard_map/ppermute | solution.py:292
  65.2 4.8 %collective-permute-start.11 = (f32[80,128]{1,0:T(8,128)S(1)}, f32[80,128]{1,0:T(8,128)S(1)}, u32[]{:S(2)}, u32[]{:S(2)}) collective-permute-start(f32[80,128]{1,0:T(8,128)S(1)} %join.1.refs_0_), channel_id=1, source_target_pairs={{0,64},{16,80},{32,96},{48,112},{64,128},{80,144},{96,160},{112,17... | collective-permute-start | bytes 122888 | tf_op jit(solution)/shard_map/ppermute | solution.py:292
  66.5 4.4 %collective-permute-start.12 = (f32[80,128]{1,0:T(8,128)S(1)}, f32[80,128]{1,0:T(8,128)S(1)}, u32[]{:S(2)}, u32[]{:S(2)}) collective-permute-start(f32[80,128]{1,0:T(8,128)S(1)} %join.1.refs_0_), channel_id=1, source_target_pairs={{0,128},{16,144},{32,160},{48,176},{64,192},{80,208},{96,224},{112... | collective-permute-start | bytes 122888 | tf_op jit(solution)/shard_map/ppermute | solution.py:292
  68.9 3.1 %collective-permute-start.13 = (f32[80,128]{1,0:T(8,128)S(1)}, f32[80,128]{1,0:T(8,128)S(1)}, u32[]{:S(2)}, u32[]{:S(2)}) collective-permute-start(f32[80,128]{1,0:T(8,128)S(1)} %join.1.refs_0_), channel_id=1, source_target_pairs={{0,192},{16,208},{32,224},{48,240},{64,0},{80,16},{96,32},{112,48}... | collective-permute-start | bytes 122888 | tf_op jit(solution)/shard_map/ppermute | solution.py:292

commit v5 on v4

--- a/solution.py
+++ b/solution.py
@@ -44,6 +44,11 @@
 def step_rows(ref, j, blocks, half):
     at = lambda i: pl.multiple_of((j * STEP + i) * blocks + half * ROWS, ROWS)
     return [ref[pl.ds(at(i), ROWS), :] for i in range(STEP)]
+
+
+def slot(j, blocks, half, modes, p):
+    at = ((j * (blocks // ROWS) + half) * modes + p) * ROWS
+    return pl.ds(pl.multiple_of(at, ROWS), ROWS)
 
 
 def wide_rows(table, first, count):
@@ -74,7 +79,7 @@
             sums = [horner(l, g) for l in wide]
             return tuple(l * a + h for l, a, h in zip(jump, held, sums))
 
-        put(h_ref, blocks, half, 0, lax.fori_loop(0, steps, back, empty, unroll=4))
+        put(h_ref, blocks, half, 0, lax.fori_loop(0, steps, back, empty, unroll=8))
     step = jnp.exp(block_len * rate)
     head = folded(step, [block_rows(h_ref, n, blocks, modes) for n in range(blocks)])
     for span in range(spans):
@@ -88,26 +93,35 @@
     return total
 
 
-def weighted_kernel(blocks, gt_ref, lam_ref, t_ref):
+def weighted_kernel(blocks, gt_ref, lam_ref, sub_ref, sub_t_ref, t_ref):
     modes = lam_ref.shape[0]
-    block_len = gt_ref.shape[0] // blocks
+    steps = gt_ref.shape[0] // blocks // STEP
+    lam = lam_ref[...]
+    jumps = jnp.exp(STEP * log_rates(lam))
     empty = cleared(t_ref, GROUP)
-    for half in range(blocks // ROWS):
-        for first in range(0, modes, GROUP):
-            wide = wide_rows(lam_ref[...], first, GROUP)
+    for first in range(0, modes, GROUP):
+        wide = wide_rows(lam, first, GROUP)
+        jump = wide_rows(jumps, first, GROUP)
+        for half in range(blocks // ROWS):
 
             def back(i, held):
-                at = pl.multiple_of((block_len - 1 - i) * blocks + half * ROWS, ROWS)
-                g = gt_ref[pl.ds(at, ROWS), :]
+                j = steps - 1 - i
+                g = step_rows(gt_ref, j, blocks, half)
+                scaled = [(k + 1.0) * row for k, row in enumerate(g)]
                 adjoint, weighted = held
-                adjoint = tuple(l * a + g for l, a in zip(wide, adjoint))
-                weighted = tuple(l * q + a for l, q, a in zip(wide, weighted, adjoint))
-                return (adjoint, weighted)
-
-            weighted = lax.fori_loop(0, block_len, back, (empty,) * 2, unroll=8)[1]
-            for k in range(GROUP):
-                at = (first + k) * blocks + half * ROWS
-                t_ref[at : at + ROWS, :] = weighted[k]
+                after, total = [], []
+                for k in range(GROUP):
+                    rows = slot(j, blocks, half, modes, first + k)
+                    head = horner(wide[k], g)
+                    part = horner(wide[k], scaled)
+                    sub_ref[rows, :] = head
+                    sub_t_ref[rows, :] = part
+                    total.append(jump[k] * (weighted[k] + STEP * adjoint[k]) + part)
+                    after.append(jump[k] * adjoint[k] + head)
+                return (tuple(after), tuple(total))
+
+            weighted = lax.fori_loop(0, steps, back, (empty,) * 2, unroll=4)[1]
+            put(t_ref, blocks, half, first, weighted)
 
 
 def folded_after(step, heads, place):
@@ -147,41 +161,64 @@
             flat_ref[pl.ds(at, ROWS), :] = terms[0]
             return held
 
-        lax.fori_loop(0, block_len, step, start, unroll=4)
+        lax.fori_loop(0, block_len, step, start, unroll=8)
     for n in range(blocks):
         out_ref[n] = flat_ref[pl.ds(n, block_len, stride=blocks), :].T.astype(jnp.bfloat16)
 
 
-def mode_sums(first, blocks, x_ref, gt_ref, lam_ref, h_ref, t_ref, parts_refs):
+def lag_sums(blocks, steps, x_ref, gt_ref, zero):
+    lags = (zero,) * STEP
+    for half in range(blocks // ROWS):
+
+        def ahead(j, held):
+            g = step_rows(gt_ref, j, blocks, half)
+            x = step_rows(x_ref, j, blocks, half)
+            return tuple(
+                total + sum(g[i] * x[i - k] for i in range(k, STEP)) for k, total in enumerate(held)
+            )
+
+        lags = lax.fori_loop(0, steps, ahead, lags, unroll=8)
+    return [jnp.sum(lag, axis=0, keepdims=True) for lag in lags]
+
+
+def mode_sums(first, blocks, lags, x_ref, gt_ref, subs, lam_ref, h_ref, t_ref, parts_refs):
+    modes = lam_ref.shape[0]
     block_len = gt_ref.shape[0] // blocks
+    steps = block_len // STEP
+    sub_ref, sub_t_ref = subs
     lam = lam_ref[first : first + GROUP, :]
+    rate = log_rates(lam)
     empty = cleared(parts_refs[0], GROUP)
     wide = wide_rows(lam, 0, GROUP)
+    jump = wide_rows(jnp.exp(STEP * rate), 0, GROUP)
+    jump_slope = wide_rows(STEP * jnp.exp((STEP - 1) * rate), 0, GROUP)
     for half in range(blocks // ROWS):
 
-        def ahead(i, held):
-            at = pl.multiple_of(i * blocks + half * ROWS, ROWS)
-            g = gt_ref[pl.ds(at, ROWS), :]
-            x = x_ref[pl.ds(at, ROWS), :]
-            state, slope, res_sum, pole_sum = held
-            slope = tuple(l * d + s for l, d, s in zip(wide, slope, state))
-            state = tuple(l * s + x for l, s in zip(wide, state))
-            res_sum = tuple(r + g * s for r, s in zip(res_sum, state))
-            pole_sum = tuple(q + g * d for q, d in zip(pole_sum, slope))
-            return (state, slope, res_sum, pole_sum)
-
-        results = lax.fori_loop(0, block_len, ahead, (empty,) * 4, unroll=8)
-        for k in range(GROUP):
-            at = k * blocks + half * ROWS
-            for ref, result in zip(parts_refs, results):
-                ref[at : at + ROWS, :] = result[k]
-    rate = log_rates(lam)
+        def ahead(j, held):
+            x = step_rows(x_ref, j, blocks, half)[::-1]
+            scaled = [k * x[k] for k in range(1, STEP)]
+            state, slope, res_sum, pole_sum = [list(part) for part in held]
+            for k in range(GROUP):
+                rows = slot(j, blocks, half, modes, first + k)
+                after = wide[k] * sub_ref[rows, :]
+                res_sum[k] = res_sum[k] + state[k] * after
+                pole_sum[k] = pole_sum[k] + (slope[k] * after + state[k] * sub_t_ref[rows, :])
+                grown = jump[k] * slope[k] + jump_slope[k] * state[k]
+                slope[k] = grown + horner(wide[k], scaled)
+                state[k] = jump[k] * state[k] + horner(wide[k], x)
+            return (tuple(state), tuple(slope), tuple(res_sum), tuple(pole_sum))
+
+        results = lax.fori_loop(0, steps, ahead, (empty,) * 4, unroll=8)
+        for ref, result in zip(parts_refs, results):
+            put(ref, blocks, half, 0, result)
     block_step = jnp.exp(block_len * rate)
     block_slope = block_len * jnp.exp((block_len - 1) * rate)
     own = lambda ref, n: ref[pl.ds(n, GROUP, stride=blocks), :]
     of_all = lambda ref, n: ref[pl.ds(first * blocks + n, GROUP, stride=blocks), :]
     s_ref, d_ref, r_ref, q_ref = parts_refs
-    state, slope, res_sum, pole_sum, total, weighted = [jnp.zeros(lam.shape, F32)] * 6
+    state, slope, total, weighted = [jnp.zeros(lam.shape, F32)] * 4
+    res_sum = horner(lam, lags)
+    pole_sum = horner(lam, [k * lags[k] for k in range(1, STEP)])
     for n in range(blocks):
         after = lam * of_all(h_ref, n)
         res_sum = res_sum + (own(r_ref, n) + state * after)
@@ -196,7 +233,7 @@
 
 def sums_kernel(blocks, shifts, *refs):
     pieces, refs = refs[: len(shifts) + 1], refs[len(shifts) + 1 :]
-    gt_ref, lam_ref, h_ref, t_ref, pay_ref, moved_ref, xt_ref, *parts = refs
+    gt_ref, sub_ref, sub_t_ref, lam_ref, h_ref, t_ref, pay_ref, moved_ref, xt_ref, *parts = refs
     modes = lam_ref.shape[0]
     chips = blocks // 2
     place = lax.axis_index("chan")
@@ -206,8 +243,11 @@
         moved_ref[source + core] = ref[0]
         moved_ref[source + 1 - core] = ref[1]
     flip_blocks(moved_ref, xt_ref)
+    steps = gt_ref.shape[0] // blocks // STEP
+    lags = lag_sums(blocks, steps, xt_ref, gt_ref, cleared(parts[0], 1)[0])
+    subs = (sub_ref, sub_t_ref)
     for first in range(0, modes, GROUP):
-        items = mode_sums(first, blocks, xt_ref, gt_ref, lam_ref, h_ref, t_ref, parts)
+        items = mode_sums(first, blocks, lags, xt_ref, gt_ref, subs, lam_ref, h_ref, t_ref, parts)
         for k, item in enumerate(items):
             pay_ref[k * modes + first : k * modes + first + GROUP, :] = item
 
@@ -335,9 +375,10 @@
         2 * work,
     )(moved_grads, poles)
     heads = swap(head, "len")
-    weighted = call(
+    subs = shape(held * block_len // STEP, chans)
+    sub_heads, sub_weighted, weighted = call(
         functools.partial(weighted_kernel, blocks),
-        shape(held, chans),
+        (subs, subs, shape(held, chans)),
         2,
         [],
         "weighted",
@@ -346,12 +387,12 @@
     pay = call(
         functools.partial(sums_kernel, blocks, shifts),
         shape(5 * modes, chans),
-        len(pieces) + 4,
+        len(pieces) + 6,
         [pltpu.VMEM((blocks, chans, block_len), jnp.bfloat16), scratch(flat, chans)]
         + [scratch(GROUP * blocks, chans)] * 4,
         "mode_sums",
         8 * work,
-    )(*pieces, flat_grads, poles, ends, weighted)
+    )(*pieces, flat_grads, sub_heads, sub_weighted, poles, ends, weighted)
     rounded = call(
         functools.partial(input_grad_kernel, blocks, spans),
         jax.ShapeDtypeStruct((blocks, chans, block_len), jnp.bfloat16),

time: 76.8 us -> 75.2 us (0.979)
  starting transfers between devices: 50.8 us -> 47.6 us
  waiting for transfers between devices: 9.33 us -> 10.8 us
  local copies, waits for them, and re-layouts: 0.89 us -> 1.74 us
    ppermute x6, waiting for transfers between devices: 3.93 us -> 7.87 us  [rotated(): lax.ppermute(part, 'len', [(i, hop(i, s)) for i in range(spans)])]
    all_to_all x3, waiting for transfers between devices: 5.38 us -> 2.88 us  [swap(): return lax.all_to_all(part, axis, split_axis=0, concat_axis=0, tiled=True)]
    ppermute x6, starting transfers between devices: 9.77 us -> 7.49 us  [rotated(): lax.ppermute(part, 'len', [(i, hop(i, s)) for i in range(spans)])]
    pallas_call x1, Pallas kernels: 5.61 us -> 4.26 us  [body(): call(functools.partial(sums_kernel, blocks, shifts), shape(5 * modes, cha...]
    all_to_all x3, starting transfers between devices: 21.3 us -> 20.3 us  [swap(): return lax.all_to_all(part, axis, split_axis=0, concat_axis=0, tiled=True)]
    squeeze x2, local copies, waits for them, and re-layouts: 0.08 us -> 0.93 us  [moved_pieces(): lax.dynamic_slice(half, ((chip + s) % chips, core, 0, 0), (1, 1, *half.sh...]
    pallas_call x1, Pallas kernels: 2.28 us -> 3.06 us  [body(): call(functools.partial(weighted_kernel, blocks), (subs, subs, shape(held,...]
  transfers between devices with their start and end apart: 17 -> 17, of which waited for: 6 -> 6; matrix products, arithmetic and copies ran while one was open for 0% -> 1% of each run, Pallas kernels for 14% -> 14%
where the time goes in v5:
time: 75.2 us; the launch traced here: 74.7 us
  starting transfers between devices  47.6 us (63%)
  Pallas kernels  13.8 us (18%)
  waiting for transfers between devices  10.8 us (14%)
  local copies, waits for them, and re-layouts  1.74 us (2%)
  between operations  0.8 us (1%)
    all_to_all x3, starting transfers between devices, swap(): return lax.all_to_all(part, axis, split_axis=0, concat_axis=0, tiled=True)  20.3 us
    ppermute x7, starting transfers between devices, moved_pieces(): return [at(0)] + [lax.ppermute(at(s), 'chan', ring(s)) for s in shifts]  16.5 us
    ppermute x6, waiting for transfers between devices, rotated(): lax.ppermute(part, 'len', [(i, hop(i, s)) for i in range(spans)])  7.87 us
    ppermute x6, starting transfers between devices, rotated(): lax.ppermute(part, 'len', [(i, hop(i, s)) for i in range(spans)])  7.49 us
    pallas_call x1, Pallas kernels, body(): call(functools.partial(sums_kernel, blocks, shifts), shape(5 * modes, cha...  4.26 us
    pallas_call x1, Pallas kernels, body(): call(functools.partial(input_grad_kernel, blocks, spans), jax.ShapeDtypeS...  3.54 us
    ppermute x1, starting transfers between devices, moved_pieces(): got = lax.ppermute(part, 'chan', [(i, i ^ 1) for i in range(blocks)])  3.33 us
    pallas_call x1, Pallas kernels, body(): call(functools.partial(weighted_kernel, blocks), (subs, subs, shape(held,...  3.06 us
  transfers between devices with their start and end apart: 17, of which 6 were waited for; matrix products, arithmetic and copies ran while one was open for 1% of the time, Pallas kernels for 14%

profile of v5, /device:TPU:1, one launch (start us, length us, event | category | flops | bytes accessed | tf_op | source)
XLA Modules:
  0.0 74.7 jit_solution(13246350058296944699)
XLA Ops:
  0.6 0.0 copy-start
  0.6 3.3 %collective-permute-start = (bf16[16,128,128]{2,1,0:T(8,128)(2,1)}, bf16[16,128,128]{2,1,0:T(8,128)(2,1)S(1)}, u32[]{:S(2)}, u32[]{:S(2)}) collective-permute-start(bf16[16,128,128]{2,1,0:T(8,128)(2,1)} %bitcast.51), channel_id=1, source_target_pairs={{0,1},{1,0},{2,3},{3,2},{4,5},{5,4},{6,7},{7,6},{8,9},{9,8},{10,11... | collective-permute-start | bytes 1572872 | tf_op jit(solution)/shard_map/ppermute | solution.py:340
  4.0 6.9 %all-to-all-start = ((bf16[16,128,128]{2,1,0:T(8,128)(2,1)}), bf16[16,128,128]{2,1,0:T(8,128)(2,1)S(1)}, u32[]{:S(2)}, u32[]{:S(2)}) async-start(bf16[16,128,128]{2,1,0:T(8,128)(2,1)} %bitcast.50), calls=%async_computation | async-start | bytes 1048576 | tf_op jit(solution)/shard_map/all_to_all | solution.py:325
  10.8 0.9 %dynamic-slice_bitcast_fusion.1 = (bf16[1,128,128]{2,1,0:T(8,128)(2,1)S(1)}, bf16[1,128,128]{2,1,0:T(8,128)(2,1)S(1)}, bf16[1,128,128]{2,1,0:T(8,128)(2,1)S(1)},...) fusion(bf16[8,2,128,128]{3,2,1,0:T(8,128)(2,1)} %bitcast.52, ...), kind=kLoop, calls=%fused_computation.9 | loop fusion | bytes 524324 | tf_op jit(solution)/shard_map/squeeze | solution.py:342
  11.7 0.0 collective-permute-done
  11.8 5.4 %collective-permute-start.1 = (bf16[2,128,128]{2,1,0:T(8,128)(2,1)S(1)}, bf16[2,128,128]{2,1,0:T(8,128)(2,1)S(1)}, u32[]{:S(2)}, u32[]{:S(2)}) collective-permute-start(bf16[2,128,128]{2,1,0:T(8,128)(2,1)S(1)} %pad_maximum_fusion.1), channel_id=1, source_target_pairs={{0,8},{1,9},{2,10},{3,11},{4,12},{5,13},{6,14},{7,15},{8,0},{9,1},... | collective-permute-start | bytes 196616 | tf_op jit(solution)/shard_map/ppermute | solution.py:347
  17.2 0.4 collective-permute-start.2
  17.6 4.3 %collective-permute-start.3 = (bf16[2,128,128]{2,1,0:T(8,128)(2,1)S(1)}, bf16[2,128,128]{2,1,0:T(8,128)(2,1)S(1)}, u32[]{:S(2)}, u32[]{:S(2)}) collective-permute-start(bf16[2,128,128]{2,1,0:T(8,128)(2,1)S(1)} %pad_maximum_fusion.3), channel_id=1, source_target_pairs={{0,10},{1,11},{2,12},{3,13},{4,14},{5,15},{6,0},{7,1},{8,2},{9,3},... | collective-permute-start | bytes 196616 | tf_op jit(solution)/shard_map/ppermute | solution.py:347
  21.8 0.4 collective-permute-start.4
  22.2 3.4 %collective-permute-start.5 = (bf16[2,128,128]{2,1,0:T(8,128)(2,1)S(1)}, bf16[2,128,128]{2,1,0:T(8,128)(2,1)S(1)}, u32[]{:S(2)}, u32[]{:S(2)}) collective-permute-start(bf16[2,128,128]{2,1,0:T(8,128)(2,1)S(1)} %pad_maximum_fusion.5), channel_id=1, source_target_pairs={{0,12},{1,13},{2,14},{3,15},{4,0},{5,1},{6,2},{7,3},{8,4},{9,5},{1... | collective-permute-start | bytes 196616 | tf_op jit(solution)/shard_map/ppermute | solution.py:347
  25.6 1.6 %all-to-all-done.moved_ref = bf16[16,128,128]{2,1,0:T(8,128)(2,1)S(1)} async-done(((bf16[16,128,128]{2,1,0:T(8,128)(2,1)}), bf16[16,128,128]{2,1,0:T(8,128)(2,1)S(1)}, u32[]{:S(2)}, u32[]{:S(2)}) %all-to-all-start) | async-done | bytes 524320 | tf_op jit(solution)/shard_map/all_to_all | solution.py:325
  27.2 0.0 copy-done
  27.2 2.2 %block_ends.1 = (f32[2048,128]{1,0:T(8,128)S(1)}, f32[256,128]{1,0:T(8,128)S(1)}, f32[16,16,128]{2,1,0:T(8,128)}) custom-call(bf16[16,128,128]{2,1,0:T(8,128)(2,1)S(1)} %all-to-all-done.moved_ref, f32[16,128]{1,0:T(8,128)S(1)} %bitcast.41), custom_call_target="tpu_custom_call" | custom-call | flops 8388608 | bytes 1048576 | tf_op jit(solution)/shard_map/block_ends/pallas_call | solution.py:369
  29.4 6.8 %all-to-all-start.1 = ((f32[16,16,128]{2,1,0:T(8,128)}), f32[16,16,128]{2,1,0:T(8,128)S(1)}, u32[]{:S(2)}, u32[]{:S(2)}) async-start(f32[16,16,128]{2,1,0:T(8,128)} %get-tuple-element.11), calls=%async_computation.1 | async-start | bytes 262144 | tf_op jit(solution)/shard_map/all_to_all | solution.py:325
  36.2 0.0 collective-permute-done.1.refs_1_
  36.2 0.1 collective-permute-start.6
  36.3 0.0 collective-permute-done.2.refs_2_
  36.3 2.7 %collective-permute-start.7 = (bf16[2,128,128]{2,1,0:T(8,128)(2,1)S(1)}, bf16[2,128,128]{2,1,0:T(8,128)(2,1)S(1)}, u32[]{:S(2)}, u32[]{:S(2)}) collective-permute-start(bf16[2,128,128]{2,1,0:T(8,128)(2,1)S(1)} %pad_maximum_fusion.7), channel_id=1, source_target_pairs={{0,14},{1,15},{2,0},{3,1},{4,2},{5,3},{6,4},{7,5},{8,6},{9,7},{10,... | collective-permute-start | bytes 196616 | tf_op jit(solution)/shard_map/ppermute | solution.py:347
  39.0 3.1 %weighted.1 = (f32[4096,128]{1,0:T(8,128)S(1)}, f32[4096,128]{1,0:T(8,128)S(1)}, f32[256,128]{1,0:T(8,128)S(1)}) custom-call(f32[2048,128]{1,0:T(8,128)S(1)} %get-tuple-element.12.gt_ref.refs_8_, f32[16,128]{1,0:T(8,128)S(1)} %bitcast.42), custom_call_target="tpu_custom_call" | custom-call | flops 16777216 | bytes 1048576 | tf_op jit(solution)/shard_map/weighted/pallas_call | solution.py:379
  42.0 0.0 collective-permute-done.3.refs_3_
  42.0 0.0 collective-permute-done.4.refs_4_
  42.0 0.0 collective-permute-done.5.refs_5_
  42.0 0.0 collective-permute-done.6.refs_6_
  42.1 0.0 collective-permute-done.7.refs_7_
  42.1 0.0 copy-start.1
  42.1 4.3 %mode_sums.1._.refs_0_ = f32[80,128]{1,0:T(8,128)S(1)} custom-call(bf16[2,128,128]{2,1,0:T(8,128)(2,1)S(1)} %pad_maximum_fusion.refs_0_, bf16[2,128,128]{2,1,0:T(8,128)(2,1)S(1)} %collective-permute-done.1.refs_1_, bf16[2,128,128]{2,1,0:T(8,128)(2,1)S(1)} %collective-permute-done.2.refs_2_, bf16[2,128,128]{2,1,0:T(8,128)(2,1)S(1)} %collective-permute-done.3.refs_3_, ...), custom_call_target="tpu_custom_call" | custom-call | flops 33554432 | bytes 1048576 | tf_op jit(solution)/shard_map/mode_sums/pallas_call | solution.py:387
  46.3 0.0 all-to-all-done.1.heads_ref.refs_4_
  46.3 0.0 copy-done.1
  46.4 3.5 %input_grad.1 = bf16[16,128,128]{2,1,0:T(8,128)(2,1)} custom-call(f32[16,16,128]{2,1,0:T(8,128)S(1)} %all-to-all-done.1.heads_ref.refs_4_, f32[2048,128]{1,0:T(8,128)S(1)} %get-tuple-element.12.gt_ref.refs_8_, f32[16,128]{1,0:T(8,128)S(1)} %bitcast.44, f32[16,128]{1,0:T(8,128)S(1)} %bitcast.47, f32[256,128]{1,0:T(8,128)S(1)} %get-tuple-element.13.refs_12_.h_ref, ...), custom_call_target="tpu_custom_call" | custom-call | flops 16777216 | bytes 1048576 | tf_op jit(solution)/shard_map/input_grad/pallas_call | solution.py:396
  49.9 6.7 %all-to-all-start.2 = ((bf16[16,128,128]{2,1,0:T(8,128)(2,1)}), bf16[16,128,128]{2,1,0:T(8,128)(2,1)S(1)}, u32[]{:S(2)}, u32[]{:S(2)}) async-start(bf16[16,128,128]{2,1,0:T(8,128)(2,1)} %input_grad.1), calls=%async_computation.2 | async-start | bytes 1048576 | tf_op jit(solution)/shard_map/all_to_all | solution.py:325
  56.6 2.7 %collective-permute-start.10 = (f32[80,128]{1,0:T(8,128)S(1)}, f32[80,128]{1,0:T(8,128)S(1)}, u32[]{:S(2)}, u32[]{:S(2)}) collective-permute-start(f32[80,128]{1,0:T(8,128)S(1)} %mode_sums.1._.refs_0_), channel_id=1, source_target_pairs={{0,48},{16,0},{32,16},{48,32},{64,112},{80,64},{96,80},{112,96},{1... | collective-permute-start | bytes 122888 | tf_op jit(solution)/shard_map/ppermute | solution.py:332
  59.3 0.6 collective-permute-start.9
  59.9 0.6 collective-permute-start.8
  60.4 0.0 collective-permute-done.10.refs_3_
  60.4 3.2 %collective-permute-done.9.refs_2_ = f32[80,128]{1,0:T(8,128)S(1)} collective-permute-done((f32[80,128]{1,0:T(8,128)S(1)}, f32[80,128]{1,0:T(8,128)S(1)}, u32[]{:S(2)}, u32[]{:S(2)}) %collective-permute-start.9) | collective-permute-done | bytes 40992 | tf_op jit(solution)/shard_map/ppermute | solution.py:332
  63.7 0.7 collective-permute-done.8.refs_1_
  64.4 0.1 join.1.refs_0_
  64.4 2.5 %collective-permute-start.13 = (f32[80,128]{1,0:T(8,128)S(1)}, f32[80,128]{1,0:T(8,128)S(1)}, u32[]{:S(2)}, u32[]{:S(2)}) collective-permute-start(f32[80,128]{1,0:T(8,128)S(1)} %join.1.refs_0_), channel_id=1, source_target_pairs={{0,192},{16,208},{32,224},{48,240},{64,0},{80,16},{96,32},{112,48}... | collective-permute-start | bytes 122888 | tf_op jit(solution)/shard_map/ppermute | solution.py:332
  66.9 0.6 collective-permute-start.12
  67.5 0.6 collective-permute-start.11
  68.1 0.0 collective-permute-done.13.refs_3_
  68.1 3.5 %collective-permute-done.12.refs_2_ = f32[80,128]{1,0:T(8,128)S(1)} collective-permute-done((f32[80,128]{1,0:T(8,128)S(1)}, f32[80,128]{1,0:T(8,128)S(1)}, u32[]{:S(2)}, u32[]{:S(2)}) %collective-permute-start.12) | collective-permute-done | bytes 40992 | tf_op jit(solution)/shard_map/ppermute | solution.py:332
  71.6 0.4 collective-permute-done.11.refs_1_
  72.0 0.7 finish.1
  72.6 1.2 %all-to-all-done.2 = bf16[16,128,128]{2,1,0:T(8,128)(2,1)S(1)} async-done(((bf16[16,128,128]{2,1,0:T(8,128)(2,1)}), bf16[16,128,128]{2,1,0:T(8,128)(2,1)S(1)}, u32[]{:S(2)}, u32[]{:S(2)}) %all-to-all-start.2) | async-done | bytes 524320 | tf_op jit(solution)/shard_map/all_to_all | solution.py:325
  73.9 0.8 %copy.8 = bf16[2048,128]{1,0:T(8,128)(2,1)} copy(bf16[2048,128]{1,0:T(8,128)(2,1)S(1)} %bitcast.49) | data formatting | bytes 1048576
  (9 shorter events, 0.1 us)
Async XLA Ops:
  0.6 26.6 %copy-start = (f32[128,16]{0,1:T(8,128)S(1)}, f32[128,16]{0,1:T(8,128)}, u32[]{:S(2)}) copy-start(f32[128,16]{0,1:T(8,128)} %param.6) | copy-start | bytes 24580
  0.6 11.1 %collective-permute-start = (bf16[16,128,128]{2,1,0:T(8,128)(2,1)}, bf16[16,128,128]{2,1,0:T(8,128)(2,1)S(1)}, u32[]{:S(2)}, u32[]{:S(2)}) collective-permute-start(bf16[16,128,128]{2,1,0:T(8,128)(2,1)} %bitcast.51), channel_id=1, source_target_pairs={{0,1},{1,0},{2,3},{3,2},{4,5},{5,4},{6,7},{7,6},{8,9},{9,8},{10,11... | collective-permute-start | bytes 1572872 | tf_op jit(solution)/shard_map/ppermute | solution.py:340
  4.0 23.2 %all-to-all-start = ((bf16[16,128,128]{2,1,0:T(8,128)(2,1)}), bf16[16,128,128]{2,1,0:T(8,128)(2,1)S(1)}, u32[]{:S(2)}, u32[]{:S(2)}) async-start(bf16[16,128,128]{2,1,0:T(8,128)(2,1)} %bitcast.50), calls=%async_computation | async-start | bytes 1048576 | tf_op jit(solution)/shard_map/all_to_all | solution.py:325
  11.8 24.4 %collective-permute-start.1 = (bf16[2,128,128]{2,1,0:T(8,128)(2,1)S(1)}, bf16[2,128,128]{2,1,0:T(8,128)(2,1)S(1)}, u32[]{:S(2)}, u32[]{:S(2)}) collective-permute-start(bf16[2,128,128]{2,1,0:T(8,128)(2,1)S(1)} %pad_maximum_fusion.1), channel_id=1, source_target_pairs={{0,8},{1,9},{2,10},{3,11},{4,12},{5,13},{6,14},{7,15},{8,0},{9,1},... | collective-permute-start | bytes 196616 | tf_op jit(solution)/shard_map/ppermute | solution.py:347
  17.2 19.1 %collective-permute-start.2 = (bf16[2,128,128]{2,1,0:T(8,128)(2,1)S(1)}, bf16[2,128,128]{2,1,0:T(8,128)(2,1)S(1)}, u32[]{:S(2)}, u32[]{:S(2)}) collective-permute-start(bf16[2,128,128]{2,1,0:T(8,128)(2,1)S(1)} %pad_maximum_fusion.2), channel_id=1, source_target_pairs={{0,6},{1,7},{2,8},{3,9},{4,10},{5,11},{6,12},{7,13},{8,14},{9,15},... | collective-permute-start | bytes 196616 | tf_op jit(solution)/shard_map/ppermute | solution.py:347
  17.6 24.5 %collective-permute-start.3 = (bf16[2,128,128]{2,1,0:T(8,128)(2,1)S(1)}, bf16[2,128,128]{2,1,0:T(8,128)(2,1)S(1)}, u32[]{:S(2)}, u32[]{:S(2)}) collective-permute-start(bf16[2,128,128]{2,1,0:T(8,128)(2,1)S(1)} %pad_maximum_fusion.3), channel_id=1, source_target_pairs={{0,10},{1,11},{2,12},{3,13},{4,14},{5,15},{6,0},{7,1},{8,2},{9,3},... | collective-permute-start | bytes 196616 | tf_op jit(solution)/shard_map/ppermute | solution.py:347
  21.8 20.2 %collective-permute-start.4 = (bf16[2,128,128]{2,1,0:T(8,128)(2,1)S(1)}, bf16[2,128,128]{2,1,0:T(8,128)(2,1)S(1)}, u32[]{:S(2)}, u32[]{:S(2)}) collective-permute-start(bf16[2,128,128]{2,1,0:T(8,128)(2,1)S(1)} %pad_maximum_fusion.4), channel_id=1, source_target_pairs={{0,4},{1,5},{2,6},{3,7},{4,8},{5,9},{6,10},{7,11},{8,12},{9,13},{1... | collective-permute-start | bytes 196616 | tf_op jit(solution)/shard_map/ppermute | solution.py:347
  22.2 19.9 %collective-permute-start.5 = (bf16[2,128,128]{2,1,0:T(8,128)(2,1)S(1)}, bf16[2,128,128]{2,1,0:T(8,128)(2,1)S(1)}, u32[]{:S(2)}, u32[]{:S(2)}) collective-permute-start(bf16[2,128,128]{2,1,0:T(8,128)(2,1)S(1)} %pad_maximum_fusion.5), channel_id=1, source_target_pairs={{0,12},{1,13},{2,14},{3,15},{4,0},{5,1},{6,2},{7,3},{8,4},{9,5},{1... | collective-permute-start | bytes 196616 | tf_op jit(solution)/shard_map/ppermute | solution.py:347
  29.4 16.9 %all-to-all-start.1 = ((f32[16,16,128]{2,1,0:T(8,128)}), f32[16,16,128]{2,1,0:T(8,128)S(1)}, u32[]{:S(2)}, u32[]{:S(2)}) async-start(f32[16,16,128]{2,1,0:T(8,128)} %get-tuple-element.11), calls=%async_computation.1 | async-start | bytes 262144 | tf_op jit(solution)/shard_map/all_to_all | solution.py:325
  36.2 5.9 %collective-permute-start.6 = (bf16[2,128,128]{2,1,0:T(8,128)(2,1)S(1)}, bf16[2,128,128]{2,1,0:T(8,128)(2,1)S(1)}, u32[]{:S(2)}, u32[]{:S(2)}) collective-permute-start(bf16[2,128,128]{2,1,0:T(8,128)(2,1)S(1)} %pad_maximum_fusion.6), channel_id=1, source_target_pairs={{0,2},{1,3},{2,4},{3,5},{4,6},{5,7},{6,8},{7,9},{8,10},{9,11},{10,... | collective-permute-start | bytes 196616 | tf_op jit(solution)/shard_map/ppermute | solution.py:347
  36.3 5.8 %collective-permute-start.7 = (bf16[2,128,128]{2,1,0:T(8,128)(2,1)S(1)}, bf16[2,128,128]{2,1,0:T(8,128)(2,1)S(1)}, u32[]{:S(2)}, u32[]{:S(2)}) collective-permute-start(bf16[2,128,128]{2,1,0:T(8,128)(2,1)S(1)} %pad_maximum_fusion.7), channel_id=1, source_target_pairs={{0,14},{1,15},{2,0},{3,1},{4,2},{5,3},{6,4},{7,5},{8,6},{9,7},{10,... | collective-permute-start | bytes 196616 | tf_op jit(solution)/shard_map/ppermute | solution.py:347
  42.1 4.3 %copy-start.1 = (f32[128,16]{0,1:T(8,128)S(1)}, f32[128,16]{0,1:T(8,128)}, u32[]{:S(2)}) copy-start(f32[128,16]{0,1:T(8,128)} %param.7) | copy-start | bytes 24580
  49.9 24.0 %all-to-all-start.2 = ((bf16[16,128,128]{2,1,0:T(8,128)(2,1)}), bf16[16,128,128]{2,1,0:T(8,128)(2,1)S(1)}, u32[]{:S(2)}, u32[]{:S(2)}) async-start(bf16[16,128,128]{2,1,0:T(8,128)(2,1)} %input_grad.1), calls=%async_computation.2 | async-start | bytes 1048576 | tf_op jit(solution)/shard_map/all_to_all | solution.py:325
  56.6 3.9 %collective-permute-start.10 = (f32[80,128]{1,0:T(8,128)S(1)}, f32[80,128]{1,0:T(8,128)S(1)}, u32[]{:S(2)}, u32[]{:S(2)}) collective-permute-start(f32[80,128]{1,0:T(8,128)S(1)} %mode_sums.1._.refs_0_), channel_id=1, source_target_pairs={{0,48},{16,0},{32,16},{48,32},{64,112},{80,64},{96,80},{112,96},{1... | collective-permute-start | bytes 122888 | tf_op jit(solution)/shard_map/ppermute | solution.py:332
  59.3 4.4 %collective-permute-start.9 = (f32[80,128]{1,0:T(8,128)S(1)}, f32[80,128]{1,0:T(8,128)S(1)}, u32[]{:S(2)}, u32[]{:S(2)}) collective-permute-start(f32[80,128]{1,0:T(8,128)S(1)} %mode_sums.1._.refs_0_), channel_id=1, source_target_pairs={{0,32},{16,48},{32,0},{48,16},{64,96},{80,112},{96,64},{112,80},{1... | collective-permute-start | bytes 122888 | tf_op jit(solution)/shard_map/ppermute | solution.py:332
  59.9 4.5 %collective-permute-start.8 = (f32[80,128]{1,0:T(8,128)S(1)}, f32[80,128]{1,0:T(8,128)S(1)}, u32[]{:S(2)}, u32[]{:S(2)}) collective-permute-start(f32[80,128]{1,0:T(8,128)S(1)} %mode_sums.1._.refs_0_), channel_id=1, source_target_pairs={{0,16},{16,32},{32,48},{48,0},{64,80},{80,96},{96,112},{112,64},{1... | collective-permute-start | bytes 122888 | tf_op jit(solution)/shard_map/ppermute | solution.py:332
  64.4 3.6 %collective-permute-start.13 = (f32[80,128]{1,0:T(8,128)S(1)}, f32[80,128]{1,0:T(8,128)S(1)}, u32[]{:S(2)}, u32[]{:S(2)}) collective-permute-start(f32[80,128]{1,0:T(8,128)S(1)} %join.1.refs_0_), channel_id=1, source_target_pairs={{0,192},{16,208},{32,224},{48,240},{64,0},{80,16},{96,32},{112,48}... | collective-permute-start | bytes 122888 | tf_op jit(solution)/shard_map/ppermute | solution.py:332
  66.9 4.7 %collective-permute-start.12 = (f32[80,128]{1,0:T(8,128)S(1)}, f32[80,128]{1,0:T(8,128)S(1)}, u32[]{:S(2)}, u32[]{:S(2)}) collective-permute-start(f32[80,128]{1,0:T(8,128)S(1)} %join.1.refs_0_), channel_id=1, source_target_pairs={{0,128},{16,144},{32,160},{48,176},{64,192},{80,208},{96,224},{112... | collective-permute-start | bytes 122888 | tf_op jit(solution)/shard_map/ppermute | solution.py:332
  67.5 4.5 %collective-permute-start.11 = (f32[80,128]{1,0:T(8,128)S(1)}, f32[80,128]{1,0:T(8,128)S(1)}, u32[]{:S(2)}, u32[]{:S(2)}) collective-permute-start(f32[80,128]{1,0:T(8,128)S(1)} %join.1.refs_0_), channel_id=1, source_target_pairs={{0,64},{16,80},{32,96},{48,112},{64,128},{80,144},{96,160},{112,17... | collective-permute-start | bytes 122888 | tf_op jit(solution)/shard_map/ppermute | solution.py:332

commit v6 on v5

--- a/solution.py
+++ b/solution.py
@@ -42,8 +42,12 @@
 
 
 def step_rows(ref, j, blocks, half):
-    at = lambda i: pl.multiple_of((j * STEP + i) * blocks + half * ROWS, ROWS)
-    return [ref[pl.ds(at(i), ROWS), :] for i in range(STEP)]
+    if ref.dtype == F32:
+        at = lambda i: pl.multiple_of((j * STEP + i) * blocks + half * ROWS, ROWS)
+        return [ref[pl.ds(at(i), ROWS), :] for i in range(STEP)]
+    at = lambda i: pl.multiple_of((j * STEP + i) * blocks, blocks)
+    rows = slice(half * ROWS, (half + 1) * ROWS)
+    return [ref[pl.ds(at(i), blocks), :].astype(F32)[rows, :] for i in range(STEP)]
 
 
 def slot(j, blocks, half, modes, p):
@@ -61,11 +65,12 @@
         ref[at : at + ROWS, :] = row
 
 
-def ends_kernel(blocks, spans, moved_ref, lam_ref, gt_ref, h_ref, head_ref):
+def ends_kernel(blocks, spans, moved_ref, lam_ref, gt_ref, h_ref, head_ref, wide_ref):
     modes = lam_ref.shape[0]
     block_len = moved_ref.shape[2]
     steps = block_len // STEP
-    flip_blocks(moved_ref, gt_ref)
+    flip_blocks(moved_ref, wide_ref)
+    gt_ref[...] = wide_ref[...].astype(jnp.bfloat16)
     lam = lam_ref[...]
     rate = log_rates(lam)
     wide = wide_rows(lam, 0, modes)
@@ -75,7 +80,7 @@
 
         def back(i, held):
             j = steps - 1 - i
-            g = step_rows(gt_ref, j, blocks, half)
+            g = step_rows(wide_ref, j, blocks, half)
             sums = [horner(l, g) for l in wide]
             return tuple(l * a + h for l, a, h in zip(jump, held, sums))
 
@@ -132,36 +137,50 @@
 
 
 def input_grad_kernel(
-    blocks, spans, heads_ref, gt_ref, lam_ref, res_ref, h_ref, _, out_ref, next_ref, flat_ref
+    blocks, spans, heads_ref, gt_ref, sub_ref, lam_ref, res_ref, h_ref, _, out_ref, next_ref, flat_ref
 ):
-    modes, chans = lam_ref.shape
+    modes = lam_ref.shape[0]
     block_len = gt_ref.shape[0] // blocks
-    rate = log_rates(lam_ref[...])
+    steps = block_len // STEP
+    lam = lam_ref[...]
+    res = res_ref[...]
+    rate = log_rates(lam)
     block_step = jnp.exp(block_len * rate)
     span_step = jnp.exp((blocks * block_len) * rate)
     total = folded_after(span_step, [heads_ref[i] for i in range(spans)], lax.axis_index("len"))
     for n in range(blocks - 1, -1, -1):
         next_ref[pl.ds(n, modes, stride=blocks), :] = total
         total = block_step * total + block_rows(h_ref, n, blocks, modes)
+    taps, power = [], res
+    for _ in range(STEP):
+        taps.append(jnp.broadcast_to(jnp.sum(power, axis=0, keepdims=True), (ROWS, lam.shape[1])))
+        power = power * lam
+    wide = wide_rows(lam, 0, modes)
+    jump = wide_rows(jnp.exp(STEP * rate), 0, modes)
+    gain = wide_rows(res, 0, modes)
     for half in range(blocks // ROWS):
-        wide = wide_rows(lam_ref[...], 0, modes)
-        gain = wide_rows(res_ref[...], 0, modes)
         start = tuple(
             next_ref[p * blocks + half * ROWS : p * blocks + half * ROWS + ROWS, :]
             for p in range(modes)
         )
 
-        def step(i, held):
-            at = pl.multiple_of((block_len - 1 - i) * blocks + half * ROWS, ROWS)
-            g = gt_ref[pl.ds(at, ROWS), :]
-            held = tuple(l * a + g for l, a in zip(wide, held))
-            terms = [r * a for r, a in zip(gain, held)]
-            while len(terms) > 1:
-                terms = [a + b for a, b in zip(terms[::2], terms[1::2])]
-            flat_ref[pl.ds(at, ROWS), :] = terms[0]
-            return held
-
-        lax.fori_loop(0, block_len, step, start, unroll=8)
+        def back(i, held):
+            j = steps - 1 - i
+            g = step_rows(gt_ref, j, blocks, half)
+            outs = [sum(taps[k] * g[at + k] for k in range(STEP - at)) for at in range(STEP)]
+            after = []
+            for p in range(modes):
+                term = gain[p] * held[p]
+                for at in range(STEP - 1, -1, -1):
+                    term = wide[p] * term
+                    outs[at] = outs[at] + term
+                after.append(jump[p] * held[p] + sub_ref[slot(j, blocks, half, modes, p), :])
+            for at in range(STEP):
+                rows = pl.multiple_of((j * STEP + at) * blocks + half * ROWS, ROWS)
+                flat_ref[pl.ds(rows, ROWS), :] = outs[at]
+            return tuple(after)
+
+        lax.fori_loop(0, steps, back, start, unroll=4)
     for n in range(blocks):
         out_ref[n] = flat_ref[pl.ds(n, block_len, stride=blocks), :].T.astype(jnp.bfloat16)
 
@@ -368,9 +387,13 @@
     pieces = moved_pieces(cut(inputs), blocks, shifts)
     flat_grads, ends, head = call(
         functools.partial(ends_kernel, blocks, spans),
-        (shape(flat, chans), shape(held, chans), shape(spans, modes, chans)),
+        (
+            jax.ShapeDtypeStruct((flat, chans), jnp.bfloat16),
+            shape(held, chans),
+            shape(spans, modes, chans),
+        ),
         2,
-        [],
+        [scratch(flat, chans)],
         "block_ends",
         2 * work,
     )(moved_grads, poles)
@@ -396,11 +419,11 @@
     rounded = call(
         functools.partial(input_grad_kernel, blocks, spans),
         jax.ShapeDtypeStruct((blocks, chans, block_len), jnp.bfloat16),
-        6,
+        7,
         [scratch(held, chans), scratch(flat, chans)],
         "input_grad",
         4 * work,
-    )(heads, flat_grads, poles, residues, ends, pay)
+    )(heads, flat_grads, sub_heads, poles, residues, ends, pay)
     input_grad = swap(rounded, "chan").reshape(blocks * chans, block_len)
     group_pay = call(
         functools.partial(join_kernel, flat),

time: 75.2 us -> 74.9 us (level)
  no operation moved by 1% of the time
where the time goes in v6:
time: 74.9 us; the launch traced here: 74.4 us
  starting transfers between devices  47.7 us (64%)
  Pallas kernels  13.4 us (18%)
  waiting for transfers between devices  10.7 us (14%)
  local copies, waits for them, and re-layouts  1.74 us (2%)
  between operations  0.79 us (1%)
    all_to_all x3, starting transfers between devices, swap(): return lax.all_to_all(part, axis, split_axis=0, concat_axis=0, tiled=True)  20.4 us
    ppermute x7, starting transfers between devices, moved_pieces(): return [at(0)] + [lax.ppermute(at(s), 'chan', ring(s)) for s in shifts]  16.5 us
    ppermute x6, waiting for transfers between devices, rotated(): lax.ppermute(part, 'len', [(i, hop(i, s)) for i in range(spans)])  7.87 us
    ppermute x6, starting transfers between devices, rotated(): lax.ppermute(part, 'len', [(i, hop(i, s)) for i in range(spans)])  7.55 us
    pallas_call x1, Pallas kernels, body(): call(functools.partial(sums_kernel, blocks, shifts), shape(5 * modes, cha...  4.29 us
    ppermute x1, starting transfers between devices, moved_pieces(): got = lax.ppermute(part, 'chan', [(i, i ^ 1) for i in range(blocks)])  3.33 us
    pallas_call x1, Pallas kernels, body(): call(functools.partial(weighted_kernel, blocks), (subs, subs, shape(held,...  3.13 us
    pallas_call x1, Pallas kernels, body(): call(functools.partial(input_grad_kernel, blocks, spans), jax.ShapeDtypeS...  3.04 us
  transfers between devices with their start and end apart: 17, of which 6 were waited for; matrix products, arithmetic and copies ran while one was open for 1% of the time, Pallas kernels for 14%

profile of v6, /device:TPU:1, one launch (start us, length us, event | category | flops | bytes accessed | tf_op | source)
XLA Modules:
  0.0 74.4 jit_solution(2396640004561582432)
XLA Ops:
  0.6 0.0 copy-start
  0.6 3.3 %collective-permute-start = (bf16[16,128,128]{2,1,0:T(8,128)(2,1)}, bf16[16,128,128]{2,1,0:T(8,128)(2,1)S(1)}, u32[]{:S(2)}, u32[]{:S(2)}) collective-permute-start(bf16[16,128,128]{2,1,0:T(8,128)(2,1)} %bitcast.51), channel_id=1, source_target_pairs={{0,1},{1,0},{2,3},{3,2},{4,5},{5,4},{6,7},{7,6},{8,9},{9,8},{10,11... | collective-permute-start | bytes 1572872 | tf_op jit(solution)/shard_map/ppermute | solution.py:359
  4.0 6.9 %all-to-all-start = ((bf16[16,128,128]{2,1,0:T(8,128)(2,1)}), bf16[16,128,128]{2,1,0:T(8,128)(2,1)S(1)}, u32[]{:S(2)}, u32[]{:S(2)}) async-start(bf16[16,128,128]{2,1,0:T(8,128)(2,1)} %bitcast.50), calls=%async_computation | async-start | bytes 1048576 | tf_op jit(solution)/shard_map/all_to_all | solution.py:344
  10.8 0.9 %dynamic-slice_bitcast_fusion.1 = (bf16[1,128,128]{2,1,0:T(8,128)(2,1)S(1)}, bf16[1,128,128]{2,1,0:T(8,128)(2,1)S(1)}, bf16[1,128,128]{2,1,0:T(8,128)(2,1)S(1)},...) fusion(bf16[8,2,128,128]{3,2,1,0:T(8,128)(2,1)} %bitcast.52, ...), kind=kLoop, calls=%fused_computation.9 | loop fusion | bytes 524324 | tf_op jit(solution)/shard_map/squeeze | solution.py:361
  11.7 0.0 collective-permute-done
  11.8 5.4 %collective-permute-start.1 = (bf16[2,128,128]{2,1,0:T(8,128)(2,1)S(1)}, bf16[2,128,128]{2,1,0:T(8,128)(2,1)S(1)}, u32[]{:S(2)}, u32[]{:S(2)}) collective-permute-start(bf16[2,128,128]{2,1,0:T(8,128)(2,1)S(1)} %pad_maximum_fusion.1), channel_id=1, source_target_pairs={{0,8},{1,9},{2,10},{3,11},{4,12},{5,13},{6,14},{7,15},{8,0},{9,1},... | collective-permute-start | bytes 196616 | tf_op jit(solution)/shard_map/ppermute | solution.py:366
  17.2 0.4 collective-permute-start.2
  17.6 4.3 %collective-permute-start.3 = (bf16[2,128,128]{2,1,0:T(8,128)(2,1)S(1)}, bf16[2,128,128]{2,1,0:T(8,128)(2,1)S(1)}, u32[]{:S(2)}, u32[]{:S(2)}) collective-permute-start(bf16[2,128,128]{2,1,0:T(8,128)(2,1)S(1)} %pad_maximum_fusion.3), channel_id=1, source_target_pairs={{0,10},{1,11},{2,12},{3,13},{4,14},{5,15},{6,0},{7,1},{8,2},{9,3},... | collective-permute-start | bytes 196616 | tf_op jit(solution)/shard_map/ppermute | solution.py:366
  21.8 0.4 collective-permute-start.4
  22.2 3.4 %collective-permute-start.5 = (bf16[2,128,128]{2,1,0:T(8,128)(2,1)S(1)}, bf16[2,128,128]{2,1,0:T(8,128)(2,1)S(1)}, u32[]{:S(2)}, u32[]{:S(2)}) collective-permute-start(bf16[2,128,128]{2,1,0:T(8,128)(2,1)S(1)} %pad_maximum_fusion.5), channel_id=1, source_target_pairs={{0,12},{1,13},{2,14},{3,15},{4,0},{5,1},{6,2},{7,3},{8,4},{9,5},{1... | collective-permute-start | bytes 196616 | tf_op jit(solution)/shard_map/ppermute | solution.py:366
  25.6 1.6 %all-to-all-done.moved_ref = bf16[16,128,128]{2,1,0:T(8,128)(2,1)S(1)} async-done(((bf16[16,128,128]{2,1,0:T(8,128)(2,1)}), bf16[16,128,128]{2,1,0:T(8,128)(2,1)S(1)}, u32[]{:S(2)}, u32[]{:S(2)}) %all-to-all-start) | async-done | bytes 524320 | tf_op jit(solution)/shard_map/all_to_all | solution.py:344
  27.2 0.0 copy-done
  27.2 2.2 %block_ends.1 = (bf16[2048,128]{1,0:T(8,128)(2,1)S(1)}, f32[256,128]{1,0:T(8,128)S(1)}, f32[16,16,128]{2,1,0:T(8,128)}) custom-call(bf16[16,128,128]{2,1,0:T(8,128)(2,1)S(1)} %all-to-all-done.moved_ref, f32[16,128]{1,0:T(8,128)S(1)} %bitcast.41), custom_call_target="tpu_custom_call" | custom-call | flops 8388608 | bytes 1048576 | tf_op jit(solution)/shard_map/block_ends/pallas_call | solution.py:388
  29.4 6.8 %all-to-all-start.1 = ((f32[16,16,128]{2,1,0:T(8,128)}), f32[16,16,128]{2,1,0:T(8,128)S(1)}, u32[]{:S(2)}, u32[]{:S(2)}) async-start(f32[16,16,128]{2,1,0:T(8,128)} %get-tuple-element.11), calls=%async_computation.1 | async-start | bytes 262144 | tf_op jit(solution)/shard_map/all_to_all | solution.py:344
  36.2 0.0 collective-permute-done.1.refs_1_
  36.2 0.1 collective-permute-start.6
  36.3 0.0 collective-permute-done.2.refs_2_
  36.3 2.7 %collective-permute-start.7 = (bf16[2,128,128]{2,1,0:T(8,128)(2,1)S(1)}, bf16[2,128,128]{2,1,0:T(8,128)(2,1)S(1)}, u32[]{:S(2)}, u32[]{:S(2)}) collective-permute-start(bf16[2,128,128]{2,1,0:T(8,128)(2,1)S(1)} %pad_maximum_fusion.7), channel_id=1, source_target_pairs={{0,14},{1,15},{2,0},{3,1},{4,2},{5,3},{6,4},{7,5},{8,6},{9,7},{10,... | collective-permute-start | bytes 196616 | tf_op jit(solution)/shard_map/ppermute | solution.py:366
  39.0 3.1 %weighted.1 = (f32[4096,128]{1,0:T(8,128)S(1)}, f32[4096,128]{1,0:T(8,128)S(1)}, f32[256,128]{1,0:T(8,128)S(1)}) custom-call(bf16[2048,128]{1,0:T(8,128)(2,1)S(1)} %get-tuple-element.12.gt_ref.refs_8_, f32[16,128]{1,0:T(8,128)S(1)} %bitcast.42), custom_call_target="tpu_custom_call" | custom-call | flops 16777216 | bytes 1048576 | tf_op jit(solution)/shard_map/weighted/pallas_call | solution.py:402
  42.1 0.0 collective-permute-done.3.refs_3_
  42.1 0.0 collective-permute-done.4.refs_4_
  42.1 0.0 collective-permute-done.5.refs_5_
  42.1 0.0 collective-permute-done.6.refs_6_
  42.1 0.0 collective-permute-done.7.refs_7_
  42.2 0.0 copy-start.1
  42.2 4.3 %mode_sums.1._.refs_0_ = f32[80,128]{1,0:T(8,128)S(1)} custom-call(bf16[2,128,128]{2,1,0:T(8,128)(2,1)S(1)} %pad_maximum_fusion.refs_0_, bf16[2,128,128]{2,1,0:T(8,128)(2,1)S(1)} %collective-permute-done.1.refs_1_, bf16[2,128,128]{2,1,0:T(8,128)(2,1)S(1)} %collective-permute-done.2.refs_2_, bf16[2,128,128]{2,1,0:T(8,128)(2,1)S(1)} %collective-permute-done.3.refs_3_, ...), custom_call_target="tpu_custom_call" | custom-call | flops 33554432 | bytes 1048576 | tf_op jit(solution)/shard_map/mode_sums/pallas_call | solution.py:410
  46.5 0.0 all-to-all-done.1.heads_ref.refs_4_
  46.5 0.0 copy-done.1
  46.5 3.0 %input_grad.1 = bf16[16,128,128]{2,1,0:T(8,128)(2,1)} custom-call(f32[16,16,128]{2,1,0:T(8,128)S(1)} %all-to-all-done.1.heads_ref.refs_4_, bf16[2048,128]{1,0:T(8,128)(2,1)S(1)} %get-tuple-element.12.gt_ref.refs_8_, f32[4096,128]{1,0:T(8,128)S(1)} %get-tuple-element.13.refs_9_.sub_ref, f32[16,128]{1,0:T(8,128)S(1)} %bitcast.44, f32[16,128]{1,0:T(8,128)S(1)} %bitcast.47, ...), custom_call_target="tpu_custom_call" | custom-call | flops 16777216 | bytes 1048576 | tf_op jit(solution)/shard_map/input_grad/pallas_call | solution.py:419
  49.5 6.8 %all-to-all-start.2 = ((bf16[16,128,128]{2,1,0:T(8,128)(2,1)}), bf16[16,128,128]{2,1,0:T(8,128)(2,1)S(1)}, u32[]{:S(2)}, u32[]{:S(2)}) async-start(bf16[16,128,128]{2,1,0:T(8,128)(2,1)} %input_grad.1), calls=%async_computation.2 | async-start | bytes 1048576 | tf_op jit(solution)/shard_map/all_to_all | solution.py:344
  56.3 2.8 %collective-permute-start.10 = (f32[80,128]{1,0:T(8,128)S(1)}, f32[80,128]{1,0:T(8,128)S(1)}, u32[]{:S(2)}, u32[]{:S(2)}) collective-permute-start(f32[80,128]{1,0:T(8,128)S(1)} %mode_sums.1._.refs_0_), channel_id=1, source_target_pairs={{0,48},{16,0},{32,16},{48,32},{64,112},{80,64},{96,80},{112,96},{1... | collective-permute-start | bytes 122888 | tf_op jit(solution)/shard_map/ppermute | solution.py:351
  59.1 0.6 collective-permute-start.9
  59.6 0.6 collective-permute-start.8
  60.2 0.0 collective-permute-done.10.refs_3_
  60.2 3.2 %collective-permute-done.9.refs_2_ = f32[80,128]{1,0:T(8,128)S(1)} collective-permute-done((f32[80,128]{1,0:T(8,128)S(1)}, f32[80,128]{1,0:T(8,128)S(1)}, u32[]{:S(2)}, u32[]{:S(2)}) %collective-permute-start.9) | collective-permute-done | bytes 40992 | tf_op jit(solution)/shard_map/ppermute | solution.py:351
  63.4 0.7 collective-permute-done.8.refs_1_
  64.2 0.1 join.1.refs_0_
  64.2 2.5 %collective-permute-start.13 = (f32[80,128]{1,0:T(8,128)S(1)}, f32[80,128]{1,0:T(8,128)S(1)}, u32[]{:S(2)}, u32[]{:S(2)}) collective-permute-start(f32[80,128]{1,0:T(8,128)S(1)} %join.1.refs_0_), channel_id=1, source_target_pairs={{0,192},{16,208},{32,224},{48,240},{64,0},{80,16},{96,32},{112,48}... | collective-permute-start | bytes 122888 | tf_op jit(solution)/shard_map/ppermute | solution.py:351
  66.7 0.6 collective-permute-start.12
  67.3 0.6 collective-permute-start.11
  67.8 0.0 collective-permute-done.13.refs_3_
  67.8 3.5 %collective-permute-done.12.refs_2_ = f32[80,128]{1,0:T(8,128)S(1)} collective-permute-done((f32[80,128]{1,0:T(8,128)S(1)}, f32[80,128]{1,0:T(8,128)S(1)}, u32[]{:S(2)}, u32[]{:S(2)}) %collective-permute-start.12) | collective-permute-done | bytes 40992 | tf_op jit(solution)/shard_map/ppermute | solution.py:351
  71.3 0.4 collective-permute-done.11.refs_1_
  71.8 0.7 finish.1
  72.4 1.2 %all-to-all-done.2 = bf16[16,128,128]{2,1,0:T(8,128)(2,1)S(1)} async-done(((bf16[16,128,128]{2,1,0:T(8,128)(2,1)}), bf16[16,128,128]{2,1,0:T(8,128)(2,1)S(1)}, u32[]{:S(2)}, u32[]{:S(2)}) %all-to-all-start.2) | async-done | bytes 524320 | tf_op jit(solution)/shard_map/all_to_all | solution.py:344
  73.6 0.8 %copy.8 = bf16[2048,128]{1,0:T(8,128)(2,1)} copy(bf16[2048,128]{1,0:T(8,128)(2,1)S(1)} %bitcast.49) | data formatting | bytes 1048576
  (9 shorter events, 0.1 us)
Async XLA Ops:
  0.6 26.6 %copy-start = (f32[128,16]{0,1:T(8,128)S(1)}, f32[128,16]{0,1:T(8,128)}, u32[]{:S(2)}) copy-start(f32[128,16]{0,1:T(8,128)} %param.6) | copy-start | bytes 24580
  0.6 11.1 %collective-permute-start = (bf16[16,128,128]{2,1,0:T(8,128)(2,1)}, bf16[16,128,128]{2,1,0:T(8,128)(2,1)S(1)}, u32[]{:S(2)}, u32[]{:S(2)}) collective-permute-start(bf16[16,128,128]{2,1,0:T(8,128)(2,1)} %bitcast.51), channel_id=1, source_target_pairs={{0,1},{1,0},{2,3},{3,2},{4,5},{5,4},{6,7},{7,6},{8,9},{9,8},{10,11... | collective-permute-start | bytes 1572872 | tf_op jit(solution)/shard_map/ppermute | solution.py:359
  4.0 23.2 %all-to-all-start = ((bf16[16,128,128]{2,1,0:T(8,128)(2,1)}), bf16[16,128,128]{2,1,0:T(8,128)(2,1)S(1)}, u32[]{:S(2)}, u32[]{:S(2)}) async-start(bf16[16,128,128]{2,1,0:T(8,128)(2,1)} %bitcast.50), calls=%async_computation | async-start | bytes 1048576 | tf_op jit(solution)/shard_map/all_to_all | solution.py:344
  11.8 24.4 %collective-permute-start.1 = (bf16[2,128,128]{2,1,0:T(8,128)(2,1)S(1)}, bf16[2,128,128]{2,1,0:T(8,128)(2,1)S(1)}, u32[]{:S(2)}, u32[]{:S(2)}) collective-permute-start(bf16[2,128,128]{2,1,0:T(8,128)(2,1)S(1)} %pad_maximum_fusion.1), channel_id=1, source_target_pairs={{0,8},{1,9},{2,10},{3,11},{4,12},{5,13},{6,14},{7,15},{8,0},{9,1},... | collective-permute-start | bytes 196616 | tf_op jit(solution)/shard_map/ppermute | solution.py:366
  17.2 19.1 %collective-permute-start.2 = (bf16[2,128,128]{2,1,0:T(8,128)(2,1)S(1)}, bf16[2,128,128]{2,1,0:T(8,128)(2,1)S(1)}, u32[]{:S(2)}, u32[]{:S(2)}) collective-permute-start(bf16[2,128,128]{2,1,0:T(8,128)(2,1)S(1)} %pad_maximum_fusion.2), channel_id=1, source_target_pairs={{0,6},{1,7},{2,8},{3,9},{4,10},{5,11},{6,12},{7,13},{8,14},{9,15},... | collective-permute-start | bytes 196616 | tf_op jit(solution)/shard_map/ppermute | solution.py:366
  17.6 24.6 %collective-permute-start.3 = (bf16[2,128,128]{2,1,0:T(8,128)(2,1)S(1)}, bf16[2,128,128]{2,1,0:T(8,128)(2,1)S(1)}, u32[]{:S(2)}, u32[]{:S(2)}) collective-permute-start(bf16[2,128,128]{2,1,0:T(8,128)(2,1)S(1)} %pad_maximum_fusion.3), channel_id=1, source_target_pairs={{0,10},{1,11},{2,12},{3,13},{4,14},{5,15},{6,0},{7,1},{8,2},{9,3},... | collective-permute-start | bytes 196616 | tf_op jit(solution)/shard_map/ppermute | solution.py:366
  21.8 20.3 %collective-permute-start.4 = (bf16[2,128,128]{2,1,0:T(8,128)(2,1)S(1)}, bf16[2,128,128]{2,1,0:T(8,128)(2,1)S(1)}, u32[]{:S(2)}, u32[]{:S(2)}) collective-permute-start(bf16[2,128,128]{2,1,0:T(8,128)(2,1)S(1)} %pad_maximum_fusion.4), channel_id=1, source_target_pairs={{0,4},{1,5},{2,6},{3,7},{4,8},{5,9},{6,10},{7,11},{8,12},{9,13},{1... | collective-permute-start | bytes 196616 | tf_op jit(solution)/shard_map/ppermute | solution.py:366
  22.2 19.9 %collective-permute-start.5 = (bf16[2,128,128]{2,1,0:T(8,128)(2,1)S(1)}, bf16[2,128,128]{2,1,0:T(8,128)(2,1)S(1)}, u32[]{:S(2)}, u32[]{:S(2)}) collective-permute-start(bf16[2,128,128]{2,1,0:T(8,128)(2,1)S(1)} %pad_maximum_fusion.5), channel_id=1, source_target_pairs={{0,12},{1,13},{2,14},{3,15},{4,0},{5,1},{6,2},{7,3},{8,4},{9,5},{1... | collective-permute-start | bytes 196616 | tf_op jit(solution)/shard_map/ppermute | solution.py:366
  29.4 17.0 %all-to-all-start.1 = ((f32[16,16,128]{2,1,0:T(8,128)}), f32[16,16,128]{2,1,0:T(8,128)S(1)}, u32[]{:S(2)}, u32[]{:S(2)}) async-start(f32[16,16,128]{2,1,0:T(8,128)} %get-tuple-element.11), calls=%async_computation.1 | async-start | bytes 262144 | tf_op jit(solution)/shard_map/all_to_all | solution.py:344
  36.2 5.9 %collective-permute-start.6 = (bf16[2,128,128]{2,1,0:T(8,128)(2,1)S(1)}, bf16[2,128,128]{2,1,0:T(8,128)(2,1)S(1)}, u32[]{:S(2)}, u32[]{:S(2)}) collective-permute-start(bf16[2,128,128]{2,1,0:T(8,128)(2,1)S(1)} %pad_maximum_fusion.6), channel_id=1, source_target_pairs={{0,2},{1,3},{2,4},{3,5},{4,6},{5,7},{6,8},{7,9},{8,10},{9,11},{10,... | collective-permute-start | bytes 196616 | tf_op jit(solution)/shard_map/ppermute | solution.py:366
  36.3 5.8 %collective-permute-start.7 = (bf16[2,128,128]{2,1,0:T(8,128)(2,1)S(1)}, bf16[2,128,128]{2,1,0:T(8,128)(2,1)S(1)}, u32[]{:S(2)}, u32[]{:S(2)}) collective-permute-start(bf16[2,128,128]{2,1,0:T(8,128)(2,1)S(1)} %pad_maximum_fusion.7), channel_id=1, source_target_pairs={{0,14},{1,15},{2,0},{3,1},{4,2},{5,3},{6,4},{7,5},{8,6},{9,7},{10,... | collective-permute-start | bytes 196616 | tf_op jit(solution)/shard_map/ppermute | solution.py:366
  42.2 4.3 %copy-start.1 = (f32[128,16]{0,1:T(8,128)S(1)}, f32[128,16]{0,1:T(8,128)}, u32[]{:S(2)}) copy-start(f32[128,16]{0,1:T(8,128)} %param.7) | copy-start | bytes 24580
  49.5 24.1 %all-to-all-start.2 = ((bf16[16,128,128]{2,1,0:T(8,128)(2,1)}), bf16[16,128,128]{2,1,0:T(8,128)(2,1)S(1)}, u32[]{:S(2)}, u32[]{:S(2)}) async-start(bf16[16,128,128]{2,1,0:T(8,128)(2,1)} %input_grad.1), calls=%async_computation.2 | async-start | bytes 1048576 | tf_op jit(solution)/shard_map/all_to_all | solution.py:344
  56.3 3.9 %collective-permute-start.10 = (f32[80,128]{1,0:T(8,128)S(1)}, f32[80,128]{1,0:T(8,128)S(1)}, u32[]{:S(2)}, u32[]{:S(2)}) collective-permute-start(f32[80,128]{1,0:T(8,128)S(1)} %mode_sums.1._.refs_0_), channel_id=1, source_target_pairs={{0,48},{16,0},{32,16},{48,32},{64,112},{80,64},{96,80},{112,96},{1... | collective-permute-start | bytes 122888 | tf_op jit(solution)/shard_map/ppermute | solution.py:351
  59.1 4.4 %collective-permute-start.9 = (f32[80,128]{1,0:T(8,128)S(1)}, f32[80,128]{1,0:T(8,128)S(1)}, u32[]{:S(2)}, u32[]{:S(2)}) collective-permute-start(f32[80,128]{1,0:T(8,128)S(1)} %mode_sums.1._.refs_0_), channel_id=1, source_target_pairs={{0,32},{16,48},{32,0},{48,16},{64,96},{80,112},{96,64},{112,80},{1... | collective-permute-start | bytes 122888 | tf_op jit(solution)/shard_map/ppermute | solution.py:351
  59.6 4.5 %collective-permute-start.8 = (f32[80,128]{1,0:T(8,128)S(1)}, f32[80,128]{1,0:T(8,128)S(1)}, u32[]{:S(2)}, u32[]{:S(2)}) collective-permute-start(f32[80,128]{1,0:T(8,128)S(1)} %mode_sums.1._.refs_0_), channel_id=1, source_target_pairs={{0,16},{16,32},{32,48},{48,0},{64,80},{80,96},{96,112},{112,64},{1... | collective-permute-start | bytes 122888 | tf_op jit(solution)/shard_map/ppermute | solution.py:351
  64.2 3.6 %collective-permute-start.13 = (f32[80,128]{1,0:T(8,128)S(1)}, f32[80,128]{1,0:T(8,128)S(1)}, u32[]{:S(2)}, u32[]{:S(2)}) collective-permute-start(f32[80,128]{1,0:T(8,128)S(1)} %join.1.refs_0_), channel_id=1, source_target_pairs={{0,192},{16,208},{32,224},{48,240},{64,0},{80,16},{96,32},{112,48}... | collective-permute-start | bytes 122888 | tf_op jit(solution)/shard_map/ppermute | solution.py:351
  66.7 4.7 %collective-permute-start.12 = (f32[80,128]{1,0:T(8,128)S(1)}, f32[80,128]{1,0:T(8,128)S(1)}, u32[]{:S(2)}, u32[]{:S(2)}) collective-permute-start(f32[80,128]{1,0:T(8,128)S(1)} %join.1.refs_0_), channel_id=1, source_target_pairs={{0,128},{16,144},{32,160},{48,176},{64,192},{80,208},{96,224},{112... | collective-permute-start | bytes 122888 | tf_op jit(solution)/shard_map/ppermute | solution.py:351
  67.3 4.5 %collective-permute-start.11 = (f32[80,128]{1,0:T(8,128)S(1)}, f32[80,128]{1,0:T(8,128)S(1)}, u32[]{:S(2)}, u32[]{:S(2)}) collective-permute-start(f32[80,128]{1,0:T(8,128)S(1)} %join.1.refs_0_), channel_id=1, source_target_pairs={{0,64},{16,80},{32,96},{48,112},{64,128},{80,144},{96,160},{112,17... | collective-permute-start | bytes 122888 | tf_op jit(solution)/shard_map/ppermute | solution.py:351

commit v7 on v6

--- a/solution.py
+++ b/solution.py
@@ -103,10 +103,10 @@
     steps = gt_ref.shape[0] // blocks // STEP
     lam = lam_ref[...]
     jumps = jnp.exp(STEP * log_rates(lam))
-    empty = cleared(t_ref, GROUP)
-    for first in range(0, modes, GROUP):
-        wide = wide_rows(lam, first, GROUP)
-        jump = wide_rows(jumps, first, GROUP)
+    empty = cleared(t_ref, modes)
+    for first in range(0, modes, modes):
+        wide = wide_rows(lam, first, modes)
+        jump = wide_rows(jumps, first, modes)
         for half in range(blocks // ROWS):
 
             def back(i, held):
@@ -115,7 +115,7 @@
                 scaled = [(k + 1.0) * row for k, row in enumerate(g)]
                 adjoint, weighted = held
                 after, total = [], []
-                for k in range(GROUP):
+                for k in range(modes):
                     rows = slot(j, blocks, half, modes, first + k)
                     head = horner(wide[k], g)
                     part = horner(wide[k], scaled)
@@ -125,7 +125,7 @@
                     after.append(jump[k] * adjoint[k] + head)
                 return (tuple(after), tuple(total))
 
-            weighted = lax.fori_loop(0, steps, back, (empty,) * 2, unroll=4)[1]
+            weighted = lax.fori_loop(0, steps, back, (empty,) * 2, unroll=2)[1]
             put(t_ref, blocks, half, first, weighted)
 
 

time: 74.9 us -> 74.7 us (level)
  no operation moved by 1% of the time
where the time goes in v7:
time: 74.7 us; the launch traced here: 74.2 us
  starting transfers between devices  47.6 us (64%)
  Pallas kernels  13.3 us (18%)
  waiting for transfers between devices  10.8 us (14%)
  local copies, waits for them, and re-layouts  1.74 us (2%)
  between operations  0.8 us (1%)
    all_to_all x3, starting transfers between devices, swap(): return lax.all_to_all(part, axis, split_axis=0, concat_axis=0, tiled=True)  20.3 us
    ppermute x7, starting transfers between devices, moved_pieces(): return [at(0)] + [lax.ppermute(at(s), 'chan', ring(s)) for s in shifts]  16.5 us
    ppermute x6, waiting for transfers between devices, rotated(): lax.ppermute(part, 'len', [(i, hop(i, s)) for i in range(spans)])  7.87 us
    ppermute x6, starting transfers between devices, rotated(): lax.ppermute(part, 'len', [(i, hop(i, s)) for i in range(spans)])  7.49 us
    pallas_call x1, Pallas kernels, body(): call(functools.partial(sums_kernel, blocks, shifts), shape(5 * modes, cha...  4.29 us
    ppermute x1, starting transfers between devices, moved_pieces(): got = lax.ppermute(part, 'chan', [(i, i ^ 1) for i in range(blocks)])  3.33 us
    pallas_call x1, Pallas kernels, body(): call(functools.partial(weighted_kernel, blocks), (subs, subs, shape(held,...  3.06 us
    pallas_call x1, Pallas kernels, body(): call(functools.partial(input_grad_kernel, blocks, spans), jax.ShapeDtypeS...  3.04 us
  transfers between devices with their start and end apart: 17, of which 6 were waited for; matrix products, arithmetic and copies ran while one was open for 1% of the time, Pallas kernels for 14%

profile of v7, /device:TPU:1, one launch (start us, length us, event | category | flops | bytes accessed | tf_op | source)
XLA Modules:
  0.0 74.2 jit_solution(6877981497169010436)
XLA Ops:
  0.6 0.0 copy-start
  0.6 3.3 %collective-permute-start = (bf16[16,128,128]{2,1,0:T(8,128)(2,1)}, bf16[16,128,128]{2,1,0:T(8,128)(2,1)S(1)}, u32[]{:S(2)}, u32[]{:S(2)}) collective-permute-start(bf16[16,128,128]{2,1,0:T(8,128)(2,1)} %bitcast.51), channel_id=1, source_target_pairs={{0,1},{1,0},{2,3},{3,2},{4,5},{5,4},{6,7},{7,6},{8,9},{9,8},{10,11... | collective-permute-start | bytes 1572872 | tf_op jit(solution)/shard_map/ppermute | solution.py:359
  4.0 6.9 %all-to-all-start = ((bf16[16,128,128]{2,1,0:T(8,128)(2,1)}), bf16[16,128,128]{2,1,0:T(8,128)(2,1)S(1)}, u32[]{:S(2)}, u32[]{:S(2)}) async-start(bf16[16,128,128]{2,1,0:T(8,128)(2,1)} %bitcast.50), calls=%async_computation | async-start | bytes 1048576 | tf_op jit(solution)/shard_map/all_to_all | solution.py:344
  10.8 0.9 %dynamic-slice_bitcast_fusion.1 = (bf16[1,128,128]{2,1,0:T(8,128)(2,1)S(1)}, bf16[1,128,128]{2,1,0:T(8,128)(2,1)S(1)}, bf16[1,128,128]{2,1,0:T(8,128)(2,1)S(1)},...) fusion(bf16[8,2,128,128]{3,2,1,0:T(8,128)(2,1)} %bitcast.52, ...), kind=kLoop, calls=%fused_computation.9 | loop fusion | bytes 524324 | tf_op jit(solution)/shard_map/squeeze | solution.py:361
  11.7 0.0 collective-permute-done
  11.8 5.4 %collective-permute-start.1 = (bf16[2,128,128]{2,1,0:T(8,128)(2,1)S(1)}, bf16[2,128,128]{2,1,0:T(8,128)(2,1)S(1)}, u32[]{:S(2)}, u32[]{:S(2)}) collective-permute-start(bf16[2,128,128]{2,1,0:T(8,128)(2,1)S(1)} %pad_maximum_fusion.1), channel_id=1, source_target_pairs={{0,8},{1,9},{2,10},{3,11},{4,12},{5,13},{6,14},{7,15},{8,0},{9,1},... | collective-permute-start | bytes 196616 | tf_op jit(solution)/shard_map/ppermute | solution.py:366
  17.2 0.4 collective-permute-start.2
  17.6 4.3 %collective-permute-start.3 = (bf16[2,128,128]{2,1,0:T(8,128)(2,1)S(1)}, bf16[2,128,128]{2,1,0:T(8,128)(2,1)S(1)}, u32[]{:S(2)}, u32[]{:S(2)}) collective-permute-start(bf16[2,128,128]{2,1,0:T(8,128)(2,1)S(1)} %pad_maximum_fusion.3), channel_id=1, source_target_pairs={{0,10},{1,11},{2,12},{3,13},{4,14},{5,15},{6,0},{7,1},{8,2},{9,3},... | collective-permute-start | bytes 196616 | tf_op jit(solution)/shard_map/ppermute | solution.py:366
  21.8 0.4 collective-permute-start.4
  22.2 3.4 %collective-permute-start.5 = (bf16[2,128,128]{2,1,0:T(8,128)(2,1)S(1)}, bf16[2,128,128]{2,1,0:T(8,128)(2,1)S(1)}, u32[]{:S(2)}, u32[]{:S(2)}) collective-permute-start(bf16[2,128,128]{2,1,0:T(8,128)(2,1)S(1)} %pad_maximum_fusion.5), channel_id=1, source_target_pairs={{0,12},{1,13},{2,14},{3,15},{4,0},{5,1},{6,2},{7,3},{8,4},{9,5},{1... | collective-permute-start | bytes 196616 | tf_op jit(solution)/shard_map/ppermute | solution.py:366
  25.6 1.6 %all-to-all-done.moved_ref = bf16[16,128,128]{2,1,0:T(8,128)(2,1)S(1)} async-done(((bf16[16,128,128]{2,1,0:T(8,128)(2,1)}), bf16[16,128,128]{2,1,0:T(8,128)(2,1)S(1)}, u32[]{:S(2)}, u32[]{:S(2)}) %all-to-all-start) | async-done | bytes 524320 | tf_op jit(solution)/shard_map/all_to_all | solution.py:344
  27.2 0.0 copy-done
  27.2 2.2 %block_ends.1 = (bf16[2048,128]{1,0:T(8,128)(2,1)S(1)}, f32[256,128]{1,0:T(8,128)S(1)}, f32[16,16,128]{2,1,0:T(8,128)}) custom-call(bf16[16,128,128]{2,1,0:T(8,128)(2,1)S(1)} %all-to-all-done.moved_ref, f32[16,128]{1,0:T(8,128)S(1)} %bitcast.41), custom_call_target="tpu_custom_call" | custom-call | flops 8388608 | bytes 1048576 | tf_op jit(solution)/shard_map/block_ends/pallas_call | solution.py:388
  29.4 6.8 %all-to-all-start.1 = ((f32[16,16,128]{2,1,0:T(8,128)}), f32[16,16,128]{2,1,0:T(8,128)S(1)}, u32[]{:S(2)}, u32[]{:S(2)}) async-start(f32[16,16,128]{2,1,0:T(8,128)} %get-tuple-element.11), calls=%async_computation.1 | async-start | bytes 262144 | tf_op jit(solution)/shard_map/all_to_all | solution.py:344
  36.2 0.0 collective-permute-done.1.refs_1_
  36.2 0.1 collective-permute-start.6
  36.3 0.0 collective-permute-done.2.refs_2_
  36.3 2.7 %collective-permute-start.7 = (bf16[2,128,128]{2,1,0:T(8,128)(2,1)S(1)}, bf16[2,128,128]{2,1,0:T(8,128)(2,1)S(1)}, u32[]{:S(2)}, u32[]{:S(2)}) collective-permute-start(bf16[2,128,128]{2,1,0:T(8,128)(2,1)S(1)} %pad_maximum_fusion.7), channel_id=1, source_target_pairs={{0,14},{1,15},{2,0},{3,1},{4,2},{5,3},{6,4},{7,5},{8,6},{9,7},{10,... | collective-permute-start | bytes 196616 | tf_op jit(solution)/shard_map/ppermute | solution.py:366
  39.0 3.1 %weighted.1 = (f32[4096,128]{1,0:T(8,128)S(1)}, f32[4096,128]{1,0:T(8,128)S(1)}, f32[256,128]{1,0:T(8,128)S(1)}) custom-call(bf16[2048,128]{1,0:T(8,128)(2,1)S(1)} %get-tuple-element.12.gt_ref.refs_8_, f32[16,128]{1,0:T(8,128)S(1)} %bitcast.42), custom_call_target="tpu_custom_call" | custom-call | flops 16777216 | bytes 1048576 | tf_op jit(solution)/shard_map/weighted/pallas_call | solution.py:402
  42.0 0.0 collective-permute-done.3.refs_3_
  42.0 0.0 collective-permute-done.4.refs_4_
  42.1 0.0 collective-permute-done.5.refs_5_
  42.1 0.0 collective-permute-done.6.refs_6_
  42.1 0.0 collective-permute-done.7.refs_7_
  42.1 0.0 copy-start.1
  42.1 4.3 %mode_sums.1._.refs_0_ = f32[80,128]{1,0:T(8,128)S(1)} custom-call(bf16[2,128,128]{2,1,0:T(8,128)(2,1)S(1)} %pad_maximum_fusion.refs_0_, bf16[2,128,128]{2,1,0:T(8,128)(2,1)S(1)} %collective-permute-done.1.refs_1_, bf16[2,128,128]{2,1,0:T(8,128)(2,1)S(1)} %collective-permute-done.2.refs_2_, bf16[2,128,128]{2,1,0:T(8,128)(2,1)S(1)} %collective-permute-done.3.refs_3_, ...), custom_call_target="tpu_custom_call" | custom-call | flops 33554432 | bytes 1048576 | tf_op jit(solution)/shard_map/mode_sums/pallas_call | solution.py:410
  46.4 0.0 all-to-all-done.1.heads_ref.refs_4_
  46.4 0.0 copy-done.1
  46.4 3.0 %input_grad.1 = bf16[16,128,128]{2,1,0:T(8,128)(2,1)} custom-call(f32[16,16,128]{2,1,0:T(8,128)S(1)} %all-to-all-done.1.heads_ref.refs_4_, bf16[2048,128]{1,0:T(8,128)(2,1)S(1)} %get-tuple-element.12.gt_ref.refs_8_, f32[4096,128]{1,0:T(8,128)S(1)} %get-tuple-element.13.refs_9_.sub_ref, f32[16,128]{1,0:T(8,128)S(1)} %bitcast.44, f32[16,128]{1,0:T(8,128)S(1)} %bitcast.47, ...), custom_call_target="tpu_custom_call" | custom-call | flops 16777216 | bytes 1048576 | tf_op jit(solution)/shard_map/input_grad/pallas_call | solution.py:419
  49.4 6.7 %all-to-all-start.2 = ((bf16[16,128,128]{2,1,0:T(8,128)(2,1)}), bf16[16,128,128]{2,1,0:T(8,128)(2,1)S(1)}, u32[]{:S(2)}, u32[]{:S(2)}) async-start(bf16[16,128,128]{2,1,0:T(8,128)(2,1)} %input_grad.1), calls=%async_computation.2 | async-start | bytes 1048576 | tf_op jit(solution)/shard_map/all_to_all | solution.py:344
  56.1 2.7 %collective-permute-start.10 = (f32[80,128]{1,0:T(8,128)S(1)}, f32[80,128]{1,0:T(8,128)S(1)}, u32[]{:S(2)}, u32[]{:S(2)}) collective-permute-start(f32[80,128]{1,0:T(8,128)S(1)} %mode_sums.1._.refs_0_), channel_id=1, source_target_pairs={{0,48},{16,0},{32,16},{48,32},{64,112},{80,64},{96,80},{112,96},{1... | collective-permute-start | bytes 122888 | tf_op jit(solution)/shard_map/ppermute | solution.py:351
  58.8 0.6 collective-permute-start.9
  59.4 0.6 collective-permute-start.8
  60.0 0.0 collective-permute-done.10.refs_3_
  60.0 3.2 %collective-permute-done.9.refs_2_ = f32[80,128]{1,0:T(8,128)S(1)} collective-permute-done((f32[80,128]{1,0:T(8,128)S(1)}, f32[80,128]{1,0:T(8,128)S(1)}, u32[]{:S(2)}, u32[]{:S(2)}) %collective-permute-start.9) | collective-permute-done | bytes 40992 | tf_op jit(solution)/shard_map/ppermute | solution.py:351
  63.2 0.7 collective-permute-done.8.refs_1_
  63.9 0.1 join.1.refs_0_
  64.0 2.5 %collective-permute-start.13 = (f32[80,128]{1,0:T(8,128)S(1)}, f32[80,128]{1,0:T(8,128)S(1)}, u32[]{:S(2)}, u32[]{:S(2)}) collective-permute-start(f32[80,128]{1,0:T(8,128)S(1)} %join.1.refs_0_), channel_id=1, source_target_pairs={{0,192},{16,208},{32,224},{48,240},{64,0},{80,16},{96,32},{112,48}... | collective-permute-start | bytes 122888 | tf_op jit(solution)/shard_map/ppermute | solution.py:351
  66.4 0.6 collective-permute-start.12
  67.0 0.6 collective-permute-start.11
  67.6 0.0 collective-permute-done.13.refs_3_
  67.6 3.5 %collective-permute-done.12.refs_2_ = f32[80,128]{1,0:T(8,128)S(1)} collective-permute-done((f32[80,128]{1,0:T(8,128)S(1)}, f32[80,128]{1,0:T(8,128)S(1)}, u32[]{:S(2)}, u32[]{:S(2)}) %collective-permute-start.12) | collective-permute-done | bytes 40992 | tf_op jit(solution)/shard_map/ppermute | solution.py:351
  71.1 0.4 collective-permute-done.11.refs_1_
  71.5 0.7 finish.1
  72.2 1.2 %all-to-all-done.2 = bf16[16,128,128]{2,1,0:T(8,128)(2,1)S(1)} async-done(((bf16[16,128,128]{2,1,0:T(8,128)(2,1)}), bf16[16,128,128]{2,1,0:T(8,128)(2,1)S(1)}, u32[]{:S(2)}, u32[]{:S(2)}) %all-to-all-start.2) | async-done | bytes 524320 | tf_op jit(solution)/shard_map/all_to_all | solution.py:344
  73.4 0.8 %copy.8 = bf16[2048,128]{1,0:T(8,128)(2,1)} copy(bf16[2048,128]{1,0:T(8,128)(2,1)S(1)} %bitcast.49) | data formatting | bytes 1048576
  (9 shorter events, 0.1 us)
Async XLA Ops:
  0.6 26.6 %copy-start = (f32[128,16]{0,1:T(8,128)S(1)}, f32[128,16]{0,1:T(8,128)}, u32[]{:S(2)}) copy-start(f32[128,16]{0,1:T(8,128)} %param.6) | copy-start | bytes 24580
  0.6 11.1 %collective-permute-start = (bf16[16,128,128]{2,1,0:T(8,128)(2,1)}, bf16[16,128,128]{2,1,0:T(8,128)(2,1)S(1)}, u32[]{:S(2)}, u32[]{:S(2)}) collective-permute-start(bf16[16,128,128]{2,1,0:T(8,128)(2,1)} %bitcast.51), channel_id=1, source_target_pairs={{0,1},{1,0},{2,3},{3,2},{4,5},{5,4},{6,7},{7,6},{8,9},{9,8},{10,11... | collective-permute-start | bytes 1572872 | tf_op jit(solution)/shard_map/ppermute | solution.py:359
  4.0 23.2 %all-to-all-start = ((bf16[16,128,128]{2,1,0:T(8,128)(2,1)}), bf16[16,128,128]{2,1,0:T(8,128)(2,1)S(1)}, u32[]{:S(2)}, u32[]{:S(2)}) async-start(bf16[16,128,128]{2,1,0:T(8,128)(2,1)} %bitcast.50), calls=%async_computation | async-start | bytes 1048576 | tf_op jit(solution)/shard_map/all_to_all | solution.py:344
  11.8 24.4 %collective-permute-start.1 = (bf16[2,128,128]{2,1,0:T(8,128)(2,1)S(1)}, bf16[2,128,128]{2,1,0:T(8,128)(2,1)S(1)}, u32[]{:S(2)}, u32[]{:S(2)}) collective-permute-start(bf16[2,128,128]{2,1,0:T(8,128)(2,1)S(1)} %pad_maximum_fusion.1), channel_id=1, source_target_pairs={{0,8},{1,9},{2,10},{3,11},{4,12},{5,13},{6,14},{7,15},{8,0},{9,1},... | collective-permute-start | bytes 196616 | tf_op jit(solution)/shard_map/ppermute | solution.py:366
  17.2 19.1 %collective-permute-start.2 = (bf16[2,128,128]{2,1,0:T(8,128)(2,1)S(1)}, bf16[2,128,128]{2,1,0:T(8,128)(2,1)S(1)}, u32[]{:S(2)}, u32[]{:S(2)}) collective-permute-start(bf16[2,128,128]{2,1,0:T(8,128)(2,1)S(1)} %pad_maximum_fusion.2), channel_id=1, source_target_pairs={{0,6},{1,7},{2,8},{3,9},{4,10},{5,11},{6,12},{7,13},{8,14},{9,15},... | collective-permute-start | bytes 196616 | tf_op jit(solution)/shard_map/ppermute | solution.py:366
  17.6 24.5 %collective-permute-start.3 = (bf16[2,128,128]{2,1,0:T(8,128)(2,1)S(1)}, bf16[2,128,128]{2,1,0:T(8,128)(2,1)S(1)}, u32[]{:S(2)}, u32[]{:S(2)}) collective-permute-start(bf16[2,128,128]{2,1,0:T(8,128)(2,1)S(1)} %pad_maximum_fusion.3), channel_id=1, source_target_pairs={{0,10},{1,11},{2,12},{3,13},{4,14},{5,15},{6,0},{7,1},{8,2},{9,3},... | collective-permute-start | bytes 196616 | tf_op jit(solution)/shard_map/ppermute | solution.py:366
  21.8 20.2 %collective-permute-start.4 = (bf16[2,128,128]{2,1,0:T(8,128)(2,1)S(1)}, bf16[2,128,128]{2,1,0:T(8,128)(2,1)S(1)}, u32[]{:S(2)}, u32[]{:S(2)}) collective-permute-start(bf16[2,128,128]{2,1,0:T(8,128)(2,1)S(1)} %pad_maximum_fusion.4), channel_id=1, source_target_pairs={{0,4},{1,5},{2,6},{3,7},{4,8},{5,9},{6,10},{7,11},{8,12},{9,13},{1... | collective-permute-start | bytes 196616 | tf_op jit(solution)/shard_map/ppermute | solution.py:366
  22.2 19.9 %collective-permute-start.5 = (bf16[2,128,128]{2,1,0:T(8,128)(2,1)S(1)}, bf16[2,128,128]{2,1,0:T(8,128)(2,1)S(1)}, u32[]{:S(2)}, u32[]{:S(2)}) collective-permute-start(bf16[2,128,128]{2,1,0:T(8,128)(2,1)S(1)} %pad_maximum_fusion.5), channel_id=1, source_target_pairs={{0,12},{1,13},{2,14},{3,15},{4,0},{5,1},{6,2},{7,3},{8,4},{9,5},{1... | collective-permute-start | bytes 196616 | tf_op jit(solution)/shard_map/ppermute | solution.py:366
  29.4 17.0 %all-to-all-start.1 = ((f32[16,16,128]{2,1,0:T(8,128)}), f32[16,16,128]{2,1,0:T(8,128)S(1)}, u32[]{:S(2)}, u32[]{:S(2)}) async-start(f32[16,16,128]{2,1,0:T(8,128)} %get-tuple-element.11), calls=%async_computation.1 | async-start | bytes 262144 | tf_op jit(solution)/shard_map/all_to_all | solution.py:344
  36.2 5.9 %collective-permute-start.6 = (bf16[2,128,128]{2,1,0:T(8,128)(2,1)S(1)}, bf16[2,128,128]{2,1,0:T(8,128)(2,1)S(1)}, u32[]{:S(2)}, u32[]{:S(2)}) collective-permute-start(bf16[2,128,128]{2,1,0:T(8,128)(2,1)S(1)} %pad_maximum_fusion.6), channel_id=1, source_target_pairs={{0,2},{1,3},{2,4},{3,5},{4,6},{5,7},{6,8},{7,9},{8,10},{9,11},{10,... | collective-permute-start | bytes 196616 | tf_op jit(solution)/shard_map/ppermute | solution.py:366
  36.3 5.8 %collective-permute-start.7 = (bf16[2,128,128]{2,1,0:T(8,128)(2,1)S(1)}, bf16[2,128,128]{2,1,0:T(8,128)(2,1)S(1)}, u32[]{:S(2)}, u32[]{:S(2)}) collective-permute-start(bf16[2,128,128]{2,1,0:T(8,128)(2,1)S(1)} %pad_maximum_fusion.7), channel_id=1, source_target_pairs={{0,14},{1,15},{2,0},{3,1},{4,2},{5,3},{6,4},{7,5},{8,6},{9,7},{10,... | collective-permute-start | bytes 196616 | tf_op jit(solution)/shard_map/ppermute | solution.py:366
  42.1 4.3 %copy-start.1 = (f32[128,16]{0,1:T(8,128)S(1)}, f32[128,16]{0,1:T(8,128)}, u32[]{:S(2)}) copy-start(f32[128,16]{0,1:T(8,128)} %param.7) | copy-start | bytes 24580
  49.4 24.0 %all-to-all-start.2 = ((bf16[16,128,128]{2,1,0:T(8,128)(2,1)}), bf16[16,128,128]{2,1,0:T(8,128)(2,1)S(1)}, u32[]{:S(2)}, u32[]{:S(2)}) async-start(bf16[16,128,128]{2,1,0:T(8,128)(2,1)} %input_grad.1), calls=%async_computation.2 | async-start | bytes 1048576 | tf_op jit(solution)/shard_map/all_to_all | solution.py:344
  56.1 3.9 %collective-permute-start.10 = (f32[80,128]{1,0:T(8,128)S(1)}, f32[80,128]{1,0:T(8,128)S(1)}, u32[]{:S(2)}, u32[]{:S(2)}) collective-permute-start(f32[80,128]{1,0:T(8,128)S(1)} %mode_sums.1._.refs_0_), channel_id=1, source_target_pairs={{0,48},{16,0},{32,16},{48,32},{64,112},{80,64},{96,80},{112,96},{1... | collective-permute-start | bytes 122888 | tf_op jit(solution)/shard_map/ppermute | solution.py:351
  58.8 4.4 %collective-permute-start.9 = (f32[80,128]{1,0:T(8,128)S(1)}, f32[80,128]{1,0:T(8,128)S(1)}, u32[]{:S(2)}, u32[]{:S(2)}) collective-permute-start(f32[80,128]{1,0:T(8,128)S(1)} %mode_sums.1._.refs_0_), channel_id=1, source_target_pairs={{0,32},{16,48},{32,0},{48,16},{64,96},{80,112},{96,64},{112,80},{1... | collective-permute-start | bytes 122888 | tf_op jit(solution)/shard_map/ppermute | solution.py:351
  59.4 4.5 %collective-permute-start.8 = (f32[80,128]{1,0:T(8,128)S(1)}, f32[80,128]{1,0:T(8,128)S(1)}, u32[]{:S(2)}, u32[]{:S(2)}) collective-permute-start(f32[80,128]{1,0:T(8,128)S(1)} %mode_sums.1._.refs_0_), channel_id=1, source_target_pairs={{0,16},{16,32},{32,48},{48,0},{64,80},{80,96},{96,112},{112,64},{1... | collective-permute-start | bytes 122888 | tf_op jit(solution)/shard_map/ppermute | solution.py:351
  64.0 3.6 %collective-permute-start.13 = (f32[80,128]{1,0:T(8,128)S(1)}, f32[80,128]{1,0:T(8,128)S(1)}, u32[]{:S(2)}, u32[]{:S(2)}) collective-permute-start(f32[80,128]{1,0:T(8,128)S(1)} %join.1.refs_0_), channel_id=1, source_target_pairs={{0,192},{16,208},{32,224},{48,240},{64,0},{80,16},{96,32},{112,48}... | collective-permute-start | bytes 122888 | tf_op jit(solution)/shard_map/ppermute | solution.py:351
  66.4 4.7 %collective-permute-start.12 = (f32[80,128]{1,0:T(8,128)S(1)}, f32[80,128]{1,0:T(8,128)S(1)}, u32[]{:S(2)}, u32[]{:S(2)}) collective-permute-start(f32[80,128]{1,0:T(8,128)S(1)} %join.1.refs_0_), channel_id=1, source_target_pairs={{0,128},{16,144},{32,160},{48,176},{64,192},{80,208},{96,224},{112... | collective-permute-start | bytes 122888 | tf_op jit(solution)/shard_map/ppermute | solution.py:351
  67.0 4.5 %collective-permute-start.11 = (f32[80,128]{1,0:T(8,128)S(1)}, f32[80,128]{1,0:T(8,128)S(1)}, u32[]{:S(2)}, u32[]{:S(2)}) collective-permute-start(f32[80,128]{1,0:T(8,128)S(1)} %join.1.refs_0_), channel_id=1, source_target_pairs={{0,64},{16,80},{32,96},{48,112},{64,128},{80,144},{96,160},{112,17... | collective-permute-start | bytes 122888 | tf_op jit(solution)/shard_map/ppermute | solution.py:351

commit v8 on v7

--- a/solution.py
+++ b/solution.py
@@ -84,7 +84,7 @@
             sums = [horner(l, g) for l in wide]
             return tuple(l * a + h for l, a, h in zip(jump, held, sums))
 
-        put(h_ref, blocks, half, 0, lax.fori_loop(0, steps, back, empty, unroll=8))
+        put(h_ref, blocks, half, 0, lax.fori_loop(0, steps, back, empty, unroll=16))
     step = jnp.exp(block_len * rate)
     head = folded(step, [block_rows(h_ref, n, blocks, modes) for n in range(blocks)])
     for span in range(spans):
@@ -180,7 +180,7 @@
                 flat_ref[pl.ds(rows, ROWS), :] = outs[at]
             return tuple(after)
 
-        lax.fori_loop(0, steps, back, start, unroll=4)
+        lax.fori_loop(0, steps, back, start, unroll=8)
     for n in range(blocks):
         out_ref[n] = flat_ref[pl.ds(n, block_len, stride=blocks), :].T.astype(jnp.bfloat16)
 
@@ -227,7 +227,7 @@
                 state[k] = jump[k] * state[k] + horner(wide[k], x)
             return (tuple(state), tuple(slope), tuple(res_sum), tuple(pole_sum))
 
-        results = lax.fori_loop(0, steps, ahead, (empty,) * 4, unroll=8)
+        results = lax.fori_loop(0, steps, ahead, (empty,) * 4, unroll=16)
         for ref, result in zip(parts_refs, results):
             put(ref, blocks, half, 0, result)
     block_step = jnp.exp(block_len * rate)

time: 74.7 us -> 74.5 us (level)
  transfers between devices with their start and end apart: 17 -> 17, of which waited for: 6 -> 6; matrix products, arithmetic and copies ran while one was open for 1% -> 1% of each run, Pallas kernels for 14% -> 13%
where the time goes in v8:
time: 74.5 us; the launch traced here: 74 us
  starting transfers between devices  47.6 us (64%)
  Pallas kernels  12.9 us (17%)
  waiting for transfers between devices  10.9 us (15%)
  local copies, waits for them, and re-layouts  1.74 us (2%)
  between operations  0.79 us (1%)
    all_to_all x3, starting transfers between devices, swap(): return lax.all_to_all(part, axis, split_axis=0, concat_axis=0, tiled=True)  20.5 us
    ppermute x7, starting transfers between devices, moved_pieces(): return [at(0)] + [lax.ppermute(at(s), 'chan', ring(s)) for s in shifts]  16.5 us
    ppermute x6, waiting for transfers between devices, rotated(): lax.ppermute(part, 'len', [(i, hop(i, s)) for i in range(spans)])  7.87 us
    ppermute x6, starting transfers between devices, rotated(): lax.ppermute(part, 'len', [(i, hop(i, s)) for i in range(spans)])  7.35 us
    pallas_call x1, Pallas kernels, body(): call(functools.partial(sums_kernel, blocks, shifts), shape(5 * modes, cha...  3.87 us
    ppermute x1, starting transfers between devices, moved_pieces(): got = lax.ppermute(part, 'chan', [(i, i ^ 1) for i in range(blocks)])  3.33 us
    pallas_call x1, Pallas kernels, body(): call(functools.partial(weighted_kernel, blocks), (subs, subs, shape(held,...  3.06 us
    all_to_all x3, waiting for transfers between devices, swap(): return lax.all_to_all(part, axis, split_axis=0, concat_axis=0, tiled=True)  3.02 us
  transfers between devices with their start and end apart: 17, of which 6 were waited for; matrix products, arithmetic and copies ran while one was open for 1% of the time, Pallas kernels for 13%

profile of v8, /device:TPU:1, one launch (start us, length us, event | category | flops | bytes accessed | tf_op | source)
XLA Modules:
  0.0 74.0 jit_solution(15416276846477380742)
XLA Ops:
  0.6 0.0 copy-start
  0.6 3.3 %collective-permute-start = (bf16[16,128,128]{2,1,0:T(8,128)(2,1)}, bf16[16,128,128]{2,1,0:T(8,128)(2,1)S(1)}, u32[]{:S(2)}, u32[]{:S(2)}) collective-permute-start(bf16[16,128,128]{2,1,0:T(8,128)(2,1)} %bitcast.51), channel_id=1, source_target_pairs={{0,1},{1,0},{2,3},{3,2},{4,5},{5,4},{6,7},{7,6},{8,9},{9,8},{10,11... | collective-permute-start | bytes 1572872 | tf_op jit(solution)/shard_map/ppermute | solution.py:359
  4.0 6.9 %all-to-all-start = ((bf16[16,128,128]{2,1,0:T(8,128)(2,1)}), bf16[16,128,128]{2,1,0:T(8,128)(2,1)S(1)}, u32[]{:S(2)}, u32[]{:S(2)}) async-start(bf16[16,128,128]{2,1,0:T(8,128)(2,1)} %bitcast.50), calls=%async_computation | async-start | bytes 1048576 | tf_op jit(solution)/shard_map/all_to_all | solution.py:344
  10.8 0.9 %dynamic-slice_bitcast_fusion.1 = (bf16[1,128,128]{2,1,0:T(8,128)(2,1)S(1)}, bf16[1,128,128]{2,1,0:T(8,128)(2,1)S(1)}, bf16[1,128,128]{2,1,0:T(8,128)(2,1)S(1)},...) fusion(bf16[8,2,128,128]{3,2,1,0:T(8,128)(2,1)} %bitcast.52, ...), kind=kLoop, calls=%fused_computation.9 | loop fusion | bytes 524324 | tf_op jit(solution)/shard_map/squeeze | solution.py:361
  11.7 0.0 collective-permute-done
  11.8 5.4 %collective-permute-start.1 = (bf16[2,128,128]{2,1,0:T(8,128)(2,1)S(1)}, bf16[2,128,128]{2,1,0:T(8,128)(2,1)S(1)}, u32[]{:S(2)}, u32[]{:S(2)}) collective-permute-start(bf16[2,128,128]{2,1,0:T(8,128)(2,1)S(1)} %pad_maximum_fusion.1), channel_id=1, source_target_pairs={{0,8},{1,9},{2,10},{3,11},{4,12},{5,13},{6,14},{7,15},{8,0},{9,1},... | collective-permute-start | bytes 196616 | tf_op jit(solution)/shard_map/ppermute | solution.py:366
  17.2 0.4 collective-permute-start.2
  17.6 4.3 %collective-permute-start.3 = (bf16[2,128,128]{2,1,0:T(8,128)(2,1)S(1)}, bf16[2,128,128]{2,1,0:T(8,128)(2,1)S(1)}, u32[]{:S(2)}, u32[]{:S(2)}) collective-permute-start(bf16[2,128,128]{2,1,0:T(8,128)(2,1)S(1)} %pad_maximum_fusion.3), channel_id=1, source_target_pairs={{0,10},{1,11},{2,12},{3,13},{4,14},{5,15},{6,0},{7,1},{8,2},{9,3},... | collective-permute-start | bytes 196616 | tf_op jit(solution)/shard_map/ppermute | solution.py:366
  21.8 0.4 collective-permute-start.4
  22.2 3.4 %collective-permute-start.5 = (bf16[2,128,128]{2,1,0:T(8,128)(2,1)S(1)}, bf16[2,128,128]{2,1,0:T(8,128)(2,1)S(1)}, u32[]{:S(2)}, u32[]{:S(2)}) collective-permute-start(bf16[2,128,128]{2,1,0:T(8,128)(2,1)S(1)} %pad_maximum_fusion.5), channel_id=1, source_target_pairs={{0,12},{1,13},{2,14},{3,15},{4,0},{5,1},{6,2},{7,3},{8,4},{9,5},{1... | collective-permute-start | bytes 196616 | tf_op jit(solution)/shard_map/ppermute | solution.py:366
  25.6 1.6 %all-to-all-done.moved_ref = bf16[16,128,128]{2,1,0:T(8,128)(2,1)S(1)} async-done(((bf16[16,128,128]{2,1,0:T(8,128)(2,1)}), bf16[16,128,128]{2,1,0:T(8,128)(2,1)S(1)}, u32[]{:S(2)}, u32[]{:S(2)}) %all-to-all-start) | async-done | bytes 524320 | tf_op jit(solution)/shard_map/all_to_all | solution.py:344
  27.2 0.0 copy-done
  27.2 2.3 %block_ends.1 = (bf16[2048,128]{1,0:T(8,128)(2,1)S(1)}, f32[256,128]{1,0:T(8,128)S(1)}, f32[16,16,128]{2,1,0:T(8,128)}) custom-call(bf16[16,128,128]{2,1,0:T(8,128)(2,1)S(1)} %all-to-all-done.moved_ref, f32[16,128]{1,0:T(8,128)S(1)} %bitcast.41), custom_call_target="tpu_custom_call" | custom-call | flops 8388608 | bytes 1048576 | tf_op jit(solution)/shard_map/block_ends/pallas_call | solution.py:388
  29.5 6.8 %all-to-all-start.1 = ((f32[16,16,128]{2,1,0:T(8,128)}), f32[16,16,128]{2,1,0:T(8,128)S(1)}, u32[]{:S(2)}, u32[]{:S(2)}) async-start(f32[16,16,128]{2,1,0:T(8,128)} %get-tuple-element.11), calls=%async_computation.1 | async-start | bytes 262144 | tf_op jit(solution)/shard_map/all_to_all | solution.py:344
  36.2 0.0 collective-permute-done.1.refs_1_
  36.2 0.1 collective-permute-start.6
  36.3 0.0 collective-permute-done.2.refs_2_
  36.3 2.7 %collective-permute-start.7 = (bf16[2,128,128]{2,1,0:T(8,128)(2,1)S(1)}, bf16[2,128,128]{2,1,0:T(8,128)(2,1)S(1)}, u32[]{:S(2)}, u32[]{:S(2)}) collective-permute-start(bf16[2,128,128]{2,1,0:T(8,128)(2,1)S(1)} %pad_maximum_fusion.7), channel_id=1, source_target_pairs={{0,14},{1,15},{2,0},{3,1},{4,2},{5,3},{6,4},{7,5},{8,6},{9,7},{10,... | collective-permute-start | bytes 196616 | tf_op jit(solution)/shard_map/ppermute | solution.py:366
  39.0 3.1 %weighted.1 = (f32[4096,128]{1,0:T(8,128)S(1)}, f32[4096,128]{1,0:T(8,128)S(1)}, f32[256,128]{1,0:T(8,128)S(1)}) custom-call(bf16[2048,128]{1,0:T(8,128)(2,1)S(1)} %get-tuple-element.12.gt_ref.refs_8_, f32[16,128]{1,0:T(8,128)S(1)} %bitcast.42), custom_call_target="tpu_custom_call" | custom-call | flops 16777216 | bytes 1048576 | tf_op jit(solution)/shard_map/weighted/pallas_call | solution.py:402
  42.1 0.0 collective-permute-done.3.refs_3_
  42.1 0.0 collective-permute-done.4.refs_4_
  42.1 0.0 collective-permute-done.5.refs_5_
  42.1 0.0 collective-permute-done.6.refs_6_
  42.1 0.0 collective-permute-done.7.refs_7_
  42.1 0.0 copy-start.1
  42.1 3.9 %mode_sums.1._.refs_0_ = f32[80,128]{1,0:T(8,128)S(1)} custom-call(bf16[2,128,128]{2,1,0:T(8,128)(2,1)S(1)} %pad_maximum_fusion.refs_0_, bf16[2,128,128]{2,1,0:T(8,128)(2,1)S(1)} %collective-permute-done.1.refs_1_, bf16[2,128,128]{2,1,0:T(8,128)(2,1)S(1)} %collective-permute-done.2.refs_2_, bf16[2,128,128]{2,1,0:T(8,128)(2,1)S(1)} %collective-permute-done.3.refs_3_, ...), custom_call_target="tpu_custom_call" | custom-call | flops 33554432 | bytes 1048576 | tf_op jit(solution)/shard_map/mode_sums/pallas_call | solution.py:410
  46.0 0.0 all-to-all-done.1.heads_ref.refs_4_
  46.0 0.0 copy-done.1
  46.0 3.0 %input_grad.1 = bf16[16,128,128]{2,1,0:T(8,128)(2,1)} custom-call(f32[16,16,128]{2,1,0:T(8,128)S(1)} %all-to-all-done.1.heads_ref.refs_4_, bf16[2048,128]{1,0:T(8,128)(2,1)S(1)} %get-tuple-element.12.gt_ref.refs_8_, f32[4096,128]{1,0:T(8,128)S(1)} %get-tuple-element.13.refs_9_.sub_ref, f32[16,128]{1,0:T(8,128)S(1)} %bitcast.44, f32[16,128]{1,0:T(8,128)S(1)} %bitcast.47, ...), custom_call_target="tpu_custom_call" | custom-call | flops 16777216 | bytes 1048576 | tf_op jit(solution)/shard_map/input_grad/pallas_call | solution.py:419
  49.0 6.8 %all-to-all-start.2 = ((bf16[16,128,128]{2,1,0:T(8,128)(2,1)}), bf16[16,128,128]{2,1,0:T(8,128)(2,1)S(1)}, u32[]{:S(2)}, u32[]{:S(2)}) async-start(bf16[16,128,128]{2,1,0:T(8,128)(2,1)} %input_grad.1), calls=%async_computation.2 | async-start | bytes 1048576 | tf_op jit(solution)/shard_map/all_to_all | solution.py:344
  55.9 2.6 %collective-permute-start.10 = (f32[80,128]{1,0:T(8,128)S(1)}, f32[80,128]{1,0:T(8,128)S(1)}, u32[]{:S(2)}, u32[]{:S(2)}) collective-permute-start(f32[80,128]{1,0:T(8,128)S(1)} %mode_sums.1._.refs_0_), channel_id=1, source_target_pairs={{0,48},{16,0},{32,16},{48,32},{64,112},{80,64},{96,80},{112,96},{1... | collective-permute-start | bytes 122888 | tf_op jit(solution)/shard_map/ppermute | solution.py:351
  58.4 0.6 collective-permute-start.9
  59.0 0.6 collective-permute-start.8
  59.6 0.0 collective-permute-done.10.refs_3_
  59.6 3.4 %collective-permute-done.9.refs_2_ = f32[80,128]{1,0:T(8,128)S(1)} collective-permute-done((f32[80,128]{1,0:T(8,128)S(1)}, f32[80,128]{1,0:T(8,128)S(1)}, u32[]{:S(2)}, u32[]{:S(2)}) %collective-permute-start.9) | collective-permute-done | bytes 40992 | tf_op jit(solution)/shard_map/ppermute | solution.py:351
  63.0 0.6 collective-permute-done.8.refs_1_
  63.5 0.1 join.1.refs_0_
  63.6 2.5 %collective-permute-start.13 = (f32[80,128]{1,0:T(8,128)S(1)}, f32[80,128]{1,0:T(8,128)S(1)}, u32[]{:S(2)}, u32[]{:S(2)}) collective-permute-start(f32[80,128]{1,0:T(8,128)S(1)} %join.1.refs_0_), channel_id=1, source_target_pairs={{0,192},{16,208},{32,224},{48,240},{64,0},{80,16},{96,32},{112,48}... | collective-permute-start | bytes 122888 | tf_op jit(solution)/shard_map/ppermute | solution.py:351
  66.1 0.6 collective-permute-start.12
  66.6 0.6 collective-permute-start.11
  67.2 0.0 collective-permute-done.13.refs_3_
  67.2 3.5 %collective-permute-done.12.refs_2_ = f32[80,128]{1,0:T(8,128)S(1)} collective-permute-done((f32[80,128]{1,0:T(8,128)S(1)}, f32[80,128]{1,0:T(8,128)S(1)}, u32[]{:S(2)}, u32[]{:S(2)}) %collective-permute-start.12) | collective-permute-done | bytes 40992 | tf_op jit(solution)/shard_map/ppermute | solution.py:351
  70.7 0.4 collective-permute-done.11.refs_1_
  71.2 0.7 finish.1
  71.8 1.4 %all-to-all-done.2 = bf16[16,128,128]{2,1,0:T(8,128)(2,1)S(1)} async-done(((bf16[16,128,128]{2,1,0:T(8,128)(2,1)}), bf16[16,128,128]{2,1,0:T(8,128)(2,1)S(1)}, u32[]{:S(2)}, u32[]{:S(2)}) %all-to-all-start.2) | async-done | bytes 524320 | tf_op jit(solution)/shard_map/all_to_all | solution.py:344
  73.2 0.8 %copy.8 = bf16[2048,128]{1,0:T(8,128)(2,1)} copy(bf16[2048,128]{1,0:T(8,128)(2,1)S(1)} %bitcast.49) | data formatting | bytes 1048576
  (9 shorter events, 0.1 us)
Async XLA Ops:
  0.6 26.6 %copy-start = (f32[128,16]{0,1:T(8,128)S(1)}, f32[128,16]{0,1:T(8,128)}, u32[]{:S(2)}) copy-start(f32[128,16]{0,1:T(8,128)} %param.6) | copy-start | bytes 24580
  0.6 11.1 %collective-permute-start = (bf16[16,128,128]{2,1,0:T(8,128)(2,1)}, bf16[16,128,128]{2,1,0:T(8,128)(2,1)S(1)}, u32[]{:S(2)}, u32[]{:S(2)}) collective-permute-start(bf16[16,128,128]{2,1,0:T(8,128)(2,1)} %bitcast.51), channel_id=1, source_target_pairs={{0,1},{1,0},{2,3},{3,2},{4,5},{5,4},{6,7},{7,6},{8,9},{9,8},{10,11... | collective-permute-start | bytes 1572872 | tf_op jit(solution)/shard_map/ppermute | solution.py:359
  4.0 23.2 %all-to-all-start = ((bf16[16,128,128]{2,1,0:T(8,128)(2,1)}), bf16[16,128,128]{2,1,0:T(8,128)(2,1)S(1)}, u32[]{:S(2)}, u32[]{:S(2)}) async-start(bf16[16,128,128]{2,1,0:T(8,128)(2,1)} %bitcast.50), calls=%async_computation | async-start | bytes 1048576 | tf_op jit(solution)/shard_map/all_to_all | solution.py:344
  11.8 24.4 %collective-permute-start.1 = (bf16[2,128,128]{2,1,0:T(8,128)(2,1)S(1)}, bf16[2,128,128]{2,1,0:T(8,128)(2,1)S(1)}, u32[]{:S(2)}, u32[]{:S(2)}) collective-permute-start(bf16[2,128,128]{2,1,0:T(8,128)(2,1)S(1)} %pad_maximum_fusion.1), channel_id=1, source_target_pairs={{0,8},{1,9},{2,10},{3,11},{4,12},{5,13},{6,14},{7,15},{8,0},{9,1},... | collective-permute-start | bytes 196616 | tf_op jit(solution)/shard_map/ppermute | solution.py:366
  17.2 19.2 %collective-permute-start.2 = (bf16[2,128,128]{2,1,0:T(8,128)(2,1)S(1)}, bf16[2,128,128]{2,1,0:T(8,128)(2,1)S(1)}, u32[]{:S(2)}, u32[]{:S(2)}) collective-permute-start(bf16[2,128,128]{2,1,0:T(8,128)(2,1)S(1)} %pad_maximum_fusion.2), channel_id=1, source_target_pairs={{0,6},{1,7},{2,8},{3,9},{4,10},{5,11},{6,12},{7,13},{8,14},{9,15},... | collective-permute-start | bytes 196616 | tf_op jit(solution)/shard_map/ppermute | solution.py:366
  17.6 24.5 %collective-permute-start.3 = (bf16[2,128,128]{2,1,0:T(8,128)(2,1)S(1)}, bf16[2,128,128]{2,1,0:T(8,128)(2,1)S(1)}, u32[]{:S(2)}, u32[]{:S(2)}) collective-permute-start(bf16[2,128,128]{2,1,0:T(8,128)(2,1)S(1)} %pad_maximum_fusion.3), channel_id=1, source_target_pairs={{0,10},{1,11},{2,12},{3,13},{4,14},{5,15},{6,0},{7,1},{8,2},{9,3},... | collective-permute-start | bytes 196616 | tf_op jit(solution)/shard_map/ppermute | solution.py:366
  21.8 20.3 %collective-permute-start.4 = (bf16[2,128,128]{2,1,0:T(8,128)(2,1)S(1)}, bf16[2,128,128]{2,1,0:T(8,128)(2,1)S(1)}, u32[]{:S(2)}, u32[]{:S(2)}) collective-permute-start(bf16[2,128,128]{2,1,0:T(8,128)(2,1)S(1)} %pad_maximum_fusion.4), channel_id=1, source_target_pairs={{0,4},{1,5},{2,6},{3,7},{4,8},{5,9},{6,10},{7,11},{8,12},{9,13},{1... | collective-permute-start | bytes 196616 | tf_op jit(solution)/shard_map/ppermute | solution.py:366
  22.2 19.9 %collective-permute-start.5 = (bf16[2,128,128]{2,1,0:T(8,128)(2,1)S(1)}, bf16[2,128,128]{2,1,0:T(8,128)(2,1)S(1)}, u32[]{:S(2)}, u32[]{:S(2)}) collective-permute-start(bf16[2,128,128]{2,1,0:T(8,128)(2,1)S(1)} %pad_maximum_fusion.5), channel_id=1, source_target_pairs={{0,12},{1,13},{2,14},{3,15},{4,0},{5,1},{6,2},{7,3},{8,4},{9,5},{1... | collective-permute-start | bytes 196616 | tf_op jit(solution)/shard_map/ppermute | solution.py:366
  29.5 16.6 %all-to-all-start.1 = ((f32[16,16,128]{2,1,0:T(8,128)}), f32[16,16,128]{2,1,0:T(8,128)S(1)}, u32[]{:S(2)}, u32[]{:S(2)}) async-start(f32[16,16,128]{2,1,0:T(8,128)} %get-tuple-element.11), calls=%async_computation.1 | async-start | bytes 262144 | tf_op jit(solution)/shard_map/all_to_all | solution.py:344
  36.2 5.9 %collective-permute-start.6 = (bf16[2,128,128]{2,1,0:T(8,128)(2,1)S(1)}, bf16[2,128,128]{2,1,0:T(8,128)(2,1)S(1)}, u32[]{:S(2)}, u32[]{:S(2)}) collective-permute-start(bf16[2,128,128]{2,1,0:T(8,128)(2,1)S(1)} %pad_maximum_fusion.6), channel_id=1, source_target_pairs={{0,2},{1,3},{2,4},{3,5},{4,6},{5,7},{6,8},{7,9},{8,10},{9,11},{10,... | collective-permute-start | bytes 196616 | tf_op jit(solution)/shard_map/ppermute | solution.py:366
  36.3 5.8 %collective-permute-start.7 = (bf16[2,128,128]{2,1,0:T(8,128)(2,1)S(1)}, bf16[2,128,128]{2,1,0:T(8,128)(2,1)S(1)}, u32[]{:S(2)}, u32[]{:S(2)}) collective-permute-start(bf16[2,128,128]{2,1,0:T(8,128)(2,1)S(1)} %pad_maximum_fusion.7), channel_id=1, source_target_pairs={{0,14},{1,15},{2,0},{3,1},{4,2},{5,3},{6,4},{7,5},{8,6},{9,7},{10,... | collective-permute-start | bytes 196616 | tf_op jit(solution)/shard_map/ppermute | solution.py:366
  42.1 3.9 %copy-start.1 = (f32[128,16]{0,1:T(8,128)S(1)}, f32[128,16]{0,1:T(8,128)}, u32[]{:S(2)}) copy-start(f32[128,16]{0,1:T(8,128)} %param.7) | copy-start | bytes 24580
  49.0 24.2 %all-to-all-start.2 = ((bf16[16,128,128]{2,1,0:T(8,128)(2,1)}), bf16[16,128,128]{2,1,0:T(8,128)(2,1)S(1)}, u32[]{:S(2)}, u32[]{:S(2)}) async-start(bf16[16,128,128]{2,1,0:T(8,128)(2,1)} %input_grad.1), calls=%async_computation.2 | async-start | bytes 1048576 | tf_op jit(solution)/shard_map/all_to_all | solution.py:344
  55.9 3.7 %collective-permute-start.10 = (f32[80,128]{1,0:T(8,128)S(1)}, f32[80,128]{1,0:T(8,128)S(1)}, u32[]{:S(2)}, u32[]{:S(2)}) collective-permute-start(f32[80,128]{1,0:T(8,128)S(1)} %mode_sums.1._.refs_0_), channel_id=1, source_target_pairs={{0,48},{16,0},{32,16},{48,32},{64,112},{80,64},{96,80},{112,96},{1... | collective-permute-start | bytes 122888 | tf_op jit(solution)/shard_map/ppermute | solution.py:351
  58.4 4.5 %collective-permute-start.9 = (f32[80,128]{1,0:T(8,128)S(1)}, f32[80,128]{1,0:T(8,128)S(1)}, u32[]{:S(2)}, u32[]{:S(2)}) collective-permute-start(f32[80,128]{1,0:T(8,128)S(1)} %mode_sums.1._.refs_0_), channel_id=1, source_target_pairs={{0,32},{16,48},{32,0},{48,16},{64,96},{80,112},{96,64},{112,80},{1... | collective-permute-start | bytes 122888 | tf_op jit(solution)/shard_map/ppermute | solution.py:351
  59.0 4.5 %collective-permute-start.8 = (f32[80,128]{1,0:T(8,128)S(1)}, f32[80,128]{1,0:T(8,128)S(1)}, u32[]{:S(2)}, u32[]{:S(2)}) collective-permute-start(f32[80,128]{1,0:T(8,128)S(1)} %mode_sums.1._.refs_0_), channel_id=1, source_target_pairs={{0,16},{16,32},{32,48},{48,0},{64,80},{80,96},{96,112},{112,64},{1... | collective-permute-start | bytes 122888 | tf_op jit(solution)/shard_map/ppermute | solution.py:351
  63.6 3.6 %collective-permute-start.13 = (f32[80,128]{1,0:T(8,128)S(1)}, f32[80,128]{1,0:T(8,128)S(1)}, u32[]{:S(2)}, u32[]{:S(2)}) collective-permute-start(f32[80,128]{1,0:T(8,128)S(1)} %join.1.refs_0_), channel_id=1, source_target_pairs={{0,192},{16,208},{32,224},{48,240},{64,0},{80,16},{96,32},{112,48}... | collective-permute-start | bytes 122888 | tf_op jit(solution)/shard_map/ppermute | solution.py:351
  66.1 4.7 %collective-permute-start.12 = (f32[80,128]{1,0:T(8,128)S(1)}, f32[80,128]{1,0:T(8,128)S(1)}, u32[]{:S(2)}, u32[]{:S(2)}) collective-permute-start(f32[80,128]{1,0:T(8,128)S(1)} %join.1.refs_0_), channel_id=1, source_target_pairs={{0,128},{16,144},{32,160},{48,176},{64,192},{80,208},{96,224},{112... | collective-permute-start | bytes 122888 | tf_op jit(solution)/shard_map/ppermute | solution.py:351
  66.6 4.5 %collective-permute-start.11 = (f32[80,128]{1,0:T(8,128)S(1)}, f32[80,128]{1,0:T(8,128)S(1)}, u32[]{:S(2)}, u32[]{:S(2)}) collective-permute-start(f32[80,128]{1,0:T(8,128)S(1)} %join.1.refs_0_), channel_id=1, source_target_pairs={{0,64},{16,80},{32,96},{48,112},{64,128},{80,144},{96,160},{112,17... | collective-permute-start | bytes 122888 | tf_op jit(solution)/shard_map/ppermute | solution.py:351
